TPU v7x, 256 devices: a whole 4x4x8 slice. The times are simulated.
256 devices in a mesh: dp: 16 (over x, y), tensor: 16 (over z, core).
Axes of the slice: x: 4, y: 4, z: 8, core: 2. Of those that a mesh axis runs over, the one named last changes fastest.
Arguments:
- hidden_x: bfloat16 [128, 128, 16384], P('dp', None, 'tensor'), may hold values from -6 to 6
- gate_z: bfloat16 [128, 128, 16384], P('dp', None, 'tensor'), may hold values from -6 to 6
- conv_weight: float32 [4, 16384], P(None, 'tensor'), may hold values from -3 to 3
- conv_bias: float32 [16384], P('tensor'), may hold values from -0.5 to 0.5
- x_weight: bfloat16 [16384, 544], P('tensor'), may hold values from -0.046875 to 0.046875
- dt_weight: bfloat16 [512, 16384], P(None, 'tensor'), may hold values from -0.25 to 0.25
- dt_bias: float32 [16384], P('tensor'), may hold values from -6 to -2
- a_log: float32 [16, 16384], P(None, 'tensor'), may hold values from -2 to 2.7
- skip_gain: float32 [16384], P('tensor'), may hold values from 0.5 to 1.5
- ssm_cache: float32 [512, 16, 16384], P('dp', None, 'tensor'), may hold values from -6 to 6
- conv_cache: float32 [512, 3, 16384], P('dp', None, 'tensor'), may hold values from -6 to 6
- holder_of: int32 [128], replicated, may hold values from 0 to 15, as said below
- slot_of: int32 [128], replicated, may hold values from 0 to 31, as said below
Outputs:
- gated_out: bfloat16 [128, 128, 16384], P('dp', None, 'tensor')
- new_ssm: float32 [512, 16, 16384], P('dp', None, 'tensor')
- new_conv: float32 [512, 3, 16384], P('dp', None, 'tensor')
Inputs may be any that keep to these rules, and one draw needn't show every extreme that they name: `holder_of`: requests 8 * g to 8 * g + 7 belong to dp group g. One holder serves at most 2 requests of one group, and in every group some holder serves exactly 2. `slot_of`: requests with the same holder have different slots.
All inputs are finite; a program needn't handle non-finite values.
Results may differ from a plain program's by a relative error of at most 0.0062.
Values may be sent and summed in bfloat16 or wider, within the bound.
No kernel may reach another device: no remote copies, remote signals or barrier semaphores. Data moves between devices by JAX's collectives and lax.ppermute only.
A program may use at most 128 MiB of HBM per device.

v0:
```python
import jax
import jax.numpy as jnp
from jax import lax
from jax.sharding import PartitionSpec as P

EPSILON = 1e-06
NORM_FLOOR = 0.25


def normalize(projected, rank_width, state_width):
    dt_raw = projected[:, :rank_width]
    inject_raw = projected[:, rank_width : rank_width + state_width]
    readout_raw = projected[:, rank_width + state_width :]
    dt_norm = dt_raw * lax.rsqrt(jnp.mean(dt_raw * dt_raw, axis=1, keepdims=True) + EPSILON)
    inject_norm = inject_raw * lax.rsqrt(
        jnp.maximum(jnp.mean(inject_raw * inject_raw, axis=1, keepdims=True), NORM_FLOOR)
    )
    readout_norm = readout_raw * lax.rsqrt(
        jnp.maximum(jnp.mean(readout_raw * readout_raw, axis=1, keepdims=True), NORM_FLOOR)
    )
    joined = jnp.concatenate([inject_norm, readout_norm], axis=1)
    return (dt_norm.astype(jnp.bfloat16), joined.astype(jnp.bfloat16))


def convolve(hidden_rows, conv_start, conv_weight, conv_bias):
    turn_len = hidden_rows.shape[1]
    extended = jnp.concatenate([conv_start, hidden_rows.astype(jnp.float32)], axis=1)
    summed = jnp.zeros(hidden_rows.shape, jnp.float32) + conv_bias[None, None, :]
    for offset in range(conv_weight.shape[0]):
        summed = (
            summed + extended[:, offset : offset + turn_len, :] * conv_weight[offset][None, None, :]
        )
    return jax.nn.silu(summed).astype(jnp.bfloat16)


def advance(carried, decay_rate, dt_now, drive_now, inject_now, readout_now):
    carried = (
        jnp.exp(dt_now[:, None, :] * decay_rate[None, :, :]) * carried
        + drive_now[:, None, :] * inject_now[:, :, None]
    )
    return (carried, jnp.sum(readout_now[:, :, None] * carried, axis=1))


def recur_blocks(
    state_start, decay_rate, dt_full, drive_full, inject_full, readout_full, block_len
):

    def time_major(values):
        moved = jnp.swapaxes(values, 0, 1)
        return moved.reshape((moved.shape[0] // block_len, block_len) + moved.shape[1:])

    def one_block(carried, slices):
        dt_block, drive_block, inject_block, readout_block = slices
        outputs = []
        for offset in range(block_len):
            carried, output_now = advance(
                carried,
                decay_rate,
                dt_block[offset],
                drive_block[offset],
                inject_block[offset],
                readout_block[offset],
            )
            outputs.append(output_now)
        return (carried, jnp.stack(outputs))

    final_state, readout = lax.scan(
        one_block,
        state_start,
        (
            time_major(dt_full),
            time_major(drive_full),
            time_major(inject_full),
            time_major(readout_full),
        ),
    )
    readout = readout.reshape((-1,) + readout.shape[2:])
    return (final_state, jnp.swapaxes(readout, 0, 1))


def body(
    hidden_x,
    gate_z,
    conv_weight,
    conv_bias,
    x_weight,
    dt_weight,
    dt_bias,
    a_log,
    skip_gain,
    ssm_cache,
    conv_cache,
    holder_of,
    slot_of,
):
    groups = lax.axis_size("dp")
    my_index = lax.axis_index("dp")
    requests = hidden_x.shape[0]
    slot_count = ssm_cache.shape[0]
    capacity = slot_count // groups
    state_width = a_log.shape[0]
    rank_width = dt_weight.shape[0]
    holders = holder_of.reshape(groups, requests)
    places = slot_of.reshape(groups, requests)
    earlier = jnp.arange(requests)[None, :] < jnp.arange(requests)[:, None]
    same_holder = holders[:, :, None] == holders[:, None, :]
    rank_within = jnp.sum((same_holder & earlier[None, :, :]).astype(jnp.int32), axis=2)
    rank_range = jnp.arange(capacity, dtype=jnp.int32)
    served = (holders == my_index)[:, None, :] & (
        rank_within[:, None, :] == rank_range[None, :, None]
    )
    occupied = jnp.any(served, axis=2)
    sources = jnp.sum(jnp.where(served, places[:, None, :], 0), axis=2)
    outgoing = (ssm_cache[sources], conv_cache[sources])
    arrived = (
        lax.all_to_all(outgoing[0], "dp", split_axis=0, concat_axis=0, tiled=True),
        lax.all_to_all(outgoing[1], "dp", split_axis=0, concat_axis=0, tiled=True),
    )
    own_holders = holders[my_index]
    own_ranks = rank_within[my_index]
    lookup = own_holders * capacity + own_ranks
    state_start = arrived[0].reshape((groups * capacity,) + arrived[0].shape[2:])[lookup]
    conv_start = arrived[1].reshape((groups * capacity,) + arrived[1].shape[2:])[lookup]
    conv_out = convolve(hidden_x, conv_start, conv_weight, conv_bias)
    flat_rows = conv_out.reshape(-1, conv_out.shape[2])
    projected = lax.psum(jnp.dot(flat_rows, x_weight, preferred_element_type=jnp.float32), "tensor")
    dt_norm, bc_norm = normalize(projected, rank_width, state_width)
    dt_full = jax.nn.softplus(
        jnp.dot(dt_norm, dt_weight, preferred_element_type=jnp.float32) + dt_bias[None, :]
    )
    dt_full = dt_full.reshape(hidden_x.shape)
    drive_full = dt_full * conv_out.astype(jnp.float32)
    bc_full = bc_norm.astype(jnp.float32).reshape(
        hidden_x.shape[0], hidden_x.shape[1], 2 * state_width
    )
    decay_rate = -jnp.exp(a_log)
    final_state, readout = recur_blocks(
        state_start,
        decay_rate,
        dt_full,
        drive_full,
        bc_full[:, :, :state_width],
        bc_full[:, :, state_width:],
        8,
    )
    gated_out = (
        (readout + skip_gain[None, None, :] * conv_out.astype(jnp.float32))
        * jax.nn.silu(gate_z.astype(jnp.float32))
    ).astype(jnp.bfloat16)
    kept_rows = conv_cache.shape[1]
    last_inputs = hidden_x[:, hidden_x.shape[1] - kept_rows :, :].astype(jnp.float32)
    placed = (own_holders[None, None, :] == jnp.arange(groups, dtype=jnp.int32)[:, None, None]) & (
        own_ranks[None, None, :] == rank_range[None, :, None]
    )
    picked_rows = jnp.sum(
        jnp.where(placed, jnp.arange(requests, dtype=jnp.int32)[None, None, :], 0), axis=2
    )
    received = (
        lax.all_to_all(
            final_state[picked_rows].astype(jnp.bfloat16),
            "dp",
            split_axis=0,
            concat_axis=0,
            tiled=True,
        ).astype(jnp.float32),
        lax.all_to_all(
            last_inputs[picked_rows].astype(jnp.bfloat16),
            "dp",
            split_axis=0,
            concat_axis=0,
            tiled=True,
        ).astype(jnp.float32),
    )
    targets = jnp.where(occupied, sources, slot_count).reshape(-1)
    new_ssm = ssm_cache.at[targets].set(
        received[0].reshape((-1,) + received[0].shape[2:]), mode="drop"
    )
    new_conv = conv_cache.at[targets].set(
        received[1].reshape((-1,) + received[1].shape[2:]), mode="drop"
    )
    return (gated_out, new_ssm, new_conv)


def solution(mesh):
    placed = (
        P("dp", None, "tensor"),
        P("dp", None, "tensor"),
        P(None, "tensor"),
        P("tensor"),
        P("tensor", None),
        P(None, "tensor"),
        P("tensor"),
        P(None, "tensor"),
        P("tensor"),
        P("dp", None, "tensor"),
        P("dp", None, "tensor"),
        P(),
        P(),
    )
    return jax.shard_map(
        body,
        mesh=mesh,
        in_specs=placed,
        out_specs=(P("dp", None, "tensor"), P("dp", None, "tensor"), P("dp", None, "tensor")),
        check_vma=False,
    )
```

profile of v0, /device:TPU:8, one launch (start us, length us, event | category | flops | bytes accessed | tf_op | source)
XLA Modules:
  0.0 345.5 jit_solution(15422881931745802605)
XLA Ops:
  7.2 1.1 copy.249
  8.3 3.2 copy.248
  12.2 1.1 gather_fusion.2
  14.3 7.4 %all-to-all-start.1 = ((f32[16,2,3,1024]{3,1,2,0:T(2,128)}), f32[16,2,3,1024]{3,1,2,0:T(2,128)S(1)}, u32[]{:S(2)}, u32[]{:S(2)}) async-start(f32[16,2,3,1024]{3,1,2,0:T(2,128)} %copy.118), calls=%async_computation.1 | async-start | bytes 786432 | tf_op jit(solution)/shard_map/all_to_all | solution.py:117
  22.0 0.9 slice.249
  23.0 4.0 %convert_element_type.40 = f32[8,128,1024]{2,1,0:T(8,128)} convert(bf16[8,128,1024]{2,1,0:T(8,128)(2,1)} %param.15) | non-fusion elementwise | flops 1048576 | bytes 6291456 | tf_op jit(solution)/shard_map/convert_element_type | solution.py:27
  27.0 3.6 %gather_fusion = f32[32,16,1024]{2,1,0:T(8,128)} fusion(f32[32,16,1024]{2,1,0:T(8,128)} %copy.248, s32[1024]{0:T(1024)S(1)} %pad_clamp_fusion.2), kind=kCustom, calls=%fused_computation | custom fusion | bytes 4194432 | tf_op jit(solution)/shard_map/gather | solution.py:114
  30.7 7.2 %all-to-all-start = ((f32[16,2,16,1024]{3,2,1,0:T(8,128)}), f32[16,2,16,1024]{3,2,1,0:T(8,128)}, u32[]{:S(2)}, u32[]{:S(2)}) async-start(f32[16,2,16,1024]{3,2,1,0:T(8,128)} %bitcast.216), calls=%async_computation | async-start | bytes 4194304 | tf_op jit(solution)/shard_map/all_to_all | solution.py:116
  38.9 7.7 %multiply_convert_fusion = bf16[8,128,1024]{2,1,0:T(8,128)(2,1)S(1)} fusion(f32[8,128,1024]{2,1,0:T(8,128)} %convert_element_type.40, f32[8,3,1024]{2,1,0:T(4,128)S(1)} %gather_fusion.3, f32[1024]{0:T(1024)S(1)} %bitcast.256, f32[1024]{0:T(1024)S(1)} %bitcast.257, f32[1024]{0:T(1024)S(1)} %bitcast.255, f32[1024]{0:T(1024)S(1)} %bitcast.254, ...), kind=kLoop, calls=%fused_computation.123 | loop fusion | flops 16777216 | bytes 6410240 | tf_op jit(solution)/shard_map/convert_element_type | solution.py:33
  46.6 1.3 copy-done.2
  47.9 2.7 fusion.40
  52.9 116.4 %all-reduce.2.cloned.1.call-done = f32[1024,544]{0,1:T(8,128)} async-done(((f32[1024,544]{0,1:T(8,128)}), f32[1024,544]{0,1:T(8,128)}) %all-reduce.2.cloned.1.call-update) | async-done | bytes 2228240 | tf_op jit(solution)/shard_map/psum | solution.py:126
  169.2 0.9 multiply_reduce_fusion.10
  170.2 0.9 fusion.33
  171.6 1.8 multiply_reduce_fusion.8
  173.4 5.2 %compare_select_fusion = f32[1024,1024]{1,0:T(8,128)S(1)} fusion(bf16[512,1024]{1,0:T(8,128)(2,1)} %param.20, f32[1024]{0:T(1024)S(1)} %copy-done.11, f32[1024,544]{0,1:T(8,128)} %all-reduce.2.cloned.1.call-done, f32[1024]{0:T(1024)S(1)} %add_rsqrt_fusion), kind=kOutput, calls=%fused_computation.97 | convolution fusion | flops 1082130432 | bytes 7348224 | tf_op jit(solution)/shard_map/dot_general | solution.py:129
  178.6 1.9 copy-done.4
  180.6 2.7 fusion.24
  183.3 7.3 %all-to-all-start.3 = ((bf16[16,2,3,1024]{3,1,2,0:T(2,128)(2,1)}), bf16[16,2,3,1024]{3,1,2,0:T(2,128)(2,1)S(1)}, u32[]{:S(2)}, u32[]{:S(2)}) async-start(bf16[16,2,3,1024]{3,1,2,0:T(2,128)(2,1)} %copy.128), calls=%async_computation.3 | async-start | bytes 393216 | tf_op jit(solution)/shard_map/all_to_all | solution.py:166
  190.5 2.2 gather_fusion.1
  192.7 114.2 %while.12 = (s32[]{:T(128)}, f32[8,16,1024]{2,1,0:T(8,128)S(1)}, f32[16,8,8,1024]{3,1,0,2:T(8,128)}, f32[16,8,8,1024]{3,1,0,2:T(8,128)}, f32[16,1024]{1,0:T(8,12...) while((s32[]{:T(128)}, f32[8,16,1024]{2,1,0:T(8,128)S(1)}, ...), condition=%wide.region_15.16_spmd, body=%wide.region_6.15_spmd.sunk | while | flops 9371657 | bytes 7171389 | solution.py:67
  192.7 3.1 constant_dynamic-slice_fusion.33
  196.9 1.2 multiply_reduce_fusion.14
  199.8 3.2 constant_dynamic-slice_fusion.33
  204.1 1.2 multiply_reduce_fusion.14
  207.0 3.2 constant_dynamic-slice_fusion.33
  211.3 1.2 multiply_reduce_fusion.14
  214.2 3.0 constant_dynamic-slice_fusion.33
  218.3 1.2 multiply_reduce_fusion.14
  221.2 3.2 constant_dynamic-slice_fusion.33
  225.5 1.2 multiply_reduce_fusion.14
  228.5 3.2 constant_dynamic-slice_fusion.33
  232.7 1.2 multiply_reduce_fusion.14
  235.7 3.2 constant_dynamic-slice_fusion.33
  239.9 1.2 multiply_reduce_fusion.14
  242.0 0.9 copy_dynamic-update-slice_fusion.2
  242.9 3.0 constant_dynamic-slice_fusion.33
  246.9 1.2 multiply_reduce_fusion.14
  249.8 3.0 constant_dynamic-slice_fusion.33
  253.9 1.2 multiply_reduce_fusion.14
  256.9 3.3 constant_dynamic-slice_fusion.33
  261.2 1.2 multiply_reduce_fusion.14
  263.3 0.9 copy_dynamic-update-slice_fusion.2
  264.2 3.2 constant_dynamic-slice_fusion.33
  268.4 1.2 multiply_reduce_fusion.14
  271.3 3.0 constant_dynamic-slice_fusion.33
  275.3 1.2 multiply_reduce_fusion.14
  277.4 0.9 copy_dynamic-update-slice_fusion.2
  278.3 3.1 constant_dynamic-slice_fusion.33
  282.4 1.2 multiply_reduce_fusion.14
  285.4 3.2 constant_dynamic-slice_fusion.33
  289.6 1.2 multiply_reduce_fusion.14
  292.6 3.3 constant_dynamic-slice_fusion.33
  296.9 1.2 multiply_reduce_fusion.14
  299.0 0.9 copy_dynamic-update-slice_fusion.2
  299.9 3.0 constant_dynamic-slice_fusion.33
  304.0 1.2 multiply_reduce_fusion.14
  306.9 1.6 gather_fusion.4
  308.6 7.2 %all-to-all-start.2 = ((bf16[16,2,16,1024]{3,2,1,0:T(8,128)(2,1)}), bf16[16,2,16,1024]{3,2,1,0:T(8,128)(2,1)S(1)}, u32[]{:S(2)}, u32[]{:S(2)}) async-start(bf16[16,2,16,1024]{3,2,1,0:T(8,128)(2,1)} %bitcast.244), calls=%async_computation.2 | async-start | bytes 2097152 | tf_op jit(solution)/shard_map/all_to_all | solution.py:159
  316.4 3.2 scatter_fusion.1
  319.7 6.5 %fusion.27 = bf16[8,128,1024]{2,1,0:T(8,128)(2,1)} fusion(bf16[8,128,1024]{2,1,0:T(8,128)(2,1)} %copy-done.2, bf16[8,128,1024]{2,1,0:T(8,128)(2,1)} %param.16, f32[16,8,8,1024]{3,1,0,2:T(8,128)} %get-tuple-element.46, f32[1024]{0:T(1024)S(1)} %copy-done.7), kind=kLoop, calls=%fused_computation.117 | loop fusion | flops 10485760 | bytes 10489856 | tf_op jit(solution)/shard_map/convert_element_type | solution.py:149
  326.1 4.5 %all-to-all-done.2 = bf16[16,2,16,1024]{3,2,1,0:T(8,128)(2,1)S(1)} async-done(((bf16[16,2,16,1024]{3,2,1,0:T(8,128)(2,1)}), bf16[16,2,16,1024]{3,2,1,0:T(8,128)(2,1)S(1)}, u32[]{:S(2)}, u32[]{:S(2)}) %all-to-all-start.2) | async-done | bytes 1048608 | tf_op jit(solution)/shard_map/all_to_all | solution.py:159
  330.7 1.7 bitcast_convert_fusion
  332.3 6.3 %scatter_fusion = f32[32,16,1024]{2,1,0:T(8,128)} fusion(f32[32,16,1024]{2,1,0:T(8,128)} %copy.248, s32[32]{0:T(128)S(1)} %fusion.38, f32[32,16,1024]{2,1,0:T(8,128)} %bitcast_convert_fusion), kind=kCustom, calls=%fused_computation.6 | custom fusion | bytes 6291584 | tf_op jit(solution)/shard_map/scatter | solution.py:175
  (521 shorter events, 44.4 us)
Async XLA Ops:
  7.2 40.8 %copy-start = (bf16[1024,544]{0,1:T(8,128)(2,1)S(1)}, bf16[1024,544]{0,1:T(8,128)(2,1)}, u32[]{:S(2)}) copy-start(bf16[1024,544]{0,1:T(8,128)(2,1)} %param.19) | copy-start | bytes 3342340
  7.2 4.3 %copy-start.9 = (s32[128]{0:T(128)S(1)}, s32[128]{0:T(128)}, u32[]{:S(2)}) copy-start(s32[128]{0:T(128)} %param.26) | copy-start | bytes 1540
  7.2 4.5 %copy-start.10 = (s32[128]{0:T(128)S(1)}, s32[128]{0:T(128)}, u32[]{:S(2)}) copy-start(s32[128]{0:T(128)} %param.27) | copy-start | bytes 1540
  14.3 16.4 %all-to-all-start.1 = ((f32[16,2,3,1024]{3,1,2,0:T(2,128)}), f32[16,2,3,1024]{3,1,2,0:T(2,128)S(1)}, u32[]{:S(2)}, u32[]{:S(2)}) async-start(f32[16,2,3,1024]{3,1,2,0:T(2,128)} %copy.118), calls=%async_computation.1 | async-start | bytes 786432 | tf_op jit(solution)/shard_map/all_to_all | solution.py:117
  23.0 7.7 %copy-start.6 = (f32[4,1024]{1,0:T(4,128)S(1)}, f32[4,1024]{1,0:T(4,128)}, u32[]{:S(2)}) copy-start(f32[4,1024]{1,0:T(4,128)} %param.17) | copy-start | bytes 49156
  27.0 11.9 %copy-start.8 = (f32[1024]{0:T(1024)S(1)}, f32[1024]{0:T(1024)}, u32[]{:S(2)}) copy-start(f32[1024]{0:T(1024)} %param.18) | copy-start | bytes 12292
  30.7 152.5 %all-to-all-start = ((f32[16,2,16,1024]{3,2,1,0:T(8,128)}), f32[16,2,16,1024]{3,2,1,0:T(8,128)}, u32[]{:S(2)}, u32[]{:S(2)}) async-start(f32[16,2,16,1024]{3,2,1,0:T(8,128)} %bitcast.216), calls=%async_computation | async-start | bytes 4194304 | tf_op jit(solution)/shard_map/all_to_all | solution.py:116
  38.0 131.3 %all-reduce.2.cloned.1.call-start = ((), (), s32[]{:S(2)}) async-start(), calls=%async_computation.4 | async-start | bytes 4456448 | tf_op jit(solution)/shard_map/psum | solution.py:126
  46.6 1.3 copy-start.2
  47.9 4.9 %copy-start.5 = (f32[16,1024]{1,0:T(8,128)S(1)}, f32[16,1024]{1,0:T(8,128)}, u32[]{:S(2)}) copy-start(f32[16,1024]{1,0:T(8,128)} %param.22) | copy-start | bytes 196612
  50.6 122.8 %copy-start.11 = (f32[1024]{0:T(1024)S(1)}, f32[1024]{0:T(1024)}, u32[]{:S(2)}) copy-start(f32[1024]{0:T(1024)} %param.21) | copy-start | bytes 12292
  173.4 7.1 %copy-start.3 = (bf16[8,128,1024]{2,1,0:T(8,128)(2,1)S(1)}, bf16[8,128,1024]{2,1,0:T(8,128)(2,1)}, u32[]{:S(2)}) copy-start(bf16[8,128,1024]{2,1,0:T(8,128)(2,1)} %copy-done.2) | copy-start | bytes 6291460
  178.6 1.9 copy-start.4
  183.3 125.3 %all-to-all-start.3 = ((bf16[16,2,3,1024]{3,1,2,0:T(2,128)(2,1)}), bf16[16,2,3,1024]{3,1,2,0:T(2,128)(2,1)S(1)}, u32[]{:S(2)}, u32[]{:S(2)}) async-start(bf16[16,2,3,1024]{3,1,2,0:T(2,128)(2,1)} %copy.128), calls=%async_computation.3 | async-start | bytes 393216 | tf_op jit(solution)/shard_map/all_to_all | solution.py:166
  308.6 22.1 %all-to-all-start.2 = ((bf16[16,2,16,1024]{3,2,1,0:T(8,128)(2,1)}), bf16[16,2,16,1024]{3,2,1,0:T(8,128)(2,1)S(1)}, u32[]{:S(2)}, u32[]{:S(2)}) async-start(bf16[16,2,16,1024]{3,2,1,0:T(8,128)(2,1)} %bitcast.244), calls=%async_computation.2 | async-start | bytes 2097152 | tf_op jit(solution)/shard_map/all_to_all | solution.py:159
  316.4 3.2 copy-start.7
  319.6 6.5 %copy-start.1 = (f32[32,3,1024]{2,0,1:T(8,128)}, f32[32,3,1024]{2,0,1:T(8,128)S(1)}, u32[]{:S(2)}) copy-start(f32[32,3,1024]{2,0,1:T(8,128)S(1)} %scatter_fusion.1) | copy-start | bytes 1179652
Sparse Core Ops, SparseCore 0:
  50.8 118.4 all-reduce.1
where the time goes:
time: 347 us; the launch traced here: 346 us
  waiting for transfers between devices  121 us (35%)
  local copies, waits for them, and re-layouts  99 us (29%)
  other arithmetic  70.6 us (20%)
  starting transfers between devices  29.1 us (8%)
  between operations  14.4 us (4%)
  matrix products  7.92 us (2%)
  loops' own time  3.5 us (1%)
    psum x1, waiting for transfers between devices, body(): lax.psum(jnp.dot(flat_rows, x_weight, preferred_element_type=jnp.float32)...  116 us
    slice x16, local copies, waits for them, and re-layouts, one_block(): drive_block[offset]  50.1 us
    reduce_sum x48, other arithmetic, advance(): return (carried, jnp.sum(readout_now[:, :, None] * carried, axis=1))  43.8 us
    dynamic_update_slice x16, local copies, waits for them, and re-layouts, recur_blocks(): lax.scan(one_block, state_start, (time_major(dt_full), time_major(drive_f...  13.8 us
    convert_element_type x1, other arithmetic, convolve(): return jax.nn.silu(summed).astype(jnp.bfloat16)  7.71 us
    unnamed x28, local copies, waits for them, and re-layouts  7.54 us
    all_to_all x1, starting transfers between devices, body(): lax.all_to_all(outgoing[1], 'dp', split_axis=0, concat_axis=0, tiled=True)  7.39 us
    all_to_all x1, starting transfers between devices, body(): lax.all_to_all(last_inputs[picked_rows].astype(jnp.bfloat16), 'dp', split...  7.25 us
  transfers between devices with their start and end apart: 5, of which 2 were waited for; matrix products, arithmetic and copies ran while one was open for 46% of the time, Pallas kernels for 0%

commit v1 on v0

v1 whole, which is shorter than its diff:
```python
import functools

import jax
import jax.numpy as jnp
from jax import lax
from jax.experimental import pallas as pl
from jax.experimental.pallas import tpu as pltpu
from jax.sharding import Mesh, PartitionSpec as P

EPSILON = 1e-06
NORM_FLOOR = 0.25
LOG2_E = 1.4426950408889634

GROUPS = 16
REQUESTS = 8
CHUNKS = 2
PER = REQUESTS // CHUNKS
TURN = 128
INNER = 1024
RANK = 512
STATE = 16
WIDE = RANK + 2 * STATE
SLOTS = 32
KEPT = 3
DEPTH = 8
CORES = 2
SHARE = PER * TURN // (DEPTH * CORES)
LANES = 128
TILES = INNER // LANES
UNROLL = 4

F32 = jnp.float32
BF16 = jnp.bfloat16
SWAP = [(0, 1), (1, 0)]


def params(mib):
    return pltpu.CompilerParams(vmem_limit_bytes=mib * 2**20)


def cost(us, bytes_accessed):
    return pl.CostEstimate(
        flops=int(us * 1.0e9), bytes_accessed=bytes_accessed, transcendentals=0
    )


def conv_kernel(order_ref, source_ref, hidden, start, weight, bias, x_weight, conv_out, sent, kept, rows):
    step = pl.program_id(0)
    for k in range(KEPT):
        rows[8 - KEPT + k : 9 - KEPT + k, :] = start[0, k : k + 1, :].astype(F32)
    for tile in range(TILES):
        cols = slice(tile * LANES, (tile + 1) * LANES)
        rows[8:, cols] = hidden[0, :, cols].astype(F32)
        total = jnp.zeros((TURN, LANES), F32) + bias[:, cols]
        for tap in range(KEPT + 1):
            first = 8 - KEPT + tap
            total = total + rows[first : first + TURN, cols] * weight[tap : tap + 1, cols]
        conv_out[0, :, cols] = (total / (1.0 + jnp.exp(-total))).astype(BF16)
    part = jnp.dot(conv_out[0], x_weight[...], preferred_element_type=F32)

    @pl.when(step < PER // 2)
    def _():
        sent[0] = part.astype(BF16)

    @pl.when(step >= PER // 2)
    def _():
        kept[0] = part


def convolve(order, source, hidden, arrived, weight, bias, x_weight):
    half = PER // 2
    return pl.pallas_call(
        conv_kernel,
        grid_spec=pltpu.PrefetchScalarGridSpec(
            num_scalar_prefetch=2,
            grid=(PER,),
            in_specs=[
                pl.BlockSpec((1, TURN, INNER), lambda i, o, s: (o[i], 0, 0)),
                pl.BlockSpec((1, 2 * KEPT, INNER), lambda i, o, s: (s[i], 0, 0)),
                pl.BlockSpec((KEPT + 1, INNER), lambda i, o, s: (0, 0)),
                pl.BlockSpec((1, INNER), lambda i, o, s: (0, 0)),
                pl.BlockSpec((INNER, WIDE), lambda i, o, s: (0, 0)),
            ],
            out_specs=[
                pl.BlockSpec((1, TURN, INNER), lambda i, o, s: (i, 0, 0)),
                pl.BlockSpec((1, TURN, WIDE), lambda i, o, s: (jnp.minimum(i, half - 1), 0, 0)),
                pl.BlockSpec((1, TURN, WIDE), lambda i, o, s: (jnp.maximum(i - half, 0), 0, 0)),
            ],
            scratch_shapes=[pltpu.VMEM((8 + TURN, INNER), F32)],
        ),
        out_shape=[
            jax.ShapeDtypeStruct((PER, TURN, INNER), BF16),
            jax.ShapeDtypeStruct((half, TURN, WIDE), BF16),
            jax.ShapeDtypeStruct((half, TURN, WIDE), F32),
        ],
        compiler_params=params(32),
        cost_estimate=cost(5, 4 * 2**20),
        name="convolve",
    )(order, source, hidden, arrived, weight, bias, x_weight)


def norm_kernel(parts, out):
    total = parts[0].astype(F32)
    for k in range(1, DEPTH):
        total = total + parts[k].astype(F32)
    rank = total[:, :RANK]
    inject = total[:, RANK : RANK + STATE]
    readout = total[:, RANK + STATE :]
    rank = rank * lax.rsqrt(jnp.mean(rank * rank, axis=1, keepdims=True) + EPSILON)
    inject = inject * lax.rsqrt(
        jnp.maximum(jnp.mean(inject * inject, axis=1, keepdims=True), NORM_FLOOR)
    )
    readout = readout * lax.rsqrt(
        jnp.maximum(jnp.mean(readout * readout, axis=1, keepdims=True), NORM_FLOOR)
    )
    joined = jnp.concatenate([rank, inject, readout], axis=1).astype(BF16)
    for k in range(DEPTH):
        out[k] = joined


def normalize(parts):
    return pl.pallas_call(
        norm_kernel,
        out_shape=jax.ShapeDtypeStruct((DEPTH, SHARE, WIDE), BF16),
        compiler_params=params(32),
        cost_estimate=cost(1.5, 2**20),
        name="normalize",
    )(parts)


def scan_kernel(
    order_ref,
    source_ref,
    holder_ref,
    own,
    other,
    dt_weight,
    dt_bias,
    a_log,
    skip,
    conv,
    gate,
    start,
    base,
    gated,
    final,
    dts,
    us,
    spread,
    rates,
    states,
):
    mine = pl.program_id(0) < PER // 2
    normed = jnp.where(mine, own[0].astype(F32), other[0].astype(F32))
    columns = normed[:, RANK:].T
    for t in range(TURN):
        spread[t * 2 * STATE : (t + 1) * 2 * STATE, :] = jnp.broadcast_to(
            columns[:, t : t + 1], (2 * STATE, LANES)
        )
    for tile in range(TILES):
        cols = slice(tile * LANES, (tile + 1) * LANES)
        rates[pl.ds(tile, STATE, stride=TILES), :] = -LOG2_E * jnp.exp(a_log[:, cols])
        states[pl.ds(tile, STATE, stride=TILES), :] = start[0, :, cols].astype(F32)
    rank = normed[:, :RANK].astype(BF16)
    pair = 2 * LANES
    for block in range(INNER // pair):
        cols = slice(block * pair, (block + 1) * pair)
        raw = jnp.dot(rank, dt_weight[:, cols], preferred_element_type=F32) + dt_bias[:, cols]
        dt = jnp.maximum(raw, 0.0) + jnp.log1p(jnp.exp(-jnp.abs(raw)))
        for k in range(2):
            tile = 2 * block + k
            dts[pl.ds(tile, TURN, stride=TILES), :] = dt[:, k * LANES : (k + 1) * LANES]
            us[pl.ds(tile, TURN, stride=TILES), :] = conv[
                0, :, tile * LANES : (tile + 1) * LANES
            ].astype(F32)
    decay = [rates[n * TILES : (n + 1) * TILES, :] for n in range(STATE)]

    def steps(i, carried):
        carried = list(carried)
        for k in range(UNROLL):
            t = i * UNROLL + k
            at = pl.multiple_of(t * TILES, TILES)
            row = pl.multiple_of(t * 2 * STATE, 2 * STATE)
            dt = dts[pl.ds(at, TILES), :]
            drive = dt * us[pl.ds(at, TILES), :]
            sums = [None] * 4
            for n in range(STATE):
                carried[n] = (
                    jnp.exp2(dt * decay[n]) * carried[n] + drive * spread[pl.ds(row + n, 1), :]
                )
                term = carried[n] * spread[pl.ds(row + STATE + n, 1), :]
                sums[n % 4] = term if sums[n % 4] is None else sums[n % 4] + term
            dts[pl.ds(at, TILES), :] = (sums[0] + sums[1]) + (sums[2] + sums[3])
        return tuple(carried)

    carried = tuple(states[n * TILES : (n + 1) * TILES, :] for n in range(STATE))
    carried = lax.fori_loop(0, TURN // UNROLL, steps, carried)
    for n in range(STATE):
        states[n * TILES : (n + 1) * TILES, :] = carried[n]
    for tile in range(TILES):
        cols = slice(tile * LANES, (tile + 1) * LANES)
        z = gate[0, :, cols].astype(F32)
        y = dts[pl.ds(tile, TURN, stride=TILES), :] + skip[:, cols] * conv[0, :, cols].astype(F32)
        gated[0, :, cols] = (y * (z / (1.0 + jnp.exp(-z)))).astype(BF16)
        final[0, :, cols] = states[pl.ds(tile, STATE, stride=TILES), :].astype(BF16)


def scan(order, source, holder, own, other, dt_weight, dt_bias, a_log, skip, conv, gate, start, base):
    half = PER // 2
    whole = lambda shape: pl.BlockSpec(shape, lambda i, o, s, h: (0,) * len(shape))
    return pl.pallas_call(
        scan_kernel,
        grid_spec=pltpu.PrefetchScalarGridSpec(
            num_scalar_prefetch=3,
            grid=(PER,),
            in_specs=[
                pl.BlockSpec((1, TURN, WIDE), lambda i, o, s, h: (jnp.minimum(i, half - 1), 0, 0)),
                pl.BlockSpec((1, TURN, WIDE), lambda i, o, s, h: (jnp.maximum(i - half, 0), 0, 0)),
                whole((RANK, INNER)),
                whole((1, INNER)),
                whole((STATE, INNER)),
                whole((1, INNER)),
                pl.BlockSpec((1, TURN, INNER), lambda i, o, s, h: ((i + half) % PER, 0, 0)),
                pl.BlockSpec((1, TURN, INNER), lambda i, o, s, h: (o[i], 0, 0)),
                pl.BlockSpec((1, STATE, INNER), lambda i, o, s, h: (s[i], 0, 0)),
                pl.BlockSpec(memory_space=pl.ANY),
            ],
            out_specs=[
                pl.BlockSpec((1, TURN, INNER), lambda i, o, s, h: (o[i], 0, 0)),
                pl.BlockSpec((1, STATE, INNER), lambda i, o, s, h: (h[i], 0, 0)),
            ],
            scratch_shapes=[
                pltpu.VMEM((TURN * TILES, LANES), F32),
                pltpu.VMEM((TURN * TILES, LANES), F32),
                pltpu.VMEM((TURN * 2 * STATE, LANES), F32),
                pltpu.VMEM((STATE * TILES, LANES), F32),
                pltpu.VMEM((STATE * TILES, LANES), F32),
            ],
        ),
        out_shape=[
            jax.ShapeDtypeStruct((REQUESTS, TURN, INNER), BF16),
            jax.ShapeDtypeStruct((GROUPS, STATE, INNER), BF16),
        ],
        input_output_aliases={12: 0} if base is not None else {},
        compiler_params=params(32),
        cost_estimate=cost(15, 4 * 2**20),
        name="scan",
    )(order, source, holder, own, other, dt_weight, dt_bias, a_log, skip, conv, gate, start,
      base if base is not None else skip)


def place_kernel(state_from, conv_from, ssm, conv, states, inputs, new_ssm, new_conv):
    slot = pl.program_id(0)
    new_ssm[0] = jnp.where(state_from[slot] > 0, states[0].astype(F32), ssm[0])
    last = inputs[0].astype(F32)[KEPT:, :]
    new_conv[0] = jnp.where(conv_from[slot] > 0, last, conv[0])


def place(state_from, conv_from, ssm, conv, states, inputs):
    return pl.pallas_call(
        place_kernel,
        grid_spec=pltpu.PrefetchScalarGridSpec(
            num_scalar_prefetch=2,
            grid=(SLOTS,),
            in_specs=[
                pl.BlockSpec((1, STATE, INNER), lambda i, s, c: (i, 0, 0)),
                pl.BlockSpec((1, KEPT, INNER), lambda i, s, c: (i, 0, 0)),
                pl.BlockSpec((1, STATE, INNER), lambda i, s, c: (jnp.maximum(s[i] - 1, 0), 0, 0)),
                pl.BlockSpec((1, 2 * KEPT, INNER), lambda i, s, c: (jnp.maximum(c[i] - 1, 0), 0, 0)),
            ],
            out_specs=[
                pl.BlockSpec((1, STATE, INNER), lambda i, s, c: (i, 0, 0)),
                pl.BlockSpec((1, KEPT, INNER), lambda i, s, c: (i, 0, 0)),
            ],
        ),
        out_shape=[
            jax.ShapeDtypeStruct((SLOTS, STATE, INNER), F32),
            jax.ShapeDtypeStruct((SLOTS, KEPT, INNER), F32),
        ],
        compiler_params=params(32),
        cost_estimate=cost(8, 6 * 2**20),
        name="place",
    )(state_from, conv_from, ssm, conv, states, inputs)


def store_kernel(slots, states, base, new_ssm, wide, sems):
    def start(g, carry):
        wide[g] = states[g].astype(F32)

        @pl.when(slots[g] < SLOTS)
        def _():
            pltpu.make_async_copy(wide.at[g], new_ssm.at[slots[g]], sems.at[g]).start()

        return carry

    def finish(g, carry):
        @pl.when(slots[g] < SLOTS)
        def _():
            pltpu.make_async_copy(wide.at[g], new_ssm.at[slots[g]], sems.at[g]).wait()

        return carry

    lax.fori_loop(0, GROUPS, start, 0)
    lax.fori_loop(0, GROUPS, finish, 0)


def store(slots, states, base):
    return pl.pallas_call(
        store_kernel,
        grid_spec=pltpu.PrefetchScalarGridSpec(
            num_scalar_prefetch=1,
            grid=(1,),
            in_specs=[
                pl.BlockSpec((GROUPS, STATE, INNER), lambda i, s: (0, 0, 0)),
                pl.BlockSpec(memory_space=pl.ANY),
            ],
            out_specs=pl.BlockSpec(memory_space=pl.ANY),
            scratch_shapes=[
                pltpu.VMEM((GROUPS, STATE, INNER), F32),
                pltpu.SemaphoreType.DMA((GROUPS,)),
            ],
        ),
        out_shape=jax.ShapeDtypeStruct((SLOTS, STATE, INNER), F32),
        input_output_aliases={2: 0},
        compiler_params=params(32),
        cost_estimate=cost(2, 2 * 2**20),
        name="store",
    )(slots, states, base)


def assign(holders):
    index = jnp.arange(REQUESTS)
    earlier = index[None, :] < index[:, None]
    same = holders[:, :, None] == holders[:, None, :]
    twice = jnp.sum(same, axis=2) > 1
    later = jnp.any(same & earlier[None], axis=2)
    first_of_two = twice & ~later
    room = PER - jnp.sum(first_of_two, axis=1, keepdims=True)
    alone_before = jnp.sum(~twice[:, None, :] & earlier[None], axis=2)
    leading = first_of_two | (~twice & (alone_before < room))
    chunk = jnp.where(leading, 0, 1).astype(jnp.int32)
    alike = chunk[:, :, None] == chunk[:, None, :]
    place_in = jnp.sum(alike & earlier[None], axis=2).astype(jnp.int32)
    return chunk, place_in


def exchange(values, axis):
    return lax.all_to_all(values, axis, split_axis=0, concat_axis=0, tiled=True)


def body(
    hidden_x,
    gate_z,
    conv_weight,
    conv_bias,
    x_weight,
    dt_weight,
    dt_bias,
    a_log,
    skip_gain,
    ssm_cache,
    conv_cache,
    holder_of,
    slot_of,
):
    me = lax.axis_index("dp")
    core = lax.axis_index("core")
    holders = holder_of.reshape(GROUPS, REQUESTS)
    places = slot_of.reshape(GROUPS, REQUESTS)
    chunk, place_in = assign(holders)

    chunk_range = jnp.arange(CHUNKS, dtype=jnp.int32)
    served = (holders == me)[:, None, :] & (chunk[:, None, :] == chunk_range[None, :, None])
    occupied = jnp.any(served, axis=2)
    slots = jnp.sum(jnp.where(served, places[:, None, :], 0), axis=2)
    targets = jnp.where(occupied, slots, SLOTS)
    hits = targets[None] == jnp.arange(SLOTS, dtype=jnp.int32)[:, None, None]
    group_range = jnp.arange(GROUPS, dtype=jnp.int32)
    state_from = jnp.sum(jnp.where(hits[:, :, 0], group_range[None] + 1, 0), axis=1)
    numbers = group_range[:, None] * CHUNKS + chunk_range[None, :] + 1
    conv_from = jnp.sum(jnp.where(hits, numbers[None], 0), axis=(1, 2))

    own_holders = holders[me]
    own_number = chunk[me] * PER + place_in[me]
    at = jnp.arange(REQUESTS, dtype=jnp.int32)
    half = PER // 2
    number_of = (at // PER) * PER + ((at % PER) // half + (1 - core)) % 2 * half + at % half
    chosen = own_number[None, :] == number_of[:, None]
    order = jnp.sum(jnp.where(chosen, at[None, :], 0), axis=1)
    holder = jnp.sum(jnp.where(chosen, own_holders[None, :], 0), axis=1)
    source = holder * CHUNKS + at // PER
    sent_to = (own_holders[None, None, :] == group_range[:, None, None]) & (
        chunk[me][None, None, :] == chunk_range[None, :, None]
    )
    picked = jnp.sum(jnp.where(sent_to, at[None, None, :], 0), axis=2)

    first = jnp.concatenate(
        [conv_cache[slots].astype(BF16), hidden_x[:, TURN - KEPT :, :][picked]], axis=2
    )
    first = exchange(first, "dp").reshape(GROUPS * CHUNKS, 2 * KEPT, INNER)
    starts = exchange(ssm_cache[slots].astype(BF16), "dp").reshape(
        GROUPS * CHUNKS, STATE, INNER
    )

    bias = conv_bias.reshape(1, INNER)
    convs, normed = [], []
    for c in range(CHUNKS):
        span = slice(c * PER, (c + 1) * PER)
        conv, sent, kept = convolve(
            order[span], source[span], hidden_x, first, conv_weight, bias, x_weight
        )
        came = lax.ppermute(sent, "core", SWAP)
        parts = (kept + came.astype(F32)).astype(BF16).reshape(DEPTH, SHARE, WIDE)
        own = exchange(normalize(exchange(parts, "z")), "z").reshape(half, TURN, WIDE)
        other = lax.ppermute(own, "core", SWAP)
        convs.append(conv)
        normed.append((own, other))

    gated = None
    returned = []
    for c in range(CHUNKS):
        swap = lambda v: jnp.concatenate([v[c * PER + half : (c + 1) * PER], v[c * PER : c * PER + half]])
        gated, final = scan(
            swap(order),
            swap(source),
            swap(holder),
            normed[c][0],
            normed[c][1],
            dt_weight,
            dt_bias.reshape(1, INNER),
            a_log,
            skip_gain.reshape(1, INNER),
            convs[c],
            gate_z,
            starts,
            gated,
        )
        returned.append(exchange(final, "dp"))
    new_ssm, new_conv = place(state_from, conv_from, ssm_cache, conv_cache, returned[0], first)
    new_ssm = store(targets[:, 1], returned[1], new_ssm)
    return (gated, new_ssm, new_conv)


def solution(mesh):
    fine = Mesh(mesh.devices.reshape(GROUPS, DEPTH, CORES), ("dp", "z", "core"))
    tensor = ("z", "core")
    placed = (
        P("dp", None, tensor),
        P("dp", None, tensor),
        P(None, tensor),
        P(tensor),
        P(tensor, None),
        P(None, tensor),
        P(tensor),
        P(None, tensor),
        P(tensor),
        P("dp", None, tensor),
        P("dp", None, tensor),
        P(),
        P(),
    )
    return jax.shard_map(
        body,
        mesh=fine,
        in_specs=placed,
        out_specs=(P("dp", None, tensor),) * 3,
        check_vma=False,
    )
```

time: 347 us -> 199 us (0.57)
  local copies, waits for them, and re-layouts: 99 us -> 24.2 us
  other arithmetic: 70.6 us -> 3.67 us
  Pallas kernels: 0 us -> 52.6 us
  waiting for transfers between devices: 121 us -> 71.5 us
  starting transfers between devices: 29.1 us -> 45 us
  between operations: 14.4 us -> 1 us
  matrix products: 7.92 us -> 0 us
  loops' own time: 3.5 us -> 0 us
    psum x1 -> x0, waiting for transfers between devices: 116 us -> none  [body(): lax.psum(jnp.dot(flat_rows, x_weight, preferred_element_type=jnp.float32)...]
    all_to_all x4 -> x8, waiting for transfers between devices: 4.54 us -> 71.5 us  [exchange(): return lax.all_to_all(values, axis, split_axis=0, concat_axis=0, tiled=True)]
    pallas_call x0 -> x8, Pallas kernels: none -> 52.6 us  [the longest x2 30.9 us: scan(): pl.pallas_call(scan_kernel, grid_spec=pltpu.PrefetchScalarGridSpec(num_sc...]
    slice x18 -> x5, local copies, waits for them, and re-layouts: 51 us -> 1.24 us  [the longest x1 0.95 us: body(): hidden_x[:, TURN - KEPT:, :][picked]]
    reduce_sum x53 -> x9, other arithmetic: 46.7 us -> 0.69 us  [the longest x1 0.18 us: body(): holder = jnp.sum(jnp.where(chosen, own_holders[None, :], 0), axis=1)]
    convert_element_type x4 -> x2, other arithmetic: 18.2 us -> 1.58 us  [body(): parts = (kept + came.astype(F32)).astype(BF16).reshape(DEPTH, SHARE, WIDE)]
    all_to_all x4 -> x8, starting transfers between devices: 29.1 us -> 43.8 us  [exchange(): return lax.all_to_all(values, axis, split_axis=0, concat_axis=0, tiled=True)]
    dynamic_update_slice x16 -> x0, local copies, waits for them, and re-layouts: 13.8 us -> none  [recur_blocks(): lax.scan(one_block, state_start, (time_major(dt_full), time_major(drive_f...]
  transfers between devices with their start and end apart: 5 -> 12, of which waited for: 2 -> 6; matrix products, arithmetic and copies ran while one was open for 46% -> 4% of each run, Pallas kernels for 0% -> 24%
where the time goes in v1:
time: 199 us; the launch traced here: 198 us
  waiting for transfers between devices  71.5 us (36%)
  Pallas kernels  52.6 us (26%)
  starting transfers between devices  45 us (23%)
  local copies, waits for them, and re-layouts  24.2 us (12%)
  other arithmetic  3.67 us (2%)
    all_to_all x8, waiting for transfers between devices, exchange(): return lax.all_to_all(values, axis, split_axis=0, concat_axis=0, tiled=True)  71.5 us
    all_to_all x8, starting transfers between devices, exchange(): return lax.all_to_all(values, axis, split_axis=0, concat_axis=0, tiled=True)  43.8 us
    pallas_call x2, Pallas kernels, scan(): pl.pallas_call(scan_kernel, grid_spec=pltpu.PrefetchScalarGridSpec(num_sc...  30.9 us
    unnamed x41, local copies, waits for them, and re-layouts  16 us
    pallas_call x1, Pallas kernels, place(): pl.pallas_call(place_kernel, grid_spec=pltpu.PrefetchScalarGridSpec(num_s...  10.8 us
    pallas_call x2, Pallas kernels, convolve(): pl.pallas_call(conv_kernel, grid_spec=pltpu.PrefetchScalarGridSpec(num_sc...  8.37 us
  transfers between devices with their start and end apart: 12, of which 6 were waited for; matrix products, arithmetic and copies ran while one was open for 4% of the time, Pallas kernels for 24%

profile of v1, /device:TPU:8, one launch (start us, length us, event | category | flops | bytes accessed | tf_op | source)
XLA Modules:
  0.0 197.9 jit_solution(1569828340232742582)
XLA Ops:
  0.7 0.8 eq.119
  1.6 0.1 fusion.1
  1.7 0.1 convert_reduce_fusion.1
  1.8 0.1 convert_reduce_fusion
  1.9 0.2 dynamic-slice_reduce_fusion
  2.1 1.0 slice.65
  3.1 0.7 broadcast_in_dim.105
  4.0 0.1 copy.65
  4.0 0.1 select_reduce_fusion.2
  4.2 0.1 copy.68
  4.3 0.1 reshape.301
  4.4 0.8 gather_fusion.1
  5.1 0.2 copy.76
  5.3 0.1 copy.67
  5.4 0.1 reshape.293
  5.5 1.1 gather_fusion
  6.7 0.5 pad_maximum_fusion
  7.3 1.0 copy.70
  8.3 7.5 %all-to-all-start = ((bf16[16,2,6,1024]{3,1,2,0:T(2,128)(2,1)}), bf16[16,2,6,1024]{3,1,2,0:T(2,128)(2,1)S(1)}, u32[]{:S(2)}, u32[]{:S(2)}) async-start(bf16[16,2,6,1024]{3,1,2,0:T(2,128)(2,1)} %copy.70), calls=%async_computation | async-start | bytes 786432 | tf_op jit(solution)/shard_map/all_to_all | solution.py:348
  15.8 0.7 copy.72.x_weight
  16.6 0.2 fusion.5
  16.8 7.2 %all-to-all-done = bf16[16,2,6,1024]{3,1,2,0:T(2,128)(2,1)S(1)} async-done(((bf16[16,2,6,1024]{3,1,2,0:T(2,128)(2,1)}), bf16[16,2,6,1024]{3,1,2,0:T(2,128)(2,1)S(1)}, u32[]{:S(2)}, u32[]{:S(2)}) %all-to-all-start) | async-done | bytes 393248 | tf_op jit(solution)/shard_map/all_to_all | solution.py:348
  24.0 0.1 copy.71
  24.1 1.6 copy-done.3
  25.7 4.2 %convolve.2 = (bf16[4,128,1024]{2,1,0:T(8,128)(2,1)S(1)}, bf16[2,128,544]{2,1,0:T(8,128)(2,1)S(1)}, f32[2,128,544]{2,1,0:T(8,128)S(1)}) custom-call(s32[4]{0:T(128)S(1)} %get-tuple-element.73.order_ref, s32[4]{0:T(128)S(1)} %get-tuple-element.52.source_ref, bf16[8,128,1024]{2,1,0:T(8,128)(2,1)S(1)} %copy-done.3, bf16[32,6,1024]{2,1,0:T(8,128)(2,1)S(1)} %bitcast.31, ...), custom_call_target="tpu_custom_call" | custom-call | flops 5000000000 | bytes 4194304 | tf_op jit(solution)/shard_map/convolve/pallas_call | solution.py:72
  29.9 1.0 copy-done.13
  30.9 4.2 %convolve.3 = (bf16[4,128,1024]{2,1,0:T(8,128)(2,1)S(1)}, bf16[2,128,544]{2,1,0:T(8,128)(2,1)S(1)}, f32[2,128,544]{2,1,0:T(8,128)S(1)}) custom-call(s32[4]{0:T(128)S(1)} %get-tuple-element.74.order_ref, s32[4]{0:T(128)S(1)} %get-tuple-element.51.source_ref, bf16[8,128,1024]{2,1,0:T(8,128)(2,1)S(1)} %copy-done.3, bf16[32,6,1024]{2,1,0:T(8,128)(2,1)S(1)} %bitcast.32, ...), custom_call_target="tpu_custom_call" | custom-call | flops 5000000000 | bytes 4194304 | tf_op jit(solution)/shard_map/convolve/pallas_call | solution.py:72
  35.1 0.6 collective-permute-start.2
  35.7 0.8 add_convert_fusion.1
  36.5 8.5 %all-to-all-start.1 = ((bf16[8,32,544]{2,1,0:T(8,128)(2,1)}), bf16[8,32,544]{2,1,0:T(8,128)(2,1)S(1)}, u32[]{:S(2)}, u32[]{:S(2)}) async-start(bf16[8,32,544]{2,1,0:T(8,128)(2,1)} %bitcast.6), calls=%async_computation.1 | async-start | bytes 655360 | tf_op jit(solution)/shard_map/all_to_all | solution.py:348
  44.9 0.8 add_convert_fusion
  45.7 12.8 %all-to-all-done.1.parts = bf16[8,32,544]{2,1,0:T(8,128)(2,1)S(1)} async-done(((bf16[8,32,544]{2,1,0:T(8,128)(2,1)}), bf16[8,32,544]{2,1,0:T(8,128)(2,1)S(1)}, u32[]{:S(2)}, u32[]{:S(2)}) %all-to-all-start.1) | async-done | bytes 278560 | tf_op jit(solution)/shard_map/all_to_all | solution.py:348
  58.6 3.4 %all-to-all-start.4 = ((bf16[8,32,544]{2,1,0:T(8,128)(2,1)}), bf16[8,32,544]{2,1,0:T(8,128)(2,1)S(1)}, u32[]{:S(2)}, u32[]{:S(2)}) async-start(bf16[8,32,544]{2,1,0:T(8,128)(2,1)} %bitcast.12), calls=%async_computation.4 | async-start | bytes 655360 | tf_op jit(solution)/shard_map/all_to_all | solution.py:348
  62.2 0.9 normalize.2
  63.1 12.6 %all-to-all-done.4.parts = bf16[8,32,544]{2,1,0:T(8,128)(2,1)S(1)} async-done(((bf16[8,32,544]{2,1,0:T(8,128)(2,1)}), bf16[8,32,544]{2,1,0:T(8,128)(2,1)S(1)}, u32[]{:S(2)}, u32[]{:S(2)}) %all-to-all-start.4) | async-done | bytes 278560 | tf_op jit(solution)/shard_map/all_to_all | solution.py:348
  75.7 3.4 %all-to-all-start.2 = ((bf16[8,32,544]{2,1,0:T(8,128)(2,1)}), bf16[8,32,544]{2,1,0:T(8,128)(2,1)S(1)}, u32[]{:S(2)}, u32[]{:S(2)}) async-start(bf16[8,32,544]{2,1,0:T(8,128)(2,1)} %normalize.2), calls=%async_computation.2 | async-start | bytes 655360 | tf_op jit(solution)/shard_map/all_to_all | solution.py:348
  79.1 0.1 pad_add_fusion
  79.3 0.2 normalize.3
  79.5 0.7 copy-done.2
  80.2 12.6 %all-to-all-done.2 = bf16[8,32,544]{2,1,0:T(8,128)(2,1)S(1)} async-done(((bf16[8,32,544]{2,1,0:T(8,128)(2,1)}), bf16[8,32,544]{2,1,0:T(8,128)(2,1)S(1)}, u32[]{:S(2)}, u32[]{:S(2)}) %all-to-all-start.2) | async-done | bytes 278560 | tf_op jit(solution)/shard_map/all_to_all | solution.py:348
  92.7 3.4 %all-to-all-start.5 = ((bf16[8,32,544]{2,1,0:T(8,128)(2,1)}), bf16[8,32,544]{2,1,0:T(8,128)(2,1)S(1)}, u32[]{:S(2)}, u32[]{:S(2)}) async-start(bf16[8,32,544]{2,1,0:T(8,128)(2,1)} %copy-done.2), calls=%async_computation.5 | async-start | bytes 655360 | tf_op jit(solution)/shard_map/all_to_all | solution.py:348
  96.3 1.6 gather_fusion.2
  98.0 11.8 %all-to-all-done.5 = bf16[8,32,544]{2,1,0:T(8,128)(2,1)S(1)} async-done(((bf16[8,32,544]{2,1,0:T(8,128)(2,1)}), bf16[8,32,544]{2,1,0:T(8,128)(2,1)S(1)}, u32[]{:S(2)}, u32[]{:S(2)}) %all-to-all-start.5) | async-done | bytes 278560 | tf_op jit(solution)/shard_map/all_to_all | solution.py:348
  109.8 5.4 %all-to-all-start.3 = ((bf16[16,2,16,1024]{3,2,1,0:T(8,128)(2,1)}), bf16[16,2,16,1024]{3,2,1,0:T(8,128)(2,1)S(1)}, u32[]{:S(2)}, u32[]{:S(2)}) async-start(bf16[16,2,16,1024]{3,2,1,0:T(8,128)(2,1)} %bitcast.45), calls=%async_computation.3 | async-start | bytes 2097152 | tf_op jit(solution)/shard_map/all_to_all | solution.py:348
  115.3 0.1 select_reduce_fusion.1.state_from
  115.4 0.1 select_reduce_fusion.conv_from
  115.5 0.1 collective-permute-start.3
  115.6 1.3 copy.74.conv
  116.9 0.6 collective-permute-start.1
  117.5 14.5 %all-to-all-done.3 = bf16[16,2,16,1024]{3,2,1,0:T(8,128)(2,1)S(1)} async-done(((bf16[16,2,16,1024]{3,2,1,0:T(8,128)(2,1)}), bf16[16,2,16,1024]{3,2,1,0:T(8,128)(2,1)S(1)}, u32[]{:S(2)}, u32[]{:S(2)}) %all-to-all-start.3) | async-done | bytes 1048608 | tf_op jit(solution)/shard_map/all_to_all | solution.py:348
  132.0 1.6 copy-done.4
  133.6 1.2 copy-done.6
  134.8 1.2 copy-done.16
  136.1 14.9 %scan.2 = (bf16[8,128,1024]{2,1,0:T(8,128)(2,1)}, bf16[16,16,1024]{2,1,0:T(8,128)(2,1)}) custom-call(s32[4]{0:T(128)S(1)} %get-tuple-element.71.order_ref, s32[4]{0:T(128)S(1)} %get-tuple-element.72.source_ref, s32[4]{0:T(128)S(1)} %pad_add_fusion.5.holder_ref, bf16[2,128,544]{2,1,0:T(8,128)(2,1)S(1)} %bitcast.37, ...), custom_call_target="tpu_custom_call" | custom-call | flops 15000000512 | bytes 4194304 | tf_op jit(solution)/shard_map/scan/pallas_call | solution.py:211
  151.0 4.9 %all-to-all-start.7 = ((bf16[16,16,1024]{2,1,0:T(8,128)(2,1)}), bf16[16,16,1024]{2,1,0:T(8,128)(2,1)S(1)}, u32[]{:S(2)}, u32[]{:S(2)}) async-start(bf16[16,16,1024]{2,1,0:T(8,128)(2,1)} %get-tuple-element.24), calls=%async_computation.7 | async-start | bytes 1048576 | tf_op jit(solution)/shard_map/all_to_all | solution.py:348
  155.9 1.6 copy-done.5
  157.5 1.2 copy-done.7
  158.7 1.2 copy-done.14
  159.9 16.0 %scan.3 = (bf16[8,128,1024]{2,1,0:T(8,128)(2,1)}, bf16[16,16,1024]{2,1,0:T(8,128)(2,1)}) custom-call(s32[4]{0:T(128)S(1)} %get-tuple-element.69.order_ref, s32[4]{0:T(128)S(1)} %get-tuple-element.70.source_ref, s32[4]{0:T(128)S(1)} %pad_add_fusion.2.holder_ref, bf16[2,128,544]{2,1,0:T(8,128)(2,1)S(1)} %bitcast.35, ...), custom_call_target="tpu_custom_call", output_to_operand_aliasing={{0}: (12, {})} | custom-call | flops 15000000512 | bytes 4194304 | tf_op jit(solution)/shard_map/scan/pallas_call | solution.py:211
  175.9 7.2 %all-to-all-start.6 = ((bf16[16,16,1024]{2,1,0:T(8,128)(2,1)}), bf16[16,16,1024]{2,1,0:T(8,128)(2,1)S(1)}, u32[]{:S(2)}, u32[]{:S(2)}) async-start(bf16[16,16,1024]{2,1,0:T(8,128)(2,1)} %get-tuple-element.23), calls=%async_computation.6 | async-start | bytes 1048576 | tf_op jit(solution)/shard_map/all_to_all | solution.py:348
  183.1 1.6 copy-done.1
  184.7 10.8 %place.1 = (f32[32,16,1024]{2,1,0:T(8,128)}, f32[32,3,1024]{2,1,0:T(4,128)S(1)}) custom-call(s32[32]{0:T(128)S(1)} %select_reduce_fusion.1.state_from, s32[32]{0:T(128)S(1)} %select_reduce_fusion.conv_from, f32[32,16,1024]{2,1,0:T(8,128)S(1)} %copy-done.1, f32[32,3,1024]{2,1,0:T(4,128)S(1)} %copy.74.conv, bf16[16,16,1024]{2,1,0:T(8,128)(2,1)S(1)} %all-to-all-done.7.states, ...), custom_call_target="tpu_custom_call" | custom-call | flops 8000000000 | bytes 6291456 | tf_op jit(solution)/shard_map/place/pallas_call | solution.py:260
  195.5 1.0 copy.75
  196.5 1.4 store.1
  (68 shorter events, 1.2 us)
Async XLA Ops:
  0.6 4.9 %copy-start.17 = (f32[32,3,1024]{2,0,1:T(8,128)S(1)}, f32[32,3,1024]{2,0,1:T(8,128)}, u32[]{:S(2)}) copy-start(f32[32,3,1024]{2,0,1:T(8,128)} %param.23) | copy-start | bytes 1179652
  5.5 10.3 %copy-start.18 = (bf16[1024,544]{0,1:T(8,128)(2,1)S(1)}, bf16[1024,544]{0,1:T(8,128)(2,1)}, u32[]{:S(2)}) copy-start(bf16[1024,544]{0,1:T(8,128)(2,1)} %param.17) | copy-start | bytes 3342340
  8.3 15.8 %copy-start.9 = (f32[4,1024]{1,0:T(4,128)S(1)}, f32[4,1024]{1,0:T(4,128)}, u32[]{:S(2)}) copy-start(f32[4,1024]{1,0:T(4,128)} %weight.3) | copy-start | bytes 49156
  8.3 15.8 %copy-start.10 = (f32[1024]{0:T(1024)S(1)}, f32[1024]{0:T(1024)}, u32[]{:S(2)}) copy-start(f32[1024]{0:T(1024)} %param.16) | copy-start | bytes 12292
  8.3 15.7 %all-to-all-start = ((bf16[16,2,6,1024]{3,1,2,0:T(2,128)(2,1)}), bf16[16,2,6,1024]{3,1,2,0:T(2,128)(2,1)S(1)}, u32[]{:S(2)}, u32[]{:S(2)}) async-start(bf16[16,2,6,1024]{3,1,2,0:T(2,128)(2,1)} %copy.70), calls=%async_computation | async-start | bytes 786432 | tf_op jit(solution)/shard_map/all_to_all | solution.py:348
  24.1 1.6 copy-start.3
  29.9 1.0 copy-start.13
  30.9 4.8 %collective-permute-start = (bf16[2,128,544]{2,1,0:T(8,128)(2,1)S(1)}, bf16[2,128,544]{2,1,0:T(8,128)(2,1)S(1)}, u32[]{:S(2)}, u32[]{:S(2)}) collective-permute-start(bf16[2,128,544]{2,1,0:T(8,128)(2,1)S(1)} %get-tuple-element.16), channel_id=1, source_target_pairs={{0,1},{1,0},{2,3},{3,2},{4,5},{5,4},{6,7},{7,6},{8,9},{9,8},{10,11... | collective-permute-start | bytes 835592 | tf_op jit(solution)/shard_map/ppermute | solution.py:412
  35.1 1.4 copy-start.15
  35.1 9.8 %collective-permute-start.2 = (bf16[2,128,544]{2,1,0:T(8,128)(2,1)S(1)}, bf16[2,128,544]{2,1,0:T(8,128)(2,1)S(1)}, u32[]{:S(2)}, u32[]{:S(2)}) collective-permute-start(bf16[2,128,544]{2,1,0:T(8,128)(2,1)S(1)} %get-tuple-element.19), channel_id=1, source_target_pairs={{0,1},{1,0},{2,3},{3,2},{4,5},{5,4},{6,7},{7,6},{8,9},{9,8},{10,11... | collective-permute-start | bytes 835592 | tf_op jit(solution)/shard_map/ppermute | solution.py:412
  36.5 22.1 %all-to-all-start.1 = ((bf16[8,32,544]{2,1,0:T(8,128)(2,1)}), bf16[8,32,544]{2,1,0:T(8,128)(2,1)S(1)}, u32[]{:S(2)}, u32[]{:S(2)}) async-start(bf16[8,32,544]{2,1,0:T(8,128)(2,1)} %bitcast.6), calls=%async_computation.1 | async-start | bytes 655360 | tf_op jit(solution)/shard_map/all_to_all | solution.py:348
  58.6 17.1 %all-to-all-start.4 = ((bf16[8,32,544]{2,1,0:T(8,128)(2,1)}), bf16[8,32,544]{2,1,0:T(8,128)(2,1)S(1)}, u32[]{:S(2)}, u32[]{:S(2)}) async-start(bf16[8,32,544]{2,1,0:T(8,128)(2,1)} %bitcast.12), calls=%async_computation.4 | async-start | bytes 655360 | tf_op jit(solution)/shard_map/all_to_all | solution.py:348
  75.7 17.1 %all-to-all-start.2 = ((bf16[8,32,544]{2,1,0:T(8,128)(2,1)}), bf16[8,32,544]{2,1,0:T(8,128)(2,1)S(1)}, u32[]{:S(2)}, u32[]{:S(2)}) async-start(bf16[8,32,544]{2,1,0:T(8,128)(2,1)} %normalize.2), calls=%async_computation.2 | async-start | bytes 655360 | tf_op jit(solution)/shard_map/all_to_all | solution.py:348
  79.3 17.0 %copy-start = (f32[32,16,1024]{2,1,0:T(8,128)S(1)}, f32[32,16,1024]{2,1,0:T(8,128)}, u32[]{:S(2)}) copy-start(f32[32,16,1024]{2,1,0:T(8,128)} %ssm.1) | copy-start | bytes 6291460
  79.4 0.7 copy-start.2
  92.7 17.1 %all-to-all-start.5 = ((bf16[8,32,544]{2,1,0:T(8,128)(2,1)}), bf16[8,32,544]{2,1,0:T(8,128)(2,1)S(1)}, u32[]{:S(2)}, u32[]{:S(2)}) async-start(bf16[8,32,544]{2,1,0:T(8,128)(2,1)} %copy-done.2), calls=%async_computation.5 | async-start | bytes 655360 | tf_op jit(solution)/shard_map/all_to_all | solution.py:348
  96.3 35.7 %copy-start.8 = (f32[16,1024]{1,0:T(8,128)S(1)}, f32[16,1024]{1,0:T(8,128)}, u32[]{:S(2)}) copy-start(f32[16,1024]{1,0:T(8,128)} %a_log.3) | copy-start | bytes 196612
  96.3 35.7 %copy-start.11 = (f32[1024]{0:T(1024)S(1)}, f32[1024]{0:T(1024)}, u32[]{:S(2)}) copy-start(f32[1024]{0:T(1024)} %param.19) | copy-start | bytes 12292
  96.3 35.7 %copy-start.12 = (f32[1024]{0:T(1024)S(1)}, f32[1024]{0:T(1024)}, u32[]{:S(2)}) copy-start(f32[1024]{0:T(1024)} %param.21) | copy-start | bytes 12292
  109.8 22.1 %all-to-all-start.3 = ((bf16[16,2,16,1024]{3,2,1,0:T(8,128)(2,1)}), bf16[16,2,16,1024]{3,2,1,0:T(8,128)(2,1)S(1)}, u32[]{:S(2)}, u32[]{:S(2)}) async-start(bf16[16,2,16,1024]{3,2,1,0:T(8,128)(2,1)} %bitcast.45), calls=%async_computation.3 | async-start | bytes 2097152 | tf_op jit(solution)/shard_map/all_to_all | solution.py:348
  115.5 16.5 %collective-permute-start.3 = (bf16[2,128,544]{2,1,0:T(8,128)(2,1)S(1)}, bf16[2,128,544]{2,1,0:T(8,128)(2,1)S(1)}, u32[]{:S(2)}, u32[]{:S(2)}) collective-permute-start(bf16[2,128,544]{2,1,0:T(8,128)(2,1)S(1)} %bitcast.36), channel_id=1, source_target_pairs={{0,1},{1,0},{2,3},{3,2},{4,5},{5,4},{6,7},{7,6},{8,9},{9,8},{10,11... | collective-permute-start | bytes 835592 | tf_op jit(solution)/shard_map/ppermute | solution.py:415
  116.9 38.9 %collective-permute-start.1 = (bf16[2,128,544]{2,1,0:T(8,128)(2,1)S(1)}, bf16[2,128,544]{2,1,0:T(8,128)(2,1)}, u32[]{:S(2)}, u32[]{:S(2)}) collective-permute-start(bf16[2,128,544]{2,1,0:T(8,128)(2,1)S(1)} %bitcast.34), channel_id=1, source_target_pairs={{0,1},{1,0},{2,3},{3,2},{4,5},{5,4},{6,7},{7,6},{8,9},{9,8},{10,11... | collective-permute-start | bytes 835592 | tf_op jit(solution)/shard_map/ppermute | solution.py:415
  132.0 1.6 copy-start.4
  133.6 1.2 copy-start.6
  134.8 1.2 copy-start.16
  151.0 24.9 %all-to-all-start.7 = ((bf16[16,16,1024]{2,1,0:T(8,128)(2,1)}), bf16[16,16,1024]{2,1,0:T(8,128)(2,1)S(1)}, u32[]{:S(2)}, u32[]{:S(2)}) async-start(bf16[16,16,1024]{2,1,0:T(8,128)(2,1)} %get-tuple-element.24), calls=%async_computation.7 | async-start | bytes 1048576 | tf_op jit(solution)/shard_map/all_to_all | solution.py:348
  155.9 1.6 copy-start.5
  157.5 1.2 copy-start.7
  158.7 1.2 copy-start.14
  175.9 20.6 %all-to-all-start.6 = ((bf16[16,16,1024]{2,1,0:T(8,128)(2,1)}), bf16[16,16,1024]{2,1,0:T(8,128)(2,1)S(1)}, u32[]{:S(2)}, u32[]{:S(2)}) async-start(bf16[16,16,1024]{2,1,0:T(8,128)(2,1)} %get-tuple-element.23), calls=%async_computation.6 | async-start | bytes 1048576 | tf_op jit(solution)/shard_map/all_to_all | solution.py:348
  183.1 1.6 copy-start.1

commit v2 on v1

v2 whole, which is shorter than its diff:
```python
import functools

import jax
import jax.numpy as jnp
from jax import lax
from jax.experimental import pallas as pl
from jax.experimental.pallas import tpu as pltpu
from jax.sharding import Mesh, PartitionSpec as P

EPSILON = 1e-06
NORM_FLOOR = 0.25
LOG2_E = 1.4426950408889634

GROUPS = 16
REQUESTS = 8
CHUNKS = 2
PER = REQUESTS // CHUNKS
TURN = 128
INNER = 1024
RANK = 512
STATE = 16
WIDE = RANK + 2 * STATE
SLOTS = 32
KEPT = 3
DEPTH = 8
CORES = 2
HALF = PER // CORES
SHARE = HALF * TURN // DEPTH
HEAD = 16
FETCHED = CHUNKS * (STATE + KEPT)
RETURNED = STATE + KEPT
LANES = 128
TILES = INNER // LANES
UNROLL = 4

F32 = jnp.float32
BF16 = jnp.bfloat16
SWAP = [(0, 1), (1, 0)]


def params():
    return pltpu.CompilerParams(vmem_limit_bytes=56 * 2**20)


def cost(us, bytes_accessed):
    return pl.CostEstimate(
        flops=int(us * 1.0e9), bytes_accessed=bytes_accessed, transcendentals=0
    )


def rows_to_tiles(tiles, first, rows):
    for tile in range(TILES):
        tiles[pl.ds(first + tile, rows.shape[0], stride=TILES), :] = rows[
            :, tile * LANES : (tile + 1) * LANES
        ]


def pack_kernel(slots, ssm, conv, out, states, tiles, inputs, sems):
    def copy(e):
        return pltpu.make_async_copy(ssm.at[slots[e]], states.at[e], sems.at[e])

    def begin(e, carry):
        copy(e).start()
        return carry

    def finish(e, carry):
        g, c = e // CHUNKS, e % CHUNKS
        for k in range(KEPT):
            row = pl.multiple_of((k * SLOTS + slots[e]) * TILES, TILES)
            out[g, CHUNKS * STATE + c * KEPT + k] = inputs[pl.ds(row, TILES), :].astype(BF16)
        copy(e).wait()
        rows_to_tiles(tiles, 0, states[e])
        for n in range(STATE):
            out[g, c * STATE + n] = tiles[n * TILES : (n + 1) * TILES, :].astype(BF16)
        return carry

    lax.fori_loop(0, GROUPS * CHUNKS, begin, 0)
    for k in range(KEPT):
        rows_to_tiles(inputs, k * SLOTS * TILES, conv[k])
    lax.fori_loop(0, GROUPS * CHUNKS, finish, 0)


def pack(slots, ssm, conv):
    return pl.pallas_call(
        pack_kernel,
        grid_spec=pltpu.PrefetchScalarGridSpec(
            num_scalar_prefetch=1,
            grid=(1,),
            in_specs=[
                pl.BlockSpec(memory_space=pl.ANY),
                pl.BlockSpec((KEPT, SLOTS, INNER), lambda i, s: (0, 0, 0)),
            ],
            out_specs=pl.BlockSpec((GROUPS, FETCHED, TILES, LANES), lambda i, s: (0, 0, 0, 0)),
            scratch_shapes=[
                pltpu.VMEM((GROUPS * CHUNKS, STATE, INNER), F32),
                pltpu.VMEM((STATE * TILES, LANES), F32),
                pltpu.VMEM((KEPT * SLOTS * TILES, LANES), F32),
                pltpu.SemaphoreType.DMA((GROUPS * CHUNKS,)),
            ],
        ),
        out_shape=jax.ShapeDtypeStruct((GROUPS, FETCHED, TILES, LANES), BF16),
        compiler_params=params(),
        cost_estimate=cost(3, 4 * 2**20),
        name="pack",
    )(slots, ssm, conv)


def silu(v):
    return v / (1.0 + jnp.exp(-v))


def conv_kernel(order_ref, hidden, weight, bias, x_weight, conv_out, sent, kept, rows):
    step = pl.program_id(0)
    rows[:8, :] = jnp.zeros((8, INNER), F32)
    for tile in range(TILES):
        cols = slice(tile * LANES, (tile + 1) * LANES)
        rows[8:, cols] = hidden[0, :, cols].astype(F32)
        total = jnp.zeros((TURN, LANES), F32) + bias[:, cols]
        for tap in range(KEPT + 1):
            first = 8 - KEPT + tap
            total = total + rows[first : first + TURN, cols] * weight[tap : tap + 1, cols]
        conv_out[0, :, cols] = silu(total).astype(BF16)
    part = jnp.dot(conv_out[0], x_weight[...], preferred_element_type=F32)
    part = part.reshape(TURN // SHARE, 1, SHARE, WIDE)

    @pl.when(step < PER)
    def _():
        sent[...] = part.astype(BF16)

    @pl.when(step >= PER)
    def _():
        kept[...] = part


def convolve(order, hidden, weight, bias, x_weight):
    spans = TURN // SHARE

    def share(i):
        return (i % HALF, i // HALF, 0, 0)

    return pl.pallas_call(
        conv_kernel,
        grid_spec=pltpu.PrefetchScalarGridSpec(
            num_scalar_prefetch=1,
            grid=(REQUESTS,),
            in_specs=[
                pl.BlockSpec((1, TURN, INNER), lambda i, o: (o[i], 0, 0)),
                pl.BlockSpec((KEPT + 1, INNER), lambda i, o: (0, 0)),
                pl.BlockSpec((1, INNER), lambda i, o: (0, 0)),
                pl.BlockSpec((INNER, WIDE), lambda i, o: (0, 0)),
            ],
            out_specs=[
                pl.BlockSpec((1, TURN, INNER), lambda i, o: (i, 0, 0)),
                pl.BlockSpec((spans, 1, SHARE, WIDE), lambda i, o: share(jnp.minimum(i, PER - 1))),
                pl.BlockSpec((spans, 1, SHARE, WIDE), lambda i, o: share(jnp.maximum(i - PER, 0))),
            ],
            scratch_shapes=[pltpu.VMEM((8 + TURN, INNER), F32)],
        ),
        out_shape=[
            jax.ShapeDtypeStruct((REQUESTS, TURN, INNER), BF16),
            jax.ShapeDtypeStruct((DEPTH, CHUNKS, SHARE, WIDE), BF16),
            jax.ShapeDtypeStruct((DEPTH, CHUNKS, SHARE, WIDE), F32),
        ],
        compiler_params=params(),
        cost_estimate=cost(8, 8 * 2**20),
        name="convolve",
    )(order, hidden, weight, bias, x_weight)


def head_kernel(
    order, holder, hidden, fetched, weight, bias, x_weight, conv_in, sent_in, kept_in,
    conv_out, sent, kept, rows, tiles, head, head_sent, head_kept, sems,
):
    for i in range(REQUESTS):
        c = i % PER // HALF
        for k in range(KEPT):
            tiles[k * TILES : (k + 1) * TILES, :] = fetched[
                holder[i], CHUNKS * STATE + c * KEPT + k
            ].astype(F32)
        for tile in range(TILES):
            rows[8 - KEPT : 8, tile * LANES : (tile + 1) * LANES] = tiles[
                pl.ds(tile, KEPT, stride=TILES), :
            ]
        rows[8:, :] = hidden[order[i]].astype(F32)
        total = jnp.zeros((HEAD, INNER), F32) + bias[...]
        for tap in range(KEPT + 1):
            first = 8 - KEPT + tap
            total = total + rows[first : first + HEAD, :] * weight[tap : tap + 1, :]
        head[i] = silu(total).astype(BF16)
    part = jnp.dot(
        head[...].reshape(REQUESTS * HEAD, INNER), x_weight[...], preferred_element_type=F32
    ).reshape(REQUESTS, HEAD, WIDE)
    head_sent[...] = part[:PER].astype(BF16)
    head_kept[...] = part[PER:]
    copies = []
    for i in range(REQUESTS):
        c, r = i % PER // HALF, i % HALF
        span = r * (TURN // SHARE)
        copies.append((head.at[i], conv_out.at[i, :HEAD]))
        if i < PER:
            copies.append((head_sent.at[i], sent.at[span, c, :HEAD]))
        else:
            copies.append((head_kept.at[i - PER], kept.at[span, c, :HEAD]))
    copies = [
        pltpu.make_async_copy(source, target, sems.at[k])
        for k, (source, target) in enumerate(copies)
    ]
    for one in copies:
        one.start()
    for one in copies:
        one.wait()


def put_heads(order, holder, hidden, fetched, weight, bias, x_weight, conv_out, sent, kept):
    anywhere = pl.BlockSpec(memory_space=pl.ANY)
    return pl.pallas_call(
        head_kernel,
        grid_spec=pltpu.PrefetchScalarGridSpec(
            num_scalar_prefetch=2,
            grid=(1,),
            in_specs=[
                pl.BlockSpec((REQUESTS, HEAD, INNER), lambda i, o, h: (0, 0, 0)),
                pl.BlockSpec((GROUPS, FETCHED, TILES, LANES), lambda i, o, h: (0, 0, 0, 0)),
                pl.BlockSpec((KEPT + 1, INNER), lambda i, o, h: (0, 0)),
                pl.BlockSpec((1, INNER), lambda i, o, h: (0, 0)),
                pl.BlockSpec((INNER, WIDE), lambda i, o, h: (0, 0)),
                anywhere,
                anywhere,
                anywhere,
            ],
            out_specs=[anywhere, anywhere, anywhere],
            scratch_shapes=[
                pltpu.VMEM((8 + HEAD, INNER), F32),
                pltpu.VMEM((KEPT * TILES, LANES), F32),
                pltpu.VMEM((REQUESTS, HEAD, INNER), BF16),
                pltpu.VMEM((PER, HEAD, WIDE), BF16),
                pltpu.VMEM((PER, HEAD, WIDE), F32),
                pltpu.SemaphoreType.DMA((2 * REQUESTS,)),
            ],
        ),
        out_shape=[
            jax.ShapeDtypeStruct(conv_out.shape, conv_out.dtype),
            jax.ShapeDtypeStruct(sent.shape, sent.dtype),
            jax.ShapeDtypeStruct(kept.shape, kept.dtype),
        ],
        input_output_aliases={7: 0, 8: 1, 9: 2},
        compiler_params=params(),
        cost_estimate=cost(3, 4 * 2**20),
        name="put_heads",
    )(order, holder, hidden, fetched, weight, bias, x_weight, conv_out, sent, kept)


def norm_kernel(parts, *outs):
    for c in range(CHUNKS):
        total = parts[0, c].astype(F32)
        for k in range(1, DEPTH):
            total = total + parts[k, c].astype(F32)
        rank = total[:, :RANK]
        inject = total[:, RANK : RANK + STATE]
        readout = total[:, RANK + STATE :]
        rank = rank * lax.rsqrt(jnp.mean(rank * rank, axis=1, keepdims=True) + EPSILON)
        inject = inject * lax.rsqrt(
            jnp.maximum(jnp.mean(inject * inject, axis=1, keepdims=True), NORM_FLOOR)
        )
        readout = readout * lax.rsqrt(
            jnp.maximum(jnp.mean(readout * readout, axis=1, keepdims=True), NORM_FLOOR)
        )
        joined = jnp.concatenate([rank, inject, readout], axis=1).astype(BF16)
        for k in range(DEPTH):
            outs[c][k] = joined


def normalize(parts):
    return pl.pallas_call(
        norm_kernel,
        out_shape=[jax.ShapeDtypeStruct((DEPTH, SHARE, WIDE), BF16)] * CHUNKS,
        compiler_params=params(),
        cost_estimate=cost(1.5, 2**20),
        name="normalize",
    )(parts)


def scan_kernel(
    order_ref, holder_ref, own, other, dt_weight, dt_bias, a_log, skip, conv, gate, start, last,
    base, gated, final, dts, us, spread, rates,
):
    step = pl.program_id(0)

    @pl.when(step == 0)
    def _():
        rows_to_tiles(rates, 0, -LOG2_E * jnp.exp(a_log[...]))

    normed = jnp.where(step < HALF, own[0].astype(F32), other[0].astype(F32))
    columns = normed[:, RANK:].T
    for t in range(TURN):
        spread[t * 2 * STATE : (t + 1) * 2 * STATE, :] = jnp.broadcast_to(
            columns[:, t : t + 1], (2 * STATE, LANES)
        )
    rows_to_tiles(dts, 0, last[0].astype(F32)[HEAD - KEPT :, :])
    for k in range(KEPT):
        final[0, STATE + k] = dts[k * TILES : (k + 1) * TILES, :].astype(BF16)
    rank = normed[:, :RANK].astype(BF16)
    pair = 2 * LANES
    for block in range(INNER // pair):
        cols = slice(block * pair, (block + 1) * pair)
        raw = jnp.dot(rank, dt_weight[:, cols], preferred_element_type=F32) + dt_bias[:, cols]
        dt = jnp.maximum(raw, 0.0) + jnp.log1p(jnp.exp(-jnp.abs(raw)))
        for k in range(2):
            tile = 2 * block + k
            dts[pl.ds(tile, TURN, stride=TILES), :] = dt[:, k * LANES : (k + 1) * LANES]
            us[pl.ds(tile, TURN, stride=TILES), :] = conv[
                0, :, tile * LANES : (tile + 1) * LANES
            ].astype(F32)
    decay = [rates[n * TILES : (n + 1) * TILES, :] for n in range(STATE)]

    def steps(i, carried):
        carried = list(carried)
        for k in range(UNROLL):
            t = i * UNROLL + k
            at = pl.multiple_of(t * TILES, TILES)
            row = pl.multiple_of(t * 2 * STATE, 2 * STATE)
            dt = dts[pl.ds(at, TILES), :]
            drive = dt * us[pl.ds(at, TILES), :]
            sums = [None] * 4
            for n in range(STATE):
                carried[n] = (
                    jnp.exp2(dt * decay[n]) * carried[n] + drive * spread[pl.ds(row + n, 1), :]
                )
                term = carried[n] * spread[pl.ds(row + STATE + n, 1), :]
                sums[n % 4] = term if sums[n % 4] is None else sums[n % 4] + term
            dts[pl.ds(at, TILES), :] = (sums[0] + sums[1]) + (sums[2] + sums[3])
        return tuple(carried)

    carried = tuple(start[0, n].astype(F32) for n in range(STATE))
    carried = lax.fori_loop(0, TURN // UNROLL, steps, carried)
    for n in range(STATE):
        final[0, n] = carried[n].astype(BF16)
    for tile in range(TILES):
        cols = slice(tile * LANES, (tile + 1) * LANES)
        z = gate[0, :, cols].astype(F32)
        y = dts[pl.ds(tile, TURN, stride=TILES), :] + skip[:, cols] * conv[0, :, cols].astype(F32)
        gated[0, :, cols] = (y * silu(z)).astype(BF16)


def scan(c, order, holder, own, other, dt_weight, dt_bias, a_log, skip, conv, gate, fetched, hidden, base):
    whole = lambda shape: pl.BlockSpec(shape, lambda i, o, h: (0,) * len(shape))

    def at(i):
        return jnp.where(i < HALF, PER + c * HALF + i, c * HALF + i - HALF)

    return pl.pallas_call(
        scan_kernel,
        grid_spec=pltpu.PrefetchScalarGridSpec(
            num_scalar_prefetch=2,
            grid=(PER,),
            in_specs=[
                pl.BlockSpec((1, TURN, WIDE), lambda i, o, h: (jnp.minimum(i, HALF - 1), 0, 0)),
                pl.BlockSpec((1, TURN, WIDE), lambda i, o, h: (jnp.maximum(i - HALF, 0), 0, 0)),
                whole((RANK, INNER)),
                whole((1, INNER)),
                whole((STATE, INNER)),
                whole((1, INNER)),
                pl.BlockSpec((1, TURN, INNER), lambda i, o, h: (at(i), 0, 0)),
                pl.BlockSpec((1, TURN, INNER), lambda i, o, h: (o[at(i)], 0, 0)),
                pl.BlockSpec((1, STATE, TILES, LANES), lambda i, o, h: (h[at(i)], c, 0, 0)),
                pl.BlockSpec((1, HEAD, INNER), lambda i, o, h: (o[at(i)], TURN // HEAD - 1, 0)),
                pl.BlockSpec(memory_space=pl.ANY),
            ],
            out_specs=[
                pl.BlockSpec((1, TURN, INNER), lambda i, o, h: (o[at(i)], 0, 0)),
                pl.BlockSpec((1, RETURNED, TILES, LANES), lambda i, o, h: (h[at(i)], 0, 0, 0)),
            ],
            scratch_shapes=[
                pltpu.VMEM((TURN * TILES, LANES), F32),
                pltpu.VMEM((TURN * TILES, LANES), F32),
                pltpu.VMEM((TURN * 2 * STATE, LANES), F32),
                pltpu.VMEM((STATE * TILES, LANES), F32),
            ],
        ),
        out_shape=[
            jax.ShapeDtypeStruct((REQUESTS, TURN, INNER), BF16),
            jax.ShapeDtypeStruct((GROUPS, RETURNED, TILES, LANES), BF16),
        ],
        input_output_aliases={12: 0} if base is not None else {},
        compiler_params=params(),
        cost_estimate=cost(15, 4 * 2**20),
        name="scan",
    )(order, holder, own, other, dt_weight, dt_bias, a_log, skip, conv, gate, fetched, hidden,
      base if base is not None else skip)


def store_kernel(slots, came, ssm_in, conv, new_ssm, new_conv, wide, tiles, inputs, sems):
    for k in range(KEPT):
        rows_to_tiles(inputs, k * SLOTS * TILES, conv[k])

    def copy(g):
        return pltpu.make_async_copy(wide.at[g], new_ssm.at[slots[g]], sems.at[g])

    def begin(g, carry):
        @pl.when(slots[g] < SLOTS)
        def _():
            for n in range(STATE):
                tiles[n * TILES : (n + 1) * TILES, :] = came[g, n].astype(F32)
            for tile in range(TILES):
                wide[g, :, tile * LANES : (tile + 1) * LANES] = tiles[
                    pl.ds(tile, STATE, stride=TILES), :
                ]
            copy(g).start()
            for k in range(KEPT):
                row = pl.multiple_of((k * SLOTS + slots[g]) * TILES, TILES)
                inputs[pl.ds(row, TILES), :] = came[g, STATE + k].astype(F32)

        return carry

    def finish(g, carry):
        @pl.when(slots[g] < SLOTS)
        def _():
            copy(g).wait()

        return carry

    lax.fori_loop(0, GROUPS, begin, 0)
    for k in range(KEPT):
        for tile in range(TILES):
            new_conv[k, :, tile * LANES : (tile + 1) * LANES] = inputs[
                pl.ds(k * SLOTS * TILES + tile, SLOTS, stride=TILES), :
            ]
    lax.fori_loop(0, GROUPS, finish, 0)


def store(slots, came, ssm, conv):
    return pl.pallas_call(
        store_kernel,
        grid_spec=pltpu.PrefetchScalarGridSpec(
            num_scalar_prefetch=1,
            grid=(1,),
            in_specs=[
                pl.BlockSpec((GROUPS, RETURNED, TILES, LANES), lambda i, s: (0, 0, 0, 0)),
                pl.BlockSpec(memory_space=pl.ANY),
                pl.BlockSpec((KEPT, SLOTS, INNER), lambda i, s: (0, 0, 0)),
            ],
            out_specs=[
                pl.BlockSpec(memory_space=pl.ANY),
                pl.BlockSpec((KEPT, SLOTS, INNER), lambda i, s: (0, 0, 0)),
            ],
            scratch_shapes=[
                pltpu.VMEM((GROUPS, STATE, INNER), F32),
                pltpu.VMEM((STATE * TILES, LANES), F32),
                pltpu.VMEM((KEPT * SLOTS * TILES, LANES), F32),
                pltpu.SemaphoreType.DMA((GROUPS,)),
            ],
        ),
        out_shape=[
            jax.ShapeDtypeStruct((SLOTS, STATE, INNER), F32),
            jax.ShapeDtypeStruct((KEPT, SLOTS, INNER), F32),
        ],
        input_output_aliases={2: 0},
        compiler_params=params(),
        cost_estimate=cost(3, 2 * 2**20),
        name="store",
    )(slots, came, ssm, conv)


def exchange(values, axis):
    return lax.all_to_all(values, axis, split_axis=0, concat_axis=0, tiled=True)


def body(
    hidden_x,
    gate_z,
    conv_weight,
    conv_bias,
    x_weight,
    dt_weight,
    dt_bias,
    a_log,
    skip_gain,
    ssm_cache,
    conv_cache,
    holder_of,
    slot_of,
):
    me = lax.axis_index("dp")
    core = lax.axis_index("core")
    holders = holder_of.reshape(GROUPS, REQUESTS)
    places = slot_of.reshape(GROUPS, REQUESTS)

    keys = holders * REQUESTS + jnp.arange(REQUESTS, dtype=jnp.int32)
    rank = jnp.sum((keys[:, None, :] < keys[:, :, None]).astype(jnp.int32), axis=2)
    served = (holders == me)[:, None, :] & (
        rank[:, None, :] % CHUNKS == jnp.arange(CHUNKS, dtype=jnp.int32)[None, :, None]
    )
    slots = jnp.sum(jnp.where(served, places[:, None, :], 0), axis=2)
    targets = jnp.where(jnp.any(served, axis=2), slots, SLOTS)

    at = jnp.arange(REQUESTS, dtype=jnp.int32)
    side = jnp.where(at < PER, 1 - core, core)
    number = (side * HALF + at % HALF) * CHUNKS + at % PER // HALF
    chosen = rank[me][None, :] == number[:, None]
    order = jnp.sum(jnp.where(chosen, at[None, :], 0), axis=1)
    holder = jnp.sum(jnp.where(chosen, holders[me][None, :], 0), axis=1)

    conv_rows = jnp.swapaxes(conv_cache, 0, 1)
    bias = conv_bias.reshape(1, INNER)
    fetched = exchange(pack(slots.reshape(-1), ssm_cache, conv_rows), "dp")
    conv, sent, kept = convolve(order, hidden_x, conv_weight, bias, x_weight)
    conv, sent, kept = put_heads(
        order, holder, hidden_x, fetched, conv_weight, bias, x_weight, conv, sent, kept
    )
    parts = (kept + lax.ppermute(sent, "core", SWAP).astype(F32)).astype(BF16)
    shares = normalize(exchange(parts, "z"))

    own = [exchange(share, "z").reshape(HALF, TURN, WIDE) for share in shares]
    other = [lax.ppermute(half, "core", SWAP) for half in own]
    gated = None
    came = []
    for c in range(CHUNKS):
        gated, final = scan(
            c,
            order,
            holder,
            own[c],
            other[c],
            dt_weight,
            dt_bias.reshape(1, INNER),
            a_log,
            skip_gain.reshape(1, INNER),
            conv,
            gate_z,
            fetched,
            hidden_x,
            gated,
        )
        came.append(exchange(final, "dp"))
    new_ssm, new_conv = ssm_cache, conv_rows
    for c in range(CHUNKS):
        new_ssm, new_conv = store(targets[:, c], came[c], new_ssm, new_conv)
    return (gated, new_ssm, jnp.swapaxes(new_conv, 0, 1))


def solution(mesh):
    fine = Mesh(mesh.devices.reshape(GROUPS, DEPTH, CORES), ("dp", "z", "core"))
    tensor = ("z", "core")
    placed = (
        P("dp", None, tensor),
        P("dp", None, tensor),
        P(None, tensor),
        P(tensor),
        P(tensor, None),
        P(None, tensor),
        P(tensor),
        P(None, tensor),
        P(tensor),
        P("dp", None, tensor),
        P("dp", None, tensor),
        P(),
        P(),
    )
    return jax.shard_map(
        body,
        mesh=fine,
        in_specs=placed,
        out_specs=(P("dp", None, tensor),) * 3,
        check_vma=False,
    )
```

time: 199 us -> 172 us (0.86)
  waiting for transfers between devices: 71.5 us -> 25.9 us
  blocking collectives: 0 us -> 44.8 us
  starting transfers between devices: 45 us -> 23.3 us
  local copies, waits for them, and re-layouts: 24.2 us -> 9.88 us
  Pallas kernels: 52.6 us -> 63.5 us
    all_to_all x8 -> x4, waiting for transfers between devices: 71.5 us -> 23.6 us  [exchange(): return lax.all_to_all(values, axis, split_axis=0, concat_axis=0, tiled=True)]
    all_to_all x0 -> x2, blocking collectives: none -> 44.8 us  [exchange(): return lax.all_to_all(values, axis, split_axis=0, concat_axis=0, tiled=True)]
    all_to_all x8 -> x4, starting transfers between devices: 43.8 us -> 23.1 us  [exchange(): return lax.all_to_all(values, axis, split_axis=0, concat_axis=0, tiled=True)]
    unnamed x41 -> x22, local copies, waits for them, and re-layouts: 16 us -> 8.08 us
    pallas_call x1 -> x2, Pallas kernels: 1.45 us -> 7.33 us  [store(): pl.pallas_call(store_kernel, grid_spec=pltpu.PrefetchScalarGridSpec(num_s...]
    gather x4 -> x0, local copies, waits for them, and re-layouts: 3.69 us -> none  [the longest x1 1.62 us: body(): ssm_cache[slots].astype(BF16)]
    pallas_call x2 -> x1, Pallas kernels: 8.37 us -> 11 us  [convolve(): pl.pallas_call(conv_kernel, grid_spec=pltpu.PrefetchScalarGridSpec(num_sc...]
    pallas_call x2, Pallas kernels: 30.9 us -> 33.2 us  [scan(): pl.pallas_call(scan_kernel, grid_spec=pltpu.PrefetchScalarGridSpec(num_sc...]
  transfers between devices with their start and end apart: 12 -> 7, of which waited for: 6 -> 4; matrix products, arithmetic and copies ran while one was open for 4% -> 2% of each run, Pallas kernels for 24% -> 28%
where the time goes in v2:
time: 172 us; the launch traced here: 171 us
  Pallas kernels  63.5 us (37%)
  blocking collectives  44.8 us (26%)
  waiting for transfers between devices  25.9 us (15%)
  starting transfers between devices  23.3 us (14%)
  local copies, waits for them, and re-layouts  9.88 us (6%)
  other arithmetic  2.37 us (1%)
    all_to_all x2, blocking collectives, exchange(): return lax.all_to_all(values, axis, split_axis=0, concat_axis=0, tiled=True)  44.8 us
    pallas_call x2, Pallas kernels, scan(): pl.pallas_call(scan_kernel, grid_spec=pltpu.PrefetchScalarGridSpec(num_sc...  33.2 us
    all_to_all x4, waiting for transfers between devices, exchange(): return lax.all_to_all(values, axis, split_axis=0, concat_axis=0, tiled=True)  23.6 us
    all_to_all x4, starting transfers between devices, exchange(): return lax.all_to_all(values, axis, split_axis=0, concat_axis=0, tiled=True)  23.1 us
    pallas_call x1, Pallas kernels, convolve(): pl.pallas_call(conv_kernel, grid_spec=pltpu.PrefetchScalarGridSpec(num_sc...  11 us
    unnamed x22, local copies, waits for them, and re-layouts  8.08 us
    pallas_call x2, Pallas kernels, store(): pl.pallas_call(store_kernel, grid_spec=pltpu.PrefetchScalarGridSpec(num_s...  7.33 us
    pallas_call x1, Pallas kernels, pack(): pl.pallas_call(pack_kernel, grid_spec=pltpu.PrefetchScalarGridSpec(num_sc...  5.58 us
  transfers between devices with their start and end apart: 7, of which 4 were waited for; matrix products, arithmetic and copies ran while one was open for 2% of the time, Pallas kernels for 28%

profile of v2, /device:TPU:8, one launch (start us, length us, event | category | flops | bytes accessed | tf_op | source)
XLA Modules:
  0.0 170.6 jit_solution(3206419499084555684)
XLA Ops:
  0.6 0.0 copy-start.6
  0.6 0.0 copy-start.7
  0.7 3.2 %copy.49.ssm.ssm_in = f32[32,16,1024]{2,1,0:T(8,128)} copy(f32[32,16,1024]{2,1,0:T(8,128)} %param.22) | data formatting | bytes 4194304
  3.8 0.0 copy-done.6
  3.8 0.1 reshape.114
  3.9 0.1 copy.37
  4.0 0.1 copy.35
  4.1 0.0 copy-done.7
  4.1 0.1 broadcast_in_dim.60
  4.2 0.1 copy.38
  4.3 0.1 copy.39
  4.4 0.6 reshape.115.slots
  5.0 5.6 %pack.1 = bf16[16,38,8,128]{3,2,1,0:T(8,128)(2,1)} custom-call(s32[32]{0:T(128)} %reshape.115.slots, f32[32,16,1024]{2,1,0:T(8,128)} %copy.49.ssm.ssm_in, f32[3,32,1024]{2,1,0:T(8,128)} %bitcast.17), custom_call_target="tpu_custom_call" | custom-call | flops 3000000000 | bytes 4194304 | tf_op jit(solution)/shard_map/pack/pallas_call | solution.py:84
  10.6 0.0 copy-start.1
  10.6 7.6 %all-to-all-start = ((bf16[16,38,8,128]{3,2,1,0:T(8,128)(2,1)}), bf16[16,38,8,128]{3,2,1,0:T(8,128)(2,1)S(1)}, u32[]{:S(2)}, u32[]{:S(2)}) async-start(bf16[16,38,8,128]{3,2,1,0:T(8,128)(2,1)} %pack.1), calls=%async_computation | async-start | bytes 2490368 | tf_op jit(solution)/shard_map/all_to_all | solution.py:465
  18.2 0.2 dynamic-slice_reduce_fusion
  18.4 0.0 copy-done.1
  18.4 1.4 copy.41.x_weight
  19.8 0.8 fusion.3
  20.6 11.0 %convolve.1 = (bf16[8,128,1024]{2,1,0:T(8,128)(2,1)}, bf16[8,2,32,544]{3,2,1,0:T(8,128)(2,1)}, f32[8,2,32,544]{3,2,1,0:T(8,128)}) custom-call(s32[8]{0:T(128)} %get-tuple-element.36.order_ref.order, bf16[8,128,1024]{2,1,0:T(8,128)(2,1)} %last.3, f32[4,1024]{1,0:T(4,128)} %weight.3, f32[1,1024]{1,0:T(1,128)} %bitcast.19, bf16[1024,544]{1,0:T(8,128)(2,1)} %copy.41.x_weight), custom_call_target="tpu_custom_call" | custom-call | flops 8000000000 | bytes 8388608 | tf_op jit(solution)/shard_map/convolve/pallas_call | solution.py:141
  31.6 5.3 %all-to-all-done.fetched.start = bf16[16,38,8,128]{3,2,1,0:T(8,128)(2,1)S(1)} async-done(((bf16[16,38,8,128]{3,2,1,0:T(8,128)(2,1)}), bf16[16,38,8,128]{3,2,1,0:T(8,128)(2,1)S(1)}, u32[]{:S(2)}, u32[]{:S(2)}) %all-to-all-start) | async-done | bytes 1245216 | tf_op jit(solution)/shard_map/all_to_all | solution.py:465
  36.9 0.0 copy-start
  36.9 1.1 copy-done
  37.9 4.4 %put_heads.1 = (bf16[8,128,1024]{2,1,0:T(8,128)(2,1)}, bf16[8,2,32,544]{3,2,1,0:T(8,128)(2,1)}, f32[8,2,32,544]{3,2,1,0:T(8,128)}) custom-call(s32[8]{0:T(128)} %get-tuple-element.36.order_ref.order, s32[8]{0:T(128)} %get-tuple-element.35.holder.holder_ref, bf16[8,128,1024]{2,1,0:T(8,128)(2,1)} %last.3, ...), custom_call_target="tpu_custom_call", output_to_operand_aliasing={{0}: (7, {}), {1}: (8, {}), {2}: (9, {})} | custom-call | flops 3000000000 | bytes 4194304 | tf_op jit(solution)/shard_map/put_heads/pallas_call | solution.py:216
  42.3 0.1 collective-permute-start
  42.4 2.3 %collective-permute-done = bf16[8,2,32,544]{3,2,1,0:T(8,128)(2,1)S(1)} collective-permute-done((bf16[8,2,32,544]{3,2,1,0:T(8,128)(2,1)}, bf16[8,2,32,544]{3,2,1,0:T(8,128)(2,1)S(1)}, u32[]{:S(2)}, u32[]{:S(2)}) %collective-permute-start) | collective-permute-done | bytes 557088 | tf_op jit(solution)/shard_map/ppermute | solution.py:510
  44.7 1.5 add_convert_fusion
  46.2 29.0 %all_to_all.30.parts = bf16[8,2,32,544]{3,2,1,0:T(8,128)(2,1)} all-to-all(bf16[8,2,32,544]{3,2,1,0:T(8,128)(2,1)S(1)} %add_convert_fusion), channel_id=1, replica_groups=mesh['dp'=16,'z'=8,'core'=2] {'z'}, dimensions={0} | all-to-all | bytes 1114112 | tf_op jit(solution)/shard_map/all_to_all | solution.py:465
  75.2 2.1 %normalize.1 = (bf16[8,32,544]{2,1,0:T(8,128)(2,1)}, bf16[8,32,544]{2,1,0:T(8,128)(2,1)}) custom-call(bf16[8,2,32,544]{3,2,1,0:T(8,128)(2,1)} %all_to_all.30.parts), custom_call_target="tpu_custom_call" | custom-call | flops 1500000000 | bytes 1048576 | tf_op jit(solution)/shard_map/normalize/pallas_call | solution.py:274
  77.3 15.8 %all_to_all.31 = bf16[8,32,544]{2,1,0:T(8,128)(2,1)S(1)} all-to-all(bf16[8,32,544]{2,1,0:T(8,128)(2,1)} %get-tuple-element.26), channel_id=1, replica_groups=mesh['dp'=16,'z'=8,'core'=2] {'z'}, dimensions={0} | all-to-all | bytes 557056 | tf_op jit(solution)/shard_map/all_to_all | solution.py:465
  93.1 0.0 copy-start.5
  93.1 3.4 %all-to-all-start.2 = ((bf16[8,32,544]{2,1,0:T(8,128)(2,1)}), bf16[8,32,544]{2,1,0:T(8,128)(2,1)S(1)}, u32[]{:S(2)}, u32[]{:S(2)}) async-start(bf16[8,32,544]{2,1,0:T(8,128)(2,1)} %get-tuple-element.24), calls=%async_computation.2 | async-start | bytes 655360 | tf_op jit(solution)/shard_map/all_to_all | solution.py:465
  96.5 0.1 collective-permute-start.2
  96.6 11.0 %all-to-all-done.2 = bf16[8,32,544]{2,1,0:T(8,128)(2,1)S(1)} async-done(((bf16[8,32,544]{2,1,0:T(8,128)(2,1)}), bf16[8,32,544]{2,1,0:T(8,128)(2,1)S(1)}, u32[]{:S(2)}, u32[]{:S(2)}) %all-to-all-start.2) | async-done | bytes 278560 | tf_op jit(solution)/shard_map/all_to_all | solution.py:465
  107.6 0.0 copy-start.4
  107.6 0.0 collective-permute-start.1
  107.6 0.0 collective-permute-done.2.other
  107.6 0.0 copy-start.9
  107.6 0.0 copy-done.5
  107.6 0.8 copy-done.9
  108.4 16.6 %scan.2 = (bf16[8,128,1024]{2,1,0:T(8,128)(2,1)}, bf16[16,19,8,128]{3,2,1,0:T(8,128)(2,1)}) custom-call(s32[8]{0:T(128)} %get-tuple-element.36.order_ref.order, s32[8]{0:T(128)} %get-tuple-element.35.holder.holder_ref, bf16[2,128,544]{2,1,0:T(8,128)(2,1)} %bitcast.16, bf16[2,128,544]{2,1,0:T(8,128)(2,1)} %copy-done.9, bf16[512,1024]{1,0:T(8,128)(2,1)} %dt_weight.3, ...), custom_call_target="tpu_custom_call" | custom-call | flops 15000000512 | bytes 4194304 | tf_op jit(solution)/shard_map/scan/pallas_call | solution.py:351
  125.0 0.0 copy-done.4
  125.0 4.9 %all-to-all-start.5 = ((bf16[16,19,8,128]{3,2,1,0:T(8,128)(2,1)}), bf16[16,19,8,128]{3,2,1,0:T(8,128)(2,1)S(1)}, u32[]{:S(2)}, u32[]{:S(2)}) async-start(bf16[16,19,8,128]{3,2,1,0:T(8,128)(2,1)} %get-tuple-element.30), calls=%async_computation.5 | async-start | bytes 1245184 | tf_op jit(solution)/shard_map/all_to_all | solution.py:465
  129.9 0.0 collective-permute-done.1.other
  129.9 0.0 copy-start.8
  129.9 0.7 copy-done.8
  130.7 16.6 %scan.3 = (bf16[8,128,1024]{2,1,0:T(8,128)(2,1)}, bf16[16,19,8,128]{3,2,1,0:T(8,128)(2,1)}) custom-call(s32[8]{0:T(128)} %get-tuple-element.36.order_ref.order, s32[8]{0:T(128)} %get-tuple-element.35.holder.holder_ref, bf16[2,128,544]{2,1,0:T(8,128)(2,1)} %bitcast.14, bf16[2,128,544]{2,1,0:T(8,128)(2,1)} %copy-done.8, ...), custom_call_target="tpu_custom_call", output_to_operand_aliasing={{0}: (12, {})} | custom-call | flops 15000000512 | bytes 4194304 | tf_op jit(solution)/shard_map/scan/pallas_call | solution.py:351
  147.2 0.0 all-to-all-done.5.came
  147.3 0.0 copy-start.2
  147.3 7.3 %all-to-all-start.4 = ((bf16[16,19,8,128]{3,2,1,0:T(8,128)(2,1)}), bf16[16,19,8,128]{3,2,1,0:T(8,128)(2,1)S(1)}, u32[]{:S(2)}, u32[]{:S(2)}) async-start(bf16[16,19,8,128]{3,2,1,0:T(8,128)(2,1)} %get-tuple-element.29), calls=%async_computation.4 | async-start | bytes 1245184 | tf_op jit(solution)/shard_map/all_to_all | solution.py:465
  154.6 0.5 slice_bitcast_fusion
  155.1 0.0 copy-done.2
  155.1 3.7 %store.2 = (f32[32,16,1024]{2,1,0:T(8,128)}, f32[3,32,1024]{2,1,0:T(8,128)}) custom-call(s32[16]{0:T(128)} %get-tuple-element.37.slots, bf16[16,19,8,128]{3,2,1,0:T(8,128)(2,1)} %copy-done.2, f32[32,16,1024]{2,1,0:T(8,128)} %copy.49.ssm.ssm_in, f32[3,32,1024]{2,1,0:T(8,128)} %bitcast.18), custom_call_target="tpu_custom_call", output_to_operand_aliasing={{0}: (2, {})} | custom-call | flops 3000000000 | bytes 2097152 | tf_op jit(solution)/shard_map/store/pallas_call | solution.py:432
  158.8 7.3 %all-to-all-done.4.came = bf16[16,19,8,128]{3,2,1,0:T(8,128)(2,1)S(1)} async-done(((bf16[16,19,8,128]{3,2,1,0:T(8,128)(2,1)}), bf16[16,19,8,128]{3,2,1,0:T(8,128)(2,1)S(1)}, u32[]{:S(2)}, u32[]{:S(2)}) %all-to-all-start.4) | async-done | bytes 622624 | tf_op jit(solution)/shard_map/all_to_all | solution.py:465
  166.1 0.0 copy-start.3
  166.1 0.8 copy-done.3
  166.9 3.7 %store.3 = (f32[32,16,1024]{2,1,0:T(8,128)}, f32[3,32,1024]{2,1,0:T(8,128)}) custom-call(s32[16]{0:T(128)} %get-tuple-element.38.slots, bf16[16,19,8,128]{3,2,1,0:T(8,128)(2,1)} %copy-done.3, f32[32,16,1024]{2,1,0:T(8,128)} %get-tuple-element.31.ssm_in, f32[3,32,1024]{2,1,0:T(8,128)} %get-tuple-element.32.conv), custom_call_target="tpu_custom_call", output_to_operand_aliasing={{0}: (2, {})} | custom-call | flops 3000000000 | bytes 2097152 | tf_op jit(solution)/shard_map/store/pallas_call | solution.py:432
  (9 shorter events, 0.1 us)
Async XLA Ops:
  0.6 3.2 %copy-start.6 = (s32[128]{0:T(128)S(1)}, s32[128]{0:T(128)}, u32[]{:S(2)}) copy-start(s32[128]{0:T(128)} %param.24) | copy-start | bytes 1540
  0.6 3.5 %copy-start.7 = (s32[128]{0:T(128)S(1)}, s32[128]{0:T(128)}, u32[]{:S(2)}) copy-start(s32[128]{0:T(128)} %param.25) | copy-start | bytes 1540
  10.6 7.8 %copy-start.1 = (bf16[1024,544]{0,1:T(8,128)(2,1)S(1)}, bf16[1024,544]{0,1:T(8,128)(2,1)}, u32[]{:S(2)}) copy-start(bf16[1024,544]{0,1:T(8,128)(2,1)} %param.17) | copy-start | bytes 3342340
  10.6 26.2 %all-to-all-start = ((bf16[16,38,8,128]{3,2,1,0:T(8,128)(2,1)}), bf16[16,38,8,128]{3,2,1,0:T(8,128)(2,1)S(1)}, u32[]{:S(2)}, u32[]{:S(2)}) async-start(bf16[16,38,8,128]{3,2,1,0:T(8,128)(2,1)} %pack.1), calls=%async_computation | async-start | bytes 2490368 | tf_op jit(solution)/shard_map/all_to_all | solution.py:465
  36.9 1.1 copy-start
  42.3 2.4 %collective-permute-start = (bf16[8,2,32,544]{3,2,1,0:T(8,128)(2,1)}, bf16[8,2,32,544]{3,2,1,0:T(8,128)(2,1)S(1)}, u32[]{:S(2)}, u32[]{:S(2)}) collective-permute-start(bf16[8,2,32,544]{3,2,1,0:T(8,128)(2,1)} %get-tuple-element.23), channel_id=1, source_target_pairs={{0,1},{1,0},{2,3},{3,2},{4,5},{5,4},{6,7},{7,6},{8,9},{9,8},{10,11... | collective-permute-start | bytes 1671176 | tf_op jit(solution)/shard_map/ppermute | solution.py:510
  93.1 14.6 %copy-start.5 = (bf16[8,32,544]{2,1,0:T(8,128)(2,1)}, bf16[8,32,544]{2,1,0:T(8,128)(2,1)S(1)}, u32[]{:S(2)}) copy-start(bf16[8,32,544]{2,1,0:T(8,128)(2,1)S(1)} %all_to_all.31) | copy-start | bytes 835588
  93.1 14.5 %all-to-all-start.2 = ((bf16[8,32,544]{2,1,0:T(8,128)(2,1)}), bf16[8,32,544]{2,1,0:T(8,128)(2,1)S(1)}, u32[]{:S(2)}, u32[]{:S(2)}) async-start(bf16[8,32,544]{2,1,0:T(8,128)(2,1)} %get-tuple-element.24), calls=%async_computation.2 | async-start | bytes 655360 | tf_op jit(solution)/shard_map/all_to_all | solution.py:465
  96.5 11.1 %collective-permute-start.2 = (bf16[2,128,544]{2,1,0:T(8,128)(2,1)S(1)}, bf16[2,128,544]{2,1,0:T(8,128)(2,1)S(1)}, u32[]{:S(2)}, u32[]{:S(2)}) collective-permute-start(bf16[2,128,544]{2,1,0:T(8,128)(2,1)S(1)} %bitcast.15), channel_id=1, source_target_pairs={{0,1},{1,0},{2,3},{3,2},{4,5},{5,4},{6,7},{7,6},{8,9},{9,8},{10,11... | collective-permute-start | bytes 835592 | tf_op jit(solution)/shard_map/ppermute | solution.py:514
  107.6 17.4 %copy-start.4 = (bf16[8,32,544]{2,1,0:T(8,128)(2,1)}, bf16[8,32,544]{2,1,0:T(8,128)(2,1)S(1)}, u32[]{:S(2)}) copy-start(bf16[8,32,544]{2,1,0:T(8,128)(2,1)S(1)} %all-to-all-done.2) | copy-start | bytes 835588
  107.6 22.3 %collective-permute-start.1 = (bf16[2,128,544]{2,1,0:T(8,128)(2,1)S(1)}, bf16[2,128,544]{2,1,0:T(8,128)(2,1)S(1)}, u32[]{:S(2)}, u32[]{:S(2)}) collective-permute-start(bf16[2,128,544]{2,1,0:T(8,128)(2,1)S(1)} %bitcast.13), channel_id=1, source_target_pairs={{0,1},{1,0},{2,3},{3,2},{4,5},{5,4},{6,7},{7,6},{8,9},{9,8},{10,11... | collective-permute-start | bytes 835592 | tf_op jit(solution)/shard_map/ppermute | solution.py:514
  107.6 0.8 copy-start.9
  125.0 22.2 %all-to-all-start.5 = ((bf16[16,19,8,128]{3,2,1,0:T(8,128)(2,1)}), bf16[16,19,8,128]{3,2,1,0:T(8,128)(2,1)S(1)}, u32[]{:S(2)}, u32[]{:S(2)}) async-start(bf16[16,19,8,128]{3,2,1,0:T(8,128)(2,1)} %get-tuple-element.30), calls=%async_computation.5 | async-start | bytes 1245184 | tf_op jit(solution)/shard_map/all_to_all | solution.py:465
  129.9 0.8 copy-start.8
  147.3 7.9 %copy-start.2 = (bf16[16,19,8,128]{3,2,1,0:T(8,128)(2,1)}, bf16[16,19,8,128]{3,2,1,0:T(8,128)(2,1)S(1)}, u32[]{:S(2)}) copy-start(bf16[16,19,8,128]{3,2,1,0:T(8,128)(2,1)S(1)} %all-to-all-done.5.came) | copy-start | bytes 1867780
  147.3 18.8 %all-to-all-start.4 = ((bf16[16,19,8,128]{3,2,1,0:T(8,128)(2,1)}), bf16[16,19,8,128]{3,2,1,0:T(8,128)(2,1)S(1)}, u32[]{:S(2)}, u32[]{:S(2)}) async-start(bf16[16,19,8,128]{3,2,1,0:T(8,128)(2,1)} %get-tuple-element.29), calls=%async_computation.4 | async-start | bytes 1245184 | tf_op jit(solution)/shard_map/all_to_all | solution.py:465
  166.1 0.8 copy-start.3

commit v3 on v2

v3 whole, which is shorter than its diff:
```python
import functools

import jax
import jax.numpy as jnp
from jax import lax
from jax.experimental import pallas as pl
from jax.experimental.pallas import tpu as pltpu
from jax.sharding import Mesh, PartitionSpec as P

EPSILON = 1e-06
NORM_FLOOR = 0.25
LOG2_E = 1.4426950408889634

GROUPS = 16
REQUESTS = 8
CHUNKS = 2
PER = REQUESTS // CHUNKS
TURN = 128
INNER = 1024
RANK = 512
STATE = 16
WIDE = RANK + 2 * STATE
SLOTS = 32
KEPT = 3
DEPTH = 8
CORES = 2
SHARE = PER * TURN // DEPTH
HEAD = 16
FETCHED = CHUNKS * (STATE + KEPT)
RETURNED = STATE + CHUNKS * KEPT
LANES = 128
TILES = INNER // LANES
UNROLL = 4

F32 = jnp.float32
BF16 = jnp.bfloat16
SWAP = [(0, 1), (1, 0)]


def params():
    return pltpu.CompilerParams(vmem_limit_bytes=56 * 2**20)


def cost(us, bytes_accessed):
    return pl.CostEstimate(
        flops=int(us * 1.0e9), bytes_accessed=bytes_accessed, transcendentals=0
    )


def rows_to_tiles(tiles, first, rows):
    for tile in range(TILES):
        tiles[pl.ds(first + tile, rows.shape[0], stride=TILES), :] = rows[
            :, tile * LANES : (tile + 1) * LANES
        ]


def block_of(part, tile):
    return slice(part * 8, (part + 1) * 8), slice(tile * LANES, (tile + 1) * LANES)


def pack_kernel(slots, ssm, conv, out, states, inputs, sems):
    def copy(e):
        return pltpu.make_async_copy(ssm.at[slots[e]], states.at[e], sems.at[e])

    def begin(e, carry):
        copy(e).start()
        return carry

    def finish(e, carry):
        g, c = e // CHUNKS, e % CHUNKS
        for k in range(KEPT):
            row = pl.multiple_of((k * SLOTS + slots[e]) * TILES, TILES)
            out[g, CHUNKS * STATE + c * KEPT + k] = inputs[pl.ds(row, TILES), :].astype(BF16)
        copy(e).wait()
        for part in range(STATE // 8):
            for tile in range(TILES):
                rows, cols = block_of(part, tile)
                out[g, c * STATE + part * TILES + tile] = states[e, rows, cols].astype(BF16)
        return carry

    lax.fori_loop(0, GROUPS * CHUNKS, begin, 0)
    for k in range(KEPT):
        rows_to_tiles(inputs, k * SLOTS * TILES, conv[k])
    lax.fori_loop(0, GROUPS * CHUNKS, finish, 0)


def pack(slots, ssm, conv):
    return pl.pallas_call(
        pack_kernel,
        grid_spec=pltpu.PrefetchScalarGridSpec(
            num_scalar_prefetch=1,
            grid=(1,),
            in_specs=[
                pl.BlockSpec(memory_space=pl.ANY),
                pl.BlockSpec((KEPT, SLOTS, INNER), lambda i, s: (0, 0, 0)),
            ],
            out_specs=pl.BlockSpec((GROUPS, FETCHED, TILES, LANES), lambda i, s: (0, 0, 0, 0)),
            scratch_shapes=[
                pltpu.VMEM((GROUPS * CHUNKS, STATE, INNER), F32),
                pltpu.VMEM((KEPT * SLOTS * TILES, LANES), F32),
                pltpu.SemaphoreType.DMA((GROUPS * CHUNKS,)),
            ],
        ),
        out_shape=jax.ShapeDtypeStruct((GROUPS, FETCHED, TILES, LANES), BF16),
        compiler_params=params(),
        cost_estimate=cost(3, 4 * 2**20),
        name="pack",
    )(slots, ssm, conv)


def silu(v):
    return v / (1.0 + jnp.exp(-v))


def conv_kernel(order_ref, hidden, weight, bias, x_weight, conv_out, sent, kept, rows):
    step = pl.program_id(0)
    rows[:8, :] = jnp.zeros((8, INNER), F32)
    for tile in range(TILES):
        cols = slice(tile * LANES, (tile + 1) * LANES)
        rows[8:, cols] = hidden[0, :, cols].astype(F32)
        total = jnp.zeros((TURN, LANES), F32) + bias[:, cols]
        for tap in range(KEPT + 1):
            first = 8 - KEPT + tap
            total = total + rows[first : first + TURN, cols] * weight[tap : tap + 1, cols]
        conv_out[0, :, cols] = silu(total).astype(BF16)
    part = jnp.dot(conv_out[0], x_weight[...], preferred_element_type=F32)

    @pl.when(step < PER)
    def _():
        sent[0] = part.astype(BF16)

    @pl.when(step >= PER)
    def _():
        kept[0] = part


def convolve(order, hidden, weight, bias, x_weight):
    return pl.pallas_call(
        conv_kernel,
        grid_spec=pltpu.PrefetchScalarGridSpec(
            num_scalar_prefetch=1,
            grid=(REQUESTS,),
            in_specs=[
                pl.BlockSpec((1, TURN, INNER), lambda i, o: (o[i], 0, 0)),
                pl.BlockSpec((KEPT + 1, INNER), lambda i, o: (0, 0)),
                pl.BlockSpec((1, INNER), lambda i, o: (0, 0)),
                pl.BlockSpec((INNER, WIDE), lambda i, o: (0, 0)),
            ],
            out_specs=[
                pl.BlockSpec((1, TURN, INNER), lambda i, o: (i, 0, 0)),
                pl.BlockSpec((1, TURN, WIDE), lambda i, o: (jnp.minimum(i, PER - 1), 0, 0)),
                pl.BlockSpec((1, TURN, WIDE), lambda i, o: (jnp.maximum(i - PER, 0), 0, 0)),
            ],
            scratch_shapes=[pltpu.VMEM((8 + TURN, INNER), F32)],
        ),
        out_shape=[
            jax.ShapeDtypeStruct((REQUESTS, TURN, INNER), BF16),
            jax.ShapeDtypeStruct((PER, TURN, WIDE), BF16),
            jax.ShapeDtypeStruct((PER, TURN, WIDE), F32),
        ],
        compiler_params=params(),
        cost_estimate=cost(8, 8 * 2**20),
        name="convolve",
    )(order, hidden, weight, bias, x_weight)


def head_kernel(
    order, holder, sides, hidden, fetched, weight, bias, x_weight, conv_in, sent_in, kept_in,
    conv_out, sent, kept, starts, rows, tiles, head, head_sent, head_kept, sems, start_sems,
):
    arriving = []
    for i in range(REQUESTS):
        first = CHUNKS * STATE + sides[i // PER] * KEPT
        arriving.append(
            pltpu.make_async_copy(
                fetched.at[holder[i], pl.ds(first, KEPT)], starts.at[i], start_sems.at[i]
            )
        )
        arriving[i].start()
    for i in range(REQUESTS):
        arriving[i].wait()
        for k in range(KEPT):
            tiles[k * TILES : (k + 1) * TILES, :] = starts[i, k].astype(F32)
        for tile in range(TILES):
            rows[8 - KEPT : 8, tile * LANES : (tile + 1) * LANES] = tiles[
                pl.ds(tile, KEPT, stride=TILES), :
            ]
        rows[8:, :] = hidden[order[i]].astype(F32)
        total = jnp.zeros((HEAD, INNER), F32) + bias[...]
        for tap in range(KEPT + 1):
            first = 8 - KEPT + tap
            total = total + rows[first : first + HEAD, :] * weight[tap : tap + 1, :]
        head[i] = silu(total).astype(BF16)
    part = jnp.dot(
        head[...].reshape(REQUESTS * HEAD, INNER), x_weight[...], preferred_element_type=F32
    ).reshape(REQUESTS, HEAD, WIDE)
    head_sent[...] = part[:PER].astype(BF16)
    head_kept[...] = part[PER:]
    copies = []
    for i in range(REQUESTS):
        copies.append((head.at[i], conv_out.at[i, :HEAD]))
        if i < PER:
            copies.append((head_sent.at[i], sent.at[i, :HEAD]))
        else:
            copies.append((head_kept.at[i - PER], kept.at[i - PER, :HEAD]))
    copies = [
        pltpu.make_async_copy(source, target, sems.at[k])
        for k, (source, target) in enumerate(copies)
    ]
    for one in copies:
        one.start()
    for one in copies:
        one.wait()


def put_heads(order, holder, sides, hidden, fetched, weight, bias, x_weight, conv_out, sent, kept):
    anywhere = pl.BlockSpec(memory_space=pl.ANY)
    return pl.pallas_call(
        head_kernel,
        grid_spec=pltpu.PrefetchScalarGridSpec(
            num_scalar_prefetch=3,
            grid=(1,),
            in_specs=[
                pl.BlockSpec((REQUESTS, HEAD, INNER), lambda i, o, h, s: (0, 0, 0)),
                anywhere,
                pl.BlockSpec((KEPT + 1, INNER), lambda i, o, h, s: (0, 0)),
                pl.BlockSpec((1, INNER), lambda i, o, h, s: (0, 0)),
                pl.BlockSpec((INNER, WIDE), lambda i, o, h, s: (0, 0)),
                anywhere,
                anywhere,
                anywhere,
            ],
            out_specs=[anywhere, anywhere, anywhere],
            scratch_shapes=[
                pltpu.VMEM((REQUESTS, KEPT, TILES, LANES), BF16),
                pltpu.VMEM((8 + HEAD, INNER), F32),
                pltpu.VMEM((KEPT * TILES, LANES), F32),
                pltpu.VMEM((REQUESTS, HEAD, INNER), BF16),
                pltpu.VMEM((PER, HEAD, WIDE), BF16),
                pltpu.VMEM((PER, HEAD, WIDE), F32),
                pltpu.SemaphoreType.DMA((2 * REQUESTS,)),
                pltpu.SemaphoreType.DMA((REQUESTS,)),
            ],
        ),
        out_shape=[
            jax.ShapeDtypeStruct(conv_out.shape, conv_out.dtype),
            jax.ShapeDtypeStruct(sent.shape, sent.dtype),
            jax.ShapeDtypeStruct(kept.shape, kept.dtype),
        ],
        input_output_aliases={8: 0, 9: 1, 10: 2},
        compiler_params=params(),
        cost_estimate=cost(3, 4 * 2**20),
        name="put_heads",
    )(order, holder, sides, hidden, fetched, weight, bias, x_weight, conv_out, sent, kept)


def norm_kernel(parts, out):
    total = parts[0].astype(F32)
    for k in range(1, DEPTH):
        total = total + parts[k].astype(F32)
    rank = total[:, :RANK]
    inject = total[:, RANK : RANK + STATE]
    readout = total[:, RANK + STATE :]
    rank = rank * lax.rsqrt(jnp.mean(rank * rank, axis=1, keepdims=True) + EPSILON)
    inject = inject * lax.rsqrt(
        jnp.maximum(jnp.mean(inject * inject, axis=1, keepdims=True), NORM_FLOOR)
    )
    readout = readout * lax.rsqrt(
        jnp.maximum(jnp.mean(readout * readout, axis=1, keepdims=True), NORM_FLOOR)
    )
    joined = jnp.concatenate([rank, inject, readout], axis=1).astype(BF16)
    for k in range(DEPTH):
        out[k] = joined


def normalize(parts):
    return pl.pallas_call(
        norm_kernel,
        out_shape=jax.ShapeDtypeStruct((DEPTH, SHARE, WIDE), BF16),
        compiler_params=params(),
        cost_estimate=cost(1.5, 2**20),
        name="normalize",
    )(parts)


def scan_kernel(
    own, order_ref, holder, sides, normed_ref, dt_weight, dt_bias, a_log, skip, conv, gate, start,
    last, other_last, base, gated, final, dts, us, spread, rates, states,
):
    step = pl.program_id(0)
    to = holder[PER + step] if own else holder[step]

    @pl.when(step == 0)
    def _():
        rows_to_tiles(rates, 0, -LOG2_E * jnp.exp(a_log[...]))

    columns = normed_ref[0, :, RANK:].astype(F32).T
    for t in range(TURN):
        spread[t * 2 * STATE : (t + 1) * 2 * STATE, :] = jnp.broadcast_to(
            columns[:, t : t + 1], (2 * STATE, LANES)
        )
    if own:
        for which, (rows, at) in enumerate(((last, to), (other_last, holder[step]))):
            rows_to_tiles(states, 0, rows[0].astype(F32)[HEAD - KEPT :, :])
            for k in range(KEPT):
                final[at, STATE + which * KEPT + k] = states[
                    k * TILES : (k + 1) * TILES, :
                ].astype(BF16)
    for part in range(STATE // 8):
        for tile in range(TILES):
            states[pl.ds(part * 8 * TILES + tile, 8, stride=TILES), :] = start[
                0, part * TILES + tile
            ].astype(F32)
    rank = normed_ref[0, :, :RANK]
    pair = 2 * LANES
    for block in range(INNER // pair):
        cols = slice(block * pair, (block + 1) * pair)
        raw = jnp.dot(rank, dt_weight[:, cols], preferred_element_type=F32) + dt_bias[:, cols]
        dt = jnp.maximum(raw, 0.0) + jnp.log1p(jnp.exp(-jnp.abs(raw)))
        for k in range(2):
            tile = 2 * block + k
            dts[pl.ds(tile, TURN, stride=TILES), :] = dt[:, k * LANES : (k + 1) * LANES]
            us[pl.ds(tile, TURN, stride=TILES), :] = conv[
                0, :, tile * LANES : (tile + 1) * LANES
            ].astype(F32)
    decay = [rates[n * TILES : (n + 1) * TILES, :] for n in range(STATE)]

    def steps(i, carried):
        carried = list(carried)
        for k in range(UNROLL):
            t = i * UNROLL + k
            at = pl.multiple_of(t * TILES, TILES)
            row = pl.multiple_of(t * 2 * STATE, 2 * STATE)
            dt = dts[pl.ds(at, TILES), :]
            drive = dt * us[pl.ds(at, TILES), :]
            sums = [None] * 4
            for n in range(STATE):
                carried[n] = (
                    jnp.exp2(dt * decay[n]) * carried[n] + drive * spread[pl.ds(row + n, 1), :]
                )
                term = carried[n] * spread[pl.ds(row + STATE + n, 1), :]
                sums[n % 4] = term if sums[n % 4] is None else sums[n % 4] + term
            dts[pl.ds(at, TILES), :] = (sums[0] + sums[1]) + (sums[2] + sums[3])
        return tuple(carried)

    carried = tuple(states[n * TILES : (n + 1) * TILES, :] for n in range(STATE))
    carried = lax.fori_loop(0, TURN // UNROLL, steps, carried)
    for n in range(STATE):
        states[n * TILES : (n + 1) * TILES, :] = carried[n]
    for part in range(STATE // 8):
        for tile in range(TILES):
            final[to, part * TILES + tile] = states[
                pl.ds(part * 8 * TILES + tile, 8, stride=TILES), :
            ].astype(BF16)
    for tile in range(TILES):
        cols = slice(tile * LANES, (tile + 1) * LANES)
        z = gate[0, :, cols].astype(F32)
        y = dts[pl.ds(tile, TURN, stride=TILES), :] + skip[:, cols] * conv[0, :, cols].astype(F32)
        gated[0, :, cols] = (y * silu(z)).astype(BF16)


def scan(order, holder, sides, normed, dt_weight, dt_bias, a_log, skip, conv, gate, fetched, hidden, base):
    own = base is None
    first = PER if own else 0
    blocks = RETURNED if own else STATE
    whole = lambda shape: pl.BlockSpec(shape, lambda i, o, h, s: (0,) * len(shape))
    ends = lambda at: pl.BlockSpec(
        (1, HEAD, INNER), lambda i, o, h, s: (o[at + i], TURN // HEAD - 1, 0)
    )
    return pl.pallas_call(
        functools.partial(scan_kernel, own),
        grid_spec=pltpu.PrefetchScalarGridSpec(
            num_scalar_prefetch=3,
            grid=(PER,),
            in_specs=[
                pl.BlockSpec((1, TURN, WIDE), lambda i, o, h, s: (i, 0, 0)),
                whole((RANK, INNER)),
                whole((1, INNER)),
                whole((STATE, INNER)),
                whole((1, INNER)),
                pl.BlockSpec((1, TURN, INNER), lambda i, o, h, s: (first + i, 0, 0)),
                pl.BlockSpec((1, TURN, INNER), lambda i, o, h, s: (o[first + i], 0, 0)),
                pl.BlockSpec(
                    (1, STATE, TILES, LANES),
                    lambda i, o, h, s: (h[first + i], s[1 if own else 0], 0, 0),
                ),
                ends(PER),
                ends(0),
                pl.BlockSpec(memory_space=pl.ANY),
            ],
            out_specs=[
                pl.BlockSpec((1, TURN, INNER), lambda i, o, h, s: (o[first + i], 0, 0)),
                whole((GROUPS, blocks, TILES, LANES)),
            ],
            scratch_shapes=[
                pltpu.VMEM((TURN * TILES, LANES), F32),
                pltpu.VMEM((TURN * TILES, LANES), F32),
                pltpu.VMEM((TURN * 2 * STATE, LANES), F32),
                pltpu.VMEM((STATE * TILES, LANES), F32),
                pltpu.VMEM((STATE * TILES, LANES), F32),
            ],
        ),
        out_shape=[
            jax.ShapeDtypeStruct((REQUESTS, TURN, INNER), BF16),
            jax.ShapeDtypeStruct((GROUPS, blocks, TILES, LANES), BF16),
        ],
        input_output_aliases={} if own else {13: 0},
        compiler_params=params(),
        cost_estimate=cost(15, 4 * 2**20),
        name="scan",
    )(order, holder, sides, normed, dt_weight, dt_bias, a_log, skip, conv, gate, fetched, hidden,
      hidden, skip if own else base)


def widen(came, wide, g):
    for part in range(STATE // 8):
        for tile in range(TILES):
            rows, cols = block_of(part, tile)
            wide[g, rows, cols] = came[g, part * TILES + tile].astype(F32)


def place_kernel(
    slots, other_slots, taken, came, ssm, conv, new_ssm, new_conv, wide, inputs, sems, base_sems
):
    def base(s):
        return pltpu.make_async_copy(ssm.at[s], new_ssm.at[s], base_sems.at[s])

    def copy(g):
        return pltpu.make_async_copy(wide.at[g], new_ssm.at[slots[g]], sems.at[g])

    def begin_base(s, carry):
        @pl.when(taken[s] == 0)
        def _():
            base(s).start()

        return carry

    def finish_base(s, carry):
        @pl.when(taken[s] == 0)
        def _():
            base(s).wait()

        return carry

    def put(slot, g, first):
        for k in range(KEPT):
            row = pl.multiple_of((k * SLOTS + slot) * TILES, TILES)
            inputs[pl.ds(row, TILES), :] = came[g, first + k].astype(F32)

    def begin(g, carry):
        @pl.when(slots[g] < SLOTS)
        def _():
            widen(came, wide, g)
            copy(g).start()
            put(slots[g], g, STATE)

        @pl.when(other_slots[g] < SLOTS)
        def _():
            put(other_slots[g], g, STATE + KEPT)

        return carry

    def finish(g, carry):
        @pl.when(slots[g] < SLOTS)
        def _():
            copy(g).wait()

        return carry

    lax.fori_loop(0, SLOTS, begin_base, 0)
    for k in range(KEPT):
        rows_to_tiles(inputs, k * SLOTS * TILES, conv[k])
    lax.fori_loop(0, GROUPS, begin, 0)
    for k in range(KEPT):
        for tile in range(TILES):
            new_conv[k, :, tile * LANES : (tile + 1) * LANES] = inputs[
                pl.ds(k * SLOTS * TILES + tile, SLOTS, stride=TILES), :
            ]
    lax.fori_loop(0, GROUPS, finish, 0)
    lax.fori_loop(0, SLOTS, finish_base, 0)


def place(slots, other_slots, taken, came, ssm, conv):
    anywhere = pl.BlockSpec(memory_space=pl.ANY)
    rows = pl.BlockSpec((KEPT, SLOTS, INNER), lambda i, s, o, t: (0, 0, 0))
    return pl.pallas_call(
        place_kernel,
        grid_spec=pltpu.PrefetchScalarGridSpec(
            num_scalar_prefetch=3,
            grid=(1,),
            in_specs=[
                pl.BlockSpec((GROUPS, RETURNED, TILES, LANES), lambda i, s, o, t: (0, 0, 0, 0)),
                anywhere,
                rows,
            ],
            out_specs=[anywhere, rows],
            scratch_shapes=[
                pltpu.VMEM((GROUPS, STATE, INNER), F32),
                pltpu.VMEM((KEPT * SLOTS * TILES, LANES), F32),
                pltpu.SemaphoreType.DMA((GROUPS,)),
                pltpu.SemaphoreType.DMA((SLOTS,)),
            ],
        ),
        out_shape=[
            jax.ShapeDtypeStruct((SLOTS, STATE, INNER), F32),
            jax.ShapeDtypeStruct((KEPT, SLOTS, INNER), F32),
        ],
        compiler_params=params(),
        cost_estimate=cost(4, 6 * 2**20),
        name="place",
    )(slots, other_slots, taken, came, ssm, conv)


def store_kernel(slots, came, ssm_in, new_ssm, wide, sems):
    def copy(g):
        return pltpu.make_async_copy(wide.at[g], new_ssm.at[slots[g]], sems.at[g])

    def begin(g, carry):
        @pl.when(slots[g] < SLOTS)
        def _():
            widen(came, wide, g)
            copy(g).start()

        return carry

    def finish(g, carry):
        @pl.when(slots[g] < SLOTS)
        def _():
            copy(g).wait()

        return carry

    lax.fori_loop(0, GROUPS, begin, 0)
    lax.fori_loop(0, GROUPS, finish, 0)


def store(slots, came, ssm):
    anywhere = pl.BlockSpec(memory_space=pl.ANY)
    return pl.pallas_call(
        store_kernel,
        grid_spec=pltpu.PrefetchScalarGridSpec(
            num_scalar_prefetch=1,
            grid=(1,),
            in_specs=[
                pl.BlockSpec((GROUPS, STATE, TILES, LANES), lambda i, s: (0, 0, 0, 0)),
                anywhere,
            ],
            out_specs=anywhere,
            scratch_shapes=[
                pltpu.VMEM((GROUPS, STATE, INNER), F32),
                pltpu.SemaphoreType.DMA((GROUPS,)),
            ],
        ),
        out_shape=jax.ShapeDtypeStruct((SLOTS, STATE, INNER), F32),
        input_output_aliases={2: 0},
        compiler_params=params(),
        cost_estimate=cost(2, 2 * 2**20),
        name="store",
    )(slots, came, ssm)


def exchange(values, axis):
    return lax.all_to_all(values, axis, split_axis=0, concat_axis=0, tiled=True)


def body(
    hidden_x,
    gate_z,
    conv_weight,
    conv_bias,
    x_weight,
    dt_weight,
    dt_bias,
    a_log,
    skip_gain,
    ssm_cache,
    conv_cache,
    holder_of,
    slot_of,
):
    me = lax.axis_index("dp")
    core = lax.axis_index("core")
    holders = holder_of.reshape(GROUPS, REQUESTS)
    places = slot_of.reshape(GROUPS, REQUESTS)

    keys = holders * REQUESTS + jnp.arange(REQUESTS, dtype=jnp.int32)
    rank = jnp.sum((keys[:, None, :] < keys[:, :, None]).astype(jnp.int32), axis=2)
    served = (holders == me)[:, None, :] & (
        rank[:, None, :] % CHUNKS == jnp.arange(CHUNKS, dtype=jnp.int32)[None, :, None]
    )
    slots = jnp.sum(jnp.where(served, places[:, None, :], 0), axis=2)
    targets = jnp.where(jnp.any(served, axis=2), slots, SLOTS)
    own_slots = jnp.where(core == 0, targets[:, 0], targets[:, 1])
    other_slots = jnp.where(core == 0, targets[:, 1], targets[:, 0])
    taken = jnp.sum(
        (own_slots[None, :] == jnp.arange(SLOTS, dtype=jnp.int32)[:, None]).astype(jnp.int32),
        axis=1,
    )

    at = jnp.arange(REQUESTS, dtype=jnp.int32)
    sides = jnp.stack([1 - core, core]).astype(jnp.int32)
    number = at % PER * CHUNKS + jnp.where(at < PER, 1 - core, core)
    chosen = rank[me][None, :] == number[:, None]
    order = jnp.sum(jnp.where(chosen, at[None, :], 0), axis=1)
    holder = jnp.sum(jnp.where(chosen, holders[me][None, :], 0), axis=1)

    conv_rows = jnp.swapaxes(conv_cache, 0, 1)
    bias = conv_bias.reshape(1, INNER)
    fetched = exchange(pack(slots.reshape(-1), ssm_cache, conv_rows), "dp")
    conv, sent, kept = convolve(order, hidden_x, conv_weight, bias, x_weight)
    conv, sent, kept = put_heads(
        order, holder, sides, hidden_x, fetched, conv_weight, bias, x_weight, conv, sent, kept
    )
    parts = (kept + lax.ppermute(sent, "core", SWAP).astype(F32)).astype(BF16)
    share = normalize(exchange(parts.reshape(DEPTH, SHARE, WIDE), "z"))

    normed = exchange(share, "z").reshape(PER, TURN, WIDE)
    gated, came = None, []
    for values in (normed, lax.ppermute(normed, "core", SWAP)):
        gated, final = scan(
            order,
            holder,
            sides,
            values,
            dt_weight,
            dt_bias.reshape(1, INNER),
            a_log,
            skip_gain.reshape(1, INNER),
            conv,
            gate_z,
            fetched,
            hidden_x,
            gated,
        )
        came.append(exchange(final, "dp"))
    new_ssm, new_conv = place(own_slots, other_slots, taken, came[0], ssm_cache, conv_rows)
    new_ssm = store(other_slots, came[1], new_ssm)
    return (gated, new_ssm, jnp.swapaxes(new_conv, 0, 1))


def solution(mesh):
    fine = Mesh(mesh.devices.reshape(GROUPS, DEPTH, CORES), ("dp", "z", "core"))
    tensor = ("z", "core")
    placed = (
        P("dp", None, tensor),
        P("dp", None, tensor),
        P(None, tensor),
        P(tensor),
        P(tensor, None),
        P(None, tensor),
        P(tensor),
        P(None, tensor),
        P(tensor),
        P("dp", None, tensor),
        P("dp", None, tensor),
        P(),
        P(),
    )
    return jax.shard_map(
        body,
        mesh=fine,
        in_specs=placed,
        out_specs=(P("dp", None, tensor),) * 3,
        check_vma=False,
    )
```

time: 172 us -> 218 us (1.27)
  the two profiles are of different devices: /device:TPU:8 before, /device:TPU:19 now
where the time goes in v3:
time: 218 us; the launch traced here: 216 us
  Pallas kernels  126 us (58%)
  blocking collectives  27.6 us (13%)
  starting transfers between devices  27.4 us (13%)
  waiting for transfers between devices  22.8 us (10%)
  local copies, waits for them, and re-layouts  9.08 us (4%)
  other arithmetic  2.79 us (1%)
    pallas_call x1, Pallas kernels, place(): pl.pallas_call(place_kernel, grid_spec=pltpu.PrefetchScalarGridSpec(num_s...  65.7 us
    pallas_call x2, Pallas kernels, scan(): pl.pallas_call(functools.partial(scan_kernel, own), grid_spec=pltpu.Prefe...  33.8 us
    all_to_all x1, blocking collectives, exchange(): return lax.all_to_all(values, axis, split_axis=0, concat_axis=0, tiled=True)  27.6 us
    all_to_all x4, starting transfers between devices, exchange(): return lax.all_to_all(values, axis, split_axis=0, concat_axis=0, tiled=True)  23.7 us
    all_to_all x4, waiting for transfers between devices, exchange(): return lax.all_to_all(values, axis, split_axis=0, concat_axis=0, tiled=True)  21.3 us
    pallas_call x1, Pallas kernels, convolve(): pl.pallas_call(conv_kernel, grid_spec=pltpu.PrefetchScalarGridSpec(num_sc...  10.9 us
    pallas_call x1, Pallas kernels, pack(): pl.pallas_call(pack_kernel, grid_spec=pltpu.PrefetchScalarGridSpec(num_sc...  5.78 us
    pallas_call x1, Pallas kernels, put_heads(): pl.pallas_call(head_kernel, grid_spec=pltpu.PrefetchScalarGridSpec(num_sc...  4.87 us
  transfers between devices with their start and end apart: 6, of which 3 were waited for; matrix products, arithmetic and copies ran while one was open for 2% of the time, Pallas kernels for 51%

profile of v3, /device:TPU:19, one launch (start us, length us, event | category | flops | bytes accessed | tf_op | source)
XLA Modules:
  0.0 216.2 jit_solution(996638723540473804)
XLA Ops:
  0.6 0.7 reshape.103
  1.4 0.1 copy.47
  1.5 0.1 copy.45
  1.6 0.7 broadcast_in_dim.62
  2.3 0.1 copy.48
  2.4 0.1 copy.49
  2.5 0.6 reshape.104.slots
  3.1 5.8 %pack.1 = bf16[16,38,8,128]{3,2,1,0:T(8,128)(2,1)} custom-call(s32[32]{0:T(128)} %reshape.104.slots, f32[32,16,1024]{2,1,0:T(8,128)} %ssm.3, f32[3,32,1024]{2,1,0:T(8,128)} %bitcast.18), custom_call_target="tpu_custom_call" | custom-call | flops 3000000000 | bytes 4194304 | tf_op jit(solution)/shard_map/pack/pallas_call | solution.py:88
  8.9 0.0 copy-start.3
  8.9 6.5 %all-to-all-start = ((bf16[16,38,8,128]{3,2,1,0:T(8,128)(2,1)}), bf16[16,38,8,128]{3,2,1,0:T(8,128)(2,1)S(1)}, u32[]{:S(2)}, u32[]{:S(2)}) async-start(bf16[16,38,8,128]{3,2,1,0:T(8,128)(2,1)} %pack.1), calls=%async_computation | async-start | bytes 2490368 | tf_op jit(solution)/shard_map/all_to_all | solution.py:563
  15.4 0.2 dynamic-slice_reduce_fusion
  15.6 0.0 copy-done.3
  15.6 1.4 copy.51.x_weight
  17.0 0.6 pad_add_fusion.sides
  17.7 0.7 fusion.3
  18.4 10.9 %convolve.1 = (bf16[8,128,1024]{2,1,0:T(8,128)(2,1)}, bf16[4,128,544]{2,1,0:T(8,128)(2,1)}, f32[4,128,544]{2,1,0:T(8,128)}) custom-call(s32[8]{0:T(128)} %get-tuple-element.28.order_ref.order, bf16[8,128,1024]{2,1,0:T(8,128)(2,1)} %other_last.3, f32[4,1024]{1,0:T(4,128)} %weight.3, f32[1,1024]{1,0:T(1,128)} %bitcast.20, bf16[1024,544]{1,0:T(8,128)(2,1)} %copy.51.x_weight), custom_call_target="tpu_custom_call" | custom-call | flops 8000000000 | bytes 8388608 | tf_op jit(solution)/shard_map/convolve/pallas_call | solution.py:138
  29.3 2.2 all-to-all-done.fetched.start
  31.5 0.0 copy-start.2
  31.5 1.1 copy-done.2
  32.5 4.9 %put_heads.1 = (bf16[8,128,1024]{2,1,0:T(8,128)(2,1)}, bf16[4,128,544]{2,1,0:T(8,128)(2,1)}, f32[4,128,544]{2,1,0:T(8,128)}) custom-call(s32[8]{0:T(128)} %get-tuple-element.28.order_ref.order, s32[8]{0:T(128)} %get-tuple-element.27.holder, s32[2]{0:T(128)} %pad_add_fusion.sides, ...), custom_call_target="tpu_custom_call", output_to_operand_aliasing={{0}: (8, {}), {1}: (9, {}), {2}: (10, {})} | custom-call | flops 3000000000 | bytes 4194304 | tf_op jit(solution)/shard_map/put_heads/pallas_call | solution.py:218
  37.4 0.0 copy-start.1
  37.4 1.5 copy.52
  38.9 1.5 collective-permute-start
  40.4 1.6 collective-permute-done
  42.0 0.3 copy.53
  42.3 0.0 copy-done.1
  42.3 0.1 add_convert_fusion
  42.5 27.6 %all_to_all.25.parts = bf16[8,64,544]{2,1,0:T(8,128)(2,1)} all-to-all(bf16[8,64,544]{2,1,0:T(8,128)(2,1)S(1)} %bitcast.15), channel_id=1, replica_groups=mesh['dp'=16,'z'=8,'core'=2] {'z'}, dimensions={0} | all-to-all | bytes 1114112 | tf_op jit(solution)/shard_map/all_to_all | solution.py:563
  70.1 2.1 normalize.1
  72.2 3.5 %all-to-all-start.2 = ((bf16[8,64,544]{2,1,0:T(8,128)(2,1)}), bf16[8,64,544]{2,1,0:T(8,128)(2,1)S(1)}, u32[]{:S(2)}, u32[]{:S(2)}) async-start(bf16[8,64,544]{2,1,0:T(8,128)(2,1)} %normalize.1), calls=%async_computation.2 | async-start | bytes 1310720 | tf_op jit(solution)/shard_map/all_to_all | solution.py:563
  75.8 19.1 %all-to-all-done.2 = bf16[8,64,544]{2,1,0:T(8,128)(2,1)S(1)} async-done(((bf16[8,64,544]{2,1,0:T(8,128)(2,1)}), bf16[8,64,544]{2,1,0:T(8,128)(2,1)S(1)}, u32[]{:S(2)}, u32[]{:S(2)}) %all-to-all-start.2) | async-done | bytes 557088 | tf_op jit(solution)/shard_map/all_to_all | solution.py:563
  94.8 0.0 copy-start
  94.9 0.3 copy.54
  95.2 2.1 collective-permute-start.1
  97.3 0.0 copy-done
  97.3 16.9 %scan.2 = (bf16[8,128,1024]{2,1,0:T(8,128)(2,1)}, bf16[16,22,8,128]{3,2,1,0:T(8,128)(2,1)}) custom-call(s32[8]{0:T(128)} %get-tuple-element.28.order_ref.order, s32[8]{0:T(128)} %get-tuple-element.27.holder, s32[2]{0:T(128)} %pad_add_fusion.sides, bf16[4,128,544]{2,1,0:T(8,128)(2,1)} %bitcast.17, bf16[512,1024]{1,0:T(8,128)(2,1)} %dt_weight.3, ...), custom_call_target="tpu_custom_call" | custom-call | flops 15000000512 | bytes 4194304 | tf_op jit(solution)/shard_map/scan/pallas_call | solution.py:370
  114.2 7.0 %all-to-all-start.4 = ((bf16[16,22,8,128]{3,2,1,0:T(8,128)(2,1)}), bf16[16,22,8,128]{3,2,1,0:T(8,128)(2,1)S(1)}, u32[]{:S(2)}, u32[]{:S(2)}) async-start(bf16[16,22,8,128]{3,2,1,0:T(8,128)(2,1)} %get-tuple-element.24), calls=%async_computation.4 | async-start | bytes 1441792 | tf_op jit(solution)/shard_map/all_to_all | solution.py:563
  121.2 0.0 collective-permute-done.1
  121.2 1.1 copy.55.normed_ref
  122.3 16.9 %scan.3 = (bf16[8,128,1024]{2,1,0:T(8,128)(2,1)}, bf16[16,16,8,128]{3,2,1,0:T(8,128)(2,1)}) custom-call(s32[8]{0:T(128)} %get-tuple-element.28.order_ref.order, s32[8]{0:T(128)} %get-tuple-element.27.holder, s32[2]{0:T(128)} %pad_add_fusion.sides, bf16[4,128,544]{2,1,0:T(8,128)(2,1)} %copy.55.normed_ref, ...), custom_call_target="tpu_custom_call", output_to_operand_aliasing={{0}: (13, {})} | custom-call | flops 15000000512 | bytes 4194304 | tf_op jit(solution)/shard_map/scan/pallas_call | solution.py:370
  139.2 0.0 all-to-all-done.4.came
  139.2 0.0 copy-start.4
  139.2 6.7 %all-to-all-start.3 = ((bf16[16,16,8,128]{3,2,1,0:T(8,128)(2,1)}), bf16[16,16,8,128]{3,2,1,0:T(8,128)(2,1)S(1)}, u32[]{:S(2)}, u32[]{:S(2)}) async-start(bf16[16,16,8,128]{3,2,1,0:T(8,128)(2,1)} %get-tuple-element.23), calls=%async_computation.3 | async-start | bytes 1048576 | tf_op jit(solution)/shard_map/all_to_all | solution.py:563
  145.9 0.5 fusion.6
  146.4 0.0 copy-start.6
  146.4 0.7 convert_reduce_fusion.1.taken
  147.1 0.0 copy-done.4
  147.1 0.0 copy-done.6
  147.1 65.7 %place.1 = (f32[32,16,1024]{2,1,0:T(8,128)}, f32[3,32,1024]{2,1,0:T(8,128)}) custom-call(s32[16]{0:T(128)} %copy-done.6, s32[16]{0:T(128)} %get-tuple-element.30.other_slots.slots, s32[32]{0:T(128)} %convert_reduce_fusion.1.taken, bf16[16,22,8,128]{3,2,1,0:T(8,128)(2,1)} %copy-done.4, f32[32,16,1024]{2,1,0:T(8,128)} %ssm.3, f32[3,32,1024]{2,1,0:T(8,128)} %bitcast.19), custom_call_target="tpu_custom_call" | custom-call | flops 4000000000 | bytes 6291456 | tf_op jit(solution)/shard_map/place/pallas_call | solution.py:486
  212.8 0.0 all-to-all-done.3.came
  212.8 0.0 copy-start.5
  212.8 0.8 copy-done.5
  213.6 2.6 %store.1 = f32[32,16,1024]{2,1,0:T(8,128)} custom-call(s32[16]{0:T(128)} %get-tuple-element.30.other_slots.slots, bf16[16,16,8,128]{3,2,1,0:T(8,128)(2,1)} %copy-done.5, f32[32,16,1024]{2,1,0:T(8,128)} %get-tuple-element.25.ssm_in), custom_call_target="tpu_custom_call", output_to_operand_aliasing={{}: (2, {})} | custom-call | flops 2000000000 | bytes 2097152 | tf_op jit(solution)/shard_map/store/pallas_call | solution.py:539
  (9 shorter events, 0.1 us)
Async XLA Ops:
  8.9 6.7 %copy-start.3 = (bf16[1024,544]{0,1:T(8,128)(2,1)S(1)}, bf16[1024,544]{0,1:T(8,128)(2,1)}, u32[]{:S(2)}) copy-start(bf16[1024,544]{0,1:T(8,128)(2,1)} %param.17) | copy-start | bytes 3342340
  8.9 22.5 %all-to-all-start = ((bf16[16,38,8,128]{3,2,1,0:T(8,128)(2,1)}), bf16[16,38,8,128]{3,2,1,0:T(8,128)(2,1)S(1)}, u32[]{:S(2)}, u32[]{:S(2)}) async-start(bf16[16,38,8,128]{3,2,1,0:T(8,128)(2,1)} %pack.1), calls=%async_computation | async-start | bytes 2490368 | tf_op jit(solution)/shard_map/all_to_all | solution.py:563
  31.5 1.1 copy-start.2
  37.4 4.9 %copy-start.1 = (f32[4,128,544]{2,1,0:T(8,128)S(1)}, f32[4,128,544]{2,1,0:T(8,128)}, u32[]{:S(2)}) copy-start(f32[4,128,544]{2,1,0:T(8,128)} %get-tuple-element.18) | copy-start | bytes 3342340
  38.9 3.1 %collective-permute-start = (bf16[4,128,544]{1,2,0:T(8,128)(2,1)S(1)}, bf16[4,128,544]{1,2,0:T(8,128)(2,1)S(1)}, u32[]{:S(2)}, u32[]{:S(2)}) collective-permute-start(bf16[4,128,544]{1,2,0:T(8,128)(2,1)S(1)} %copy.52), channel_id=1, source_target_pairs={{0,1},{1,0},{2,3},{3,2},{4,5},{5,4},{6,7},{7,6},{8,9},{9,8},{10,11... | collective-permute-start | bytes 1671176 | tf_op jit(solution)/shard_map/ppermute | solution.py:614
  72.2 22.7 %all-to-all-start.2 = ((bf16[8,64,544]{2,1,0:T(8,128)(2,1)}), bf16[8,64,544]{2,1,0:T(8,128)(2,1)S(1)}, u32[]{:S(2)}, u32[]{:S(2)}) async-start(bf16[8,64,544]{2,1,0:T(8,128)(2,1)} %normalize.1), calls=%async_computation.2 | async-start | bytes 1310720 | tf_op jit(solution)/shard_map/all_to_all | solution.py:563
  94.8 2.5 %copy-start = (bf16[8,64,544]{2,1,0:T(8,128)(2,1)}, bf16[8,64,544]{2,1,0:T(8,128)(2,1)S(1)}, u32[]{:S(2)}) copy-start(bf16[8,64,544]{2,1,0:T(8,128)(2,1)S(1)} %all-to-all-done.2) | copy-start | bytes 1671172
  95.2 26.0 %collective-permute-start.1 = (bf16[4,128,544]{1,2,0:T(8,128)(2,1)S(1)}, bf16[4,128,544]{1,2,0:T(8,128)(2,1)S(1)}, u32[]{:S(2)}, u32[]{:S(2)}) collective-permute-start(bf16[4,128,544]{1,2,0:T(8,128)(2,1)S(1)} %copy.54), channel_id=1, source_target_pairs={{0,1},{1,0},{2,3},{3,2},{4,5},{5,4},{6,7},{7,6},{8,9},{9,8},{10,11... | collective-permute-start | bytes 1671176 | tf_op jit(solution)/shard_map/ppermute | solution.py:619
  114.2 25.0 %all-to-all-start.4 = ((bf16[16,22,8,128]{3,2,1,0:T(8,128)(2,1)}), bf16[16,22,8,128]{3,2,1,0:T(8,128)(2,1)S(1)}, u32[]{:S(2)}, u32[]{:S(2)}) async-start(bf16[16,22,8,128]{3,2,1,0:T(8,128)(2,1)} %get-tuple-element.24), calls=%async_computation.4 | async-start | bytes 1441792 | tf_op jit(solution)/shard_map/all_to_all | solution.py:563
  139.2 7.9 %copy-start.4 = (bf16[16,22,8,128]{3,2,1,0:T(8,128)(2,1)}, bf16[16,22,8,128]{3,2,1,0:T(8,128)(2,1)S(1)}, u32[]{:S(2)}) copy-start(bf16[16,22,8,128]{3,2,1,0:T(8,128)(2,1)S(1)} %all-to-all-done.4.came) | copy-start | bytes 2162692
  139.2 73.6 %all-to-all-start.3 = ((bf16[16,16,8,128]{3,2,1,0:T(8,128)(2,1)}), bf16[16,16,8,128]{3,2,1,0:T(8,128)(2,1)S(1)}, u32[]{:S(2)}, u32[]{:S(2)}) async-start(bf16[16,16,8,128]{3,2,1,0:T(8,128)(2,1)} %get-tuple-element.23), calls=%async_computation.3 | async-start | bytes 1048576 | tf_op jit(solution)/shard_map/all_to_all | solution.py:563
  146.4 0.7 copy-start.6
  212.8 0.8 copy-start.5

commit v4 on v3

--- a/solution.py
+++ b/solution.py
@@ -19,18 +19,21 @@
 INNER = 1024
 RANK = 512
 STATE = 16
-WIDE = RANK + 2 * STATE
+USED = RANK + 2 * STATE
+WIDE = 640
 SLOTS = 32
 KEPT = 3
 DEPTH = 8
 CORES = 2
 SHARE = PER * TURN // DEPTH
 HEAD = 16
+EDGE = 4
+EDGES = PER * EDGE
 FETCHED = CHUNKS * (STATE + KEPT)
 RETURNED = STATE + CHUNKS * KEPT
 LANES = 128
 TILES = INNER // LANES
-UNROLL = 4
+UNROLL = 16
 
 F32 = jnp.float32
 BF16 = jnp.bfloat16
@@ -109,7 +112,8 @@
 
 
 def silu(v):
-    return v / (1.0 + jnp.exp(-v))
+    half = 0.5 * v
+    return half + half * jnp.tanh(half)
 
 
 def conv_kernel(order_ref, hidden, weight, bias, x_weight, conv_out, sent, kept, rows):
@@ -165,8 +169,8 @@
 
 
 def head_kernel(
-    order, holder, sides, hidden, fetched, weight, bias, x_weight, conv_in, sent_in, kept_in,
-    conv_out, sent, kept, starts, rows, tiles, head, head_sent, head_kept, sems, start_sems,
+    order, holder, sides, hidden, fetched, weight, bias, x_weight, conv_in,
+    conv_out, sent, kept, starts, rows, tiles, head, sems, start_sems,
 ):
     arriving = []
     for i in range(REQUESTS):
@@ -177,6 +181,7 @@
             )
         )
         arriving[i].start()
+    leaving = []
     for i in range(REQUESTS):
         arriving[i].wait()
         for k in range(KEPT):
@@ -191,30 +196,20 @@
             first = 8 - KEPT + tap
             total = total + rows[first : first + HEAD, :] * weight[tap : tap + 1, :]
         head[i] = silu(total).astype(BF16)
+        leaving.append(pltpu.make_async_copy(head.at[i], conv_out.at[i, :HEAD], sems.at[i]))
+        leaving[i].start()
     part = jnp.dot(
         head[...].reshape(REQUESTS * HEAD, INNER), x_weight[...], preferred_element_type=F32
-    ).reshape(REQUESTS, HEAD, WIDE)
-    head_sent[...] = part[:PER].astype(BF16)
-    head_kept[...] = part[PER:]
-    copies = []
-    for i in range(REQUESTS):
-        copies.append((head.at[i], conv_out.at[i, :HEAD]))
-        if i < PER:
-            copies.append((head_sent.at[i], sent.at[i, :HEAD]))
-        else:
-            copies.append((head_kept.at[i - PER], kept.at[i - PER, :HEAD]))
-    copies = [
-        pltpu.make_async_copy(source, target, sems.at[k])
-        for k, (source, target) in enumerate(copies)
-    ]
-    for one in copies:
-        one.start()
-    for one in copies:
+    ).reshape(REQUESTS, HEAD, WIDE)[:, :EDGE]
+    sent[...] = part[:PER].reshape(EDGES, WIDE).astype(BF16)
+    kept[...] = part[PER:].reshape(EDGES, WIDE)
+    for one in leaving:
         one.wait()
 
 
-def put_heads(order, holder, sides, hidden, fetched, weight, bias, x_weight, conv_out, sent, kept):
+def put_heads(order, holder, sides, hidden, fetched, weight, bias, x_weight, conv_out):
     anywhere = pl.BlockSpec(memory_space=pl.ANY)
+    edges = pl.BlockSpec((EDGES, WIDE), lambda i, o, h, s: (0, 0))
     return pl.pallas_call(
         head_kernel,
         grid_spec=pltpu.PrefetchScalarGridSpec(
@@ -227,65 +222,68 @@
                 pl.BlockSpec((1, INNER), lambda i, o, h, s: (0, 0)),
                 pl.BlockSpec((INNER, WIDE), lambda i, o, h, s: (0, 0)),
                 anywhere,
-                anywhere,
-                anywhere,
-            ],
-            out_specs=[anywhere, anywhere, anywhere],
+            ],
+            out_specs=[anywhere, edges, edges],
             scratch_shapes=[
                 pltpu.VMEM((REQUESTS, KEPT, TILES, LANES), BF16),
                 pltpu.VMEM((8 + HEAD, INNER), F32),
                 pltpu.VMEM((KEPT * TILES, LANES), F32),
                 pltpu.VMEM((REQUESTS, HEAD, INNER), BF16),
-                pltpu.VMEM((PER, HEAD, WIDE), BF16),
-                pltpu.VMEM((PER, HEAD, WIDE), F32),
-                pltpu.SemaphoreType.DMA((2 * REQUESTS,)),
+                pltpu.SemaphoreType.DMA((REQUESTS,)),
                 pltpu.SemaphoreType.DMA((REQUESTS,)),
             ],
         ),
         out_shape=[
             jax.ShapeDtypeStruct(conv_out.shape, conv_out.dtype),
-            jax.ShapeDtypeStruct(sent.shape, sent.dtype),
-            jax.ShapeDtypeStruct(kept.shape, kept.dtype),
+            jax.ShapeDtypeStruct((EDGES, WIDE), BF16),
+            jax.ShapeDtypeStruct((EDGES, WIDE), F32),
         ],
-        input_output_aliases={8: 0, 9: 1, 10: 2},
+        input_output_aliases={8: 0},
         compiler_params=params(),
-        cost_estimate=cost(3, 4 * 2**20),
+        cost_estimate=cost(4, 4 * 2**20),
         name="put_heads",
-    )(order, holder, sides, hidden, fetched, weight, bias, x_weight, conv_out, sent, kept)
-
-
-def norm_kernel(parts, out):
+    )(order, holder, sides, hidden, fetched, weight, bias, x_weight, conv_out)
+
+
+def norm(total):
+    rank = total[:, :RANK]
+    inject = total[:, RANK : RANK + STATE]
+    readout = total[:, RANK + STATE : USED]
+    rank = rank * lax.rsqrt(jnp.mean(rank * rank, axis=1, keepdims=True) + EPSILON)
+    inject = inject * lax.rsqrt(
+        jnp.maximum(jnp.mean(inject * inject, axis=1, keepdims=True), NORM_FLOOR)
+    )
+    readout = readout * lax.rsqrt(
+        jnp.maximum(jnp.mean(readout * readout, axis=1, keepdims=True), NORM_FLOOR)
+    )
+    rest = jnp.zeros((total.shape[0], WIDE - USED), F32)
+    return jnp.concatenate([rank, inject, readout, rest], axis=1)
+
+
+def norm_kernel(parts, edge, edge_came, out):
     total = parts[0].astype(F32)
     for k in range(1, DEPTH):
         total = total + parts[k].astype(F32)
-    rank = total[:, :RANK]
-    inject = total[:, RANK : RANK + STATE]
-    readout = total[:, RANK + STATE :]
-    rank = rank * lax.rsqrt(jnp.mean(rank * rank, axis=1, keepdims=True) + EPSILON)
-    inject = inject * lax.rsqrt(
-        jnp.maximum(jnp.mean(inject * inject, axis=1, keepdims=True), NORM_FLOOR)
-    )
-    readout = readout * lax.rsqrt(
-        jnp.maximum(jnp.mean(readout * readout, axis=1, keepdims=True), NORM_FLOOR)
-    )
-    joined = jnp.concatenate([rank, inject, readout], axis=1).astype(BF16)
+    joined = norm(total).astype(BF16)
+    edges = (edge[...] + edge_came[...].astype(F32)).astype(BF16)
     for k in range(DEPTH):
-        out[k] = joined
-
-
-def normalize(parts):
+        out[k, :SHARE] = joined
+        out[k, SHARE:] = edges
+
+
+def normalize(parts, edge, edge_came):
     return pl.pallas_call(
         norm_kernel,
-        out_shape=jax.ShapeDtypeStruct((DEPTH, SHARE, WIDE), BF16),
+        out_shape=jax.ShapeDtypeStruct((DEPTH, SHARE + EDGES, WIDE), BF16),
         compiler_params=params(),
         cost_estimate=cost(1.5, 2**20),
         name="normalize",
-    )(parts)
+    )(parts, edge, edge_came)
 
 
 def scan_kernel(
-    own, order_ref, holder, sides, normed_ref, dt_weight, dt_bias, a_log, skip, conv, gate, start,
-    last, other_last, base, gated, final, dts, us, spread, rates, states,
+    own, order_ref, holder, sides, shares, edge_parts, dt_weight, dt_bias, a_log, skip, conv, gate, start,
+    last, other_last, base, gated, final, dts, us, spread, rates, states, edges,
 ):
     step = pl.program_id(0)
     to = holder[PER + step] if own else holder[step]
@@ -293,8 +291,17 @@
     @pl.when(step == 0)
     def _():
         rows_to_tiles(rates, 0, -LOG2_E * jnp.exp(a_log[...]))
-
-    columns = normed_ref[0, :, RANK:].astype(F32).T
+        total = edge_parts[0, SHARE:].astype(F32)
+        for k in range(1, DEPTH):
+            total = total + edge_parts[k, SHARE:].astype(F32)
+        total = norm(total).astype(BF16).astype(F32)
+        for k in range(PER):
+            edges[k, :EDGE] = total[k * EDGE : (k + 1) * EDGE]
+
+    normed = jnp.concatenate([shares[0, :SHARE], shares[1, :SHARE]], axis=0).astype(F32)
+    first = lax.broadcasted_iota(jnp.int32, (8, WIDE), 0) < KEPT
+    normed = jnp.concatenate([jnp.where(first, edges[step], normed[:8]), normed[8:]], axis=0)
+    columns = normed[:, RANK:].T[: 2 * STATE]
     for t in range(TURN):
         spread[t * 2 * STATE : (t + 1) * 2 * STATE, :] = jnp.broadcast_to(
             columns[:, t : t + 1], (2 * STATE, LANES)
@@ -311,7 +318,7 @@
             states[pl.ds(part * 8 * TILES + tile, 8, stride=TILES), :] = start[
                 0, part * TILES + tile
             ].astype(F32)
-    rank = normed_ref[0, :, :RANK]
+    rank = normed[:, :RANK].astype(BF16)
     pair = 2 * LANES
     for block in range(INNER // pair):
         cols = slice(block * pair, (block + 1) * pair)
@@ -373,7 +380,8 @@
             num_scalar_prefetch=3,
             grid=(PER,),
             in_specs=[
-                pl.BlockSpec((1, TURN, WIDE), lambda i, o, h, s: (i, 0, 0)),
+                pl.BlockSpec((DEPTH // PER, SHARE + EDGES, WIDE), lambda i, o, h, s: (i, 0, 0)),
+                whole((DEPTH, SHARE + EDGES, WIDE)),
                 whole((RANK, INNER)),
                 whole((1, INNER)),
                 whole((STATE, INNER)),
@@ -398,60 +406,43 @@
                 pltpu.VMEM((TURN * 2 * STATE, LANES), F32),
                 pltpu.VMEM((STATE * TILES, LANES), F32),
                 pltpu.VMEM((STATE * TILES, LANES), F32),
+                pltpu.VMEM((PER, 8, WIDE), F32),
             ],
         ),
         out_shape=[
             jax.ShapeDtypeStruct((REQUESTS, TURN, INNER), BF16),
             jax.ShapeDtypeStruct((GROUPS, blocks, TILES, LANES), BF16),
         ],
-        input_output_aliases={} if own else {13: 0},
+        input_output_aliases={} if own else {14: 0},
         compiler_params=params(),
         cost_estimate=cost(15, 4 * 2**20),
         name="scan",
-    )(order, holder, sides, normed, dt_weight, dt_bias, a_log, skip, conv, gate, fetched, hidden,
+    )(order, holder, sides, normed, normed, dt_weight, dt_bias, a_log, skip, conv, gate, fetched, hidden,
       hidden, skip if own else base)
 
 
-def widen(came, wide, g):
+def widen(came, wide, g, row):
     for part in range(STATE // 8):
         for tile in range(TILES):
             rows, cols = block_of(part, tile)
-            wide[g, rows, cols] = came[g, part * TILES + tile].astype(F32)
-
-
-def place_kernel(
-    slots, other_slots, taken, came, ssm, conv, new_ssm, new_conv, wide, inputs, sems, base_sems
-):
-    def base(s):
-        return pltpu.make_async_copy(ssm.at[s], new_ssm.at[s], base_sems.at[s])
-
-    def copy(g):
-        return pltpu.make_async_copy(wide.at[g], new_ssm.at[slots[g]], sems.at[g])
-
-    def begin_base(s, carry):
-        @pl.when(taken[s] == 0)
-        def _():
-            base(s).start()
-
-        return carry
-
-    def finish_base(s, carry):
-        @pl.when(taken[s] == 0)
-        def _():
-            base(s).wait()
-
-        return carry
+            wide[row, rows, cols] = came[g, part * TILES + tile].astype(F32)
+
+
+def place_kernel(slots, other_slots, came, ssm, conv, new_ssm, new_conv, inputs, sem):
+    base = pltpu.make_async_copy(ssm, new_ssm, sem)
+    base.start()
+    for k in range(KEPT):
+        rows_to_tiles(inputs, k * SLOTS * TILES, conv[k])
 
     def put(slot, g, first):
         for k in range(KEPT):
             row = pl.multiple_of((k * SLOTS + slot) * TILES, TILES)
             inputs[pl.ds(row, TILES), :] = came[g, first + k].astype(F32)
 
-    def begin(g, carry):
+    def each(g, carry):
         @pl.when(slots[g] < SLOTS)
         def _():
-            widen(came, wide, g)
-            copy(g).start()
+            widen(came, new_ssm, g, slots[g])
             put(slots[g], g, STATE)
 
         @pl.when(other_slots[g] < SLOTS)
@@ -460,45 +451,31 @@
 
         return carry
 
-    def finish(g, carry):
-        @pl.when(slots[g] < SLOTS)
-        def _():
-            copy(g).wait()
-
-        return carry
-
-    lax.fori_loop(0, SLOTS, begin_base, 0)
-    for k in range(KEPT):
-        rows_to_tiles(inputs, k * SLOTS * TILES, conv[k])
-    lax.fori_loop(0, GROUPS, begin, 0)
+    base.wait()
+    lax.fori_loop(0, GROUPS, each, 0)
     for k in range(KEPT):
         for tile in range(TILES):
             new_conv[k, :, tile * LANES : (tile + 1) * LANES] = inputs[
                 pl.ds(k * SLOTS * TILES + tile, SLOTS, stride=TILES), :
             ]
-    lax.fori_loop(0, GROUPS, finish, 0)
-    lax.fori_loop(0, SLOTS, finish_base, 0)
-
-
-def place(slots, other_slots, taken, came, ssm, conv):
-    anywhere = pl.BlockSpec(memory_space=pl.ANY)
-    rows = pl.BlockSpec((KEPT, SLOTS, INNER), lambda i, s, o, t: (0, 0, 0))
+
+
+def place(slots, other_slots, came, ssm, conv):
+    rows = pl.BlockSpec((KEPT, SLOTS, INNER), lambda i, s, o: (0, 0, 0))
     return pl.pallas_call(
         place_kernel,
         grid_spec=pltpu.PrefetchScalarGridSpec(
-            num_scalar_prefetch=3,
+            num_scalar_prefetch=2,
             grid=(1,),
             in_specs=[
-                pl.BlockSpec((GROUPS, RETURNED, TILES, LANES), lambda i, s, o, t: (0, 0, 0, 0)),
-                anywhere,
+                pl.BlockSpec((GROUPS, RETURNED, TILES, LANES), lambda i, s, o: (0, 0, 0, 0)),
+                pl.BlockSpec(memory_space=pl.ANY),
                 rows,
             ],
-            out_specs=[anywhere, rows],
+            out_specs=[pl.BlockSpec((SLOTS, STATE, INNER), lambda i, s, o: (0, 0, 0)), rows],
             scratch_shapes=[
-                pltpu.VMEM((GROUPS, STATE, INNER), F32),
                 pltpu.VMEM((KEPT * SLOTS * TILES, LANES), F32),
-                pltpu.SemaphoreType.DMA((GROUPS,)),
-                pltpu.SemaphoreType.DMA((SLOTS,)),
+                pltpu.SemaphoreType.DMA,
             ],
         ),
         out_shape=[
@@ -506,9 +483,9 @@
             jax.ShapeDtypeStruct((KEPT, SLOTS, INNER), F32),
         ],
         compiler_params=params(),
-        cost_estimate=cost(4, 6 * 2**20),
+        cost_estimate=cost(6, 6 * 2**20),
         name="place",
-    )(slots, other_slots, taken, came, ssm, conv)
+    )(slots, other_slots, came, ssm, conv)
 
 
 def store_kernel(slots, came, ssm_in, new_ssm, wide, sems):
@@ -518,7 +495,7 @@
     def begin(g, carry):
         @pl.when(slots[g] < SLOTS)
         def _():
-            widen(came, wide, g)
+            widen(came, wide, g, g)
             copy(g).start()
 
         return carry
@@ -592,10 +569,6 @@
     targets = jnp.where(jnp.any(served, axis=2), slots, SLOTS)
     own_slots = jnp.where(core == 0, targets[:, 0], targets[:, 1])
     other_slots = jnp.where(core == 0, targets[:, 1], targets[:, 0])
-    taken = jnp.sum(
-        (own_slots[None, :] == jnp.arange(SLOTS, dtype=jnp.int32)[:, None]).astype(jnp.int32),
-        axis=1,
-    )
 
     at = jnp.arange(REQUESTS, dtype=jnp.int32)
     sides = jnp.stack([1 - core, core]).astype(jnp.int32)
@@ -606,15 +579,18 @@
 
     conv_rows = jnp.swapaxes(conv_cache, 0, 1)
     bias = conv_bias.reshape(1, INNER)
-    fetched = exchange(pack(slots.reshape(-1), ssm_cache, conv_rows), "dp")
+    x_weight = jnp.pad(x_weight, ((0, 0), (0, WIDE - USED)))
+    packed = pack(slots.reshape(-1), ssm_cache, conv_rows)
+    packed, order, x_weight = lax.optimization_barrier((packed, order, x_weight))
+    fetched = exchange(packed, "dp")
     conv, sent, kept = convolve(order, hidden_x, conv_weight, bias, x_weight)
-    conv, sent, kept = put_heads(
-        order, holder, sides, hidden_x, fetched, conv_weight, bias, x_weight, conv, sent, kept
-    )
     parts = (kept + lax.ppermute(sent, "core", SWAP).astype(F32)).astype(BF16)
-    share = normalize(exchange(parts.reshape(DEPTH, SHARE, WIDE), "z"))
-
-    normed = exchange(share, "z").reshape(PER, TURN, WIDE)
+    parts, fetched = lax.optimization_barrier((parts, fetched))
+    parts = exchange(parts.reshape(DEPTH, SHARE, WIDE), "z")
+    conv, edge_sent, edge = put_heads(
+        order, holder, sides, hidden_x, fetched, conv_weight, bias, x_weight, conv
+    )
+    normed = exchange(normalize(parts, edge, lax.ppermute(edge_sent, "core", SWAP)), "z")
     gated, came = None, []
     for values in (normed, lax.ppermute(normed, "core", SWAP)):
         gated, final = scan(
@@ -632,8 +608,10 @@
             hidden_x,
             gated,
         )
+        if came:
+            came[0], final = lax.optimization_barrier((came[0], final))
         came.append(exchange(final, "dp"))
-    new_ssm, new_conv = place(own_slots, other_slots, taken, came[0], ssm_cache, conv_rows)
+    new_ssm, new_conv = place(own_slots, other_slots, came[0], ssm_cache, conv_rows)
     new_ssm = store(other_slots, came[1], new_ssm)
     return (gated, new_ssm, jnp.swapaxes(new_conv, 0, 1))
 

time: 218 us -> 161 us (0.74)
  the two profiles are of different devices: /device:TPU:19 before, /device:TPU:8 now
where the time goes in v4:
time: 161 us; the launch traced here: 160 us
  Pallas kernels  66.5 us (41%)
  waiting for transfers between devices  42.6 us (26%)
  starting transfers between devices  36.6 us (23%)
  local copies, waits for them, and re-layouts  8.96 us (6%)
  other arithmetic  4.4 us (3%)
    all_to_all x5, waiting for transfers between devices, exchange(): return lax.all_to_all(values, axis, split_axis=0, concat_axis=0, tiled=True)  38.9 us
    all_to_all x5, starting transfers between devices, exchange(): return lax.all_to_all(values, axis, split_axis=0, concat_axis=0, tiled=True)  36.5 us
    pallas_call x2, Pallas kernels, scan(): pl.pallas_call(functools.partial(scan_kernel, own), grid_spec=pltpu.Prefe...  35.3 us
    pallas_call x1, Pallas kernels, convolve(): pl.pallas_call(conv_kernel, grid_spec=pltpu.PrefetchScalarGridSpec(num_sc...  10.7 us
    pallas_call x1, Pallas kernels, pack(): pl.pallas_call(pack_kernel, grid_spec=pltpu.PrefetchScalarGridSpec(num_sc...  5.33 us
    pallas_call x1, Pallas kernels, place(): pl.pallas_call(place_kernel, grid_spec=pltpu.PrefetchScalarGridSpec(num_s...  5.27 us
    unnamed x15, local copies, waits for them, and re-layouts  5.19 us
    pallas_call x1, Pallas kernels, put_heads(): pl.pallas_call(head_kernel, grid_spec=pltpu.PrefetchScalarGridSpec(num_sc...  5.01 us
  transfers between devices with their start and end apart: 8, of which 6 were waited for; matrix products, arithmetic and copies ran while one was open for 2% of the time, Pallas kernels for 35%

profile of v4, /device:TPU:8, one launch (start us, length us, event | category | flops | bytes accessed | tf_op | source)
XLA Modules:
  0.0 159.8 jit_solution(2433189505675442422)
XLA Ops:
  0.6 0.7 reshape.91
  1.4 0.1 copy.30
  1.5 0.2 dynamic-slice_reduce_fusion
  1.7 0.1 copy.29
  1.8 0.7 broadcast_in_dim.54
  2.5 0.1 copy.32
  2.6 0.1 copy.33
  2.7 0.6 reshape.92.slots
  3.3 1.7 %copy.34 = bf16[1024,544]{1,0:T(8,128)(2,1)S(1)} copy(bf16[1024,544]{0,1:T(8,128)(2,1)} %param.17) | data formatting | bytes 2228224 | tf_op args[4]
  5.0 1.2 pad.4.x_weight
  6.2 0.8 fusion.3
  7.0 5.3 %pack.1 = bf16[16,38,8,128]{3,2,1,0:T(8,128)(2,1)} custom-call(s32[32]{0:T(128)} %reshape.92.slots, f32[32,16,1024]{2,1,0:T(8,128)} %ssm.3, f32[3,32,1024]{2,1,0:T(8,128)} %bitcast.14), custom_call_target="tpu_custom_call" | custom-call | flops 3000000000 | bytes 4194304 | tf_op jit(solution)/shard_map/pack/pallas_call | solution.py:91
  12.3 7.6 %all-to-all-start = ((bf16[16,38,8,128]{3,2,1,0:T(8,128)(2,1)}), bf16[16,38,8,128]{3,2,1,0:T(8,128)(2,1)S(1)}, u32[]{:S(2)}, u32[]{:S(2)}) async-start(bf16[16,38,8,128]{3,2,1,0:T(8,128)(2,1)} %pack.1), calls=%async_computation | async-start | bytes 2490368 | tf_op jit(solution)/shard_map/all_to_all | solution.py:540
  20.0 10.7 %convolve.1 = (bf16[8,128,1024]{2,1,0:T(8,128)(2,1)}, bf16[4,128,640]{2,1,0:T(8,128)(2,1)}, f32[4,128,640]{2,1,0:T(8,128)}) custom-call(s32[8]{0:T(128)} %get-tuple-element.22.order_ref.order, bf16[8,128,1024]{2,1,0:T(8,128)(2,1)} %other_last.3, f32[4,1024]{1,0:T(4,128)} %weight.3, f32[1,1024]{1,0:T(1,128)} %bitcast.16, bf16[1024,640]{1,0:T(8,128)(2,1)} %pad.4.x_weight), custom_call_target="tpu_custom_call" | custom-call | flops 8000000000 | bytes 8388608 | tf_op jit(solution)/shard_map/convolve/pallas_call | solution.py:142
  30.7 0.0 collective-permute-start
  30.7 2.3 %collective-permute-done = bf16[4,128,640]{2,1,0:T(8,128)(2,1)S(1)} collective-permute-done((bf16[4,128,640]{2,1,0:T(8,128)(2,1)}, bf16[4,128,640]{2,1,0:T(8,128)(2,1)S(1)}, u32[]{:S(2)}, u32[]{:S(2)}) %collective-permute-start) | collective-permute-done | bytes 655392 | tf_op jit(solution)/shard_map/ppermute | solution.py:587
  33.0 2.3 %add_convert_fusion = bf16[4,128,640]{2,1,0:T(8,128)(2,1)} fusion(f32[4,128,640]{2,1,0:T(8,128)} %get-tuple-element.24, bf16[4,128,640]{2,1,0:T(8,128)(2,1)S(1)} %collective-permute-done), kind=kLoop, calls=%fused_computation | loop fusion | flops 983040 | bytes 2621440 | tf_op jit(solution)/shard_map/convert_element_type | solution.py:587
  35.3 3.3 %all-to-all-done.fetched.start = bf16[16,38,8,128]{3,2,1,0:T(8,128)(2,1)S(1)} async-done(((bf16[16,38,8,128]{3,2,1,0:T(8,128)(2,1)}), bf16[16,38,8,128]{3,2,1,0:T(8,128)(2,1)S(1)}, u32[]{:S(2)}, u32[]{:S(2)}) %all-to-all-start) | async-done | bytes 1245216 | tf_op jit(solution)/shard_map/all_to_all | solution.py:540
  38.6 0.0 copy-start
  38.6 8.5 %all-to-all-start.1 = ((bf16[8,64,640]{2,1,0:T(8,128)(2,1)}), bf16[8,64,640]{2,1,0:T(8,128)(2,1)S(1)}, u32[]{:S(2)}, u32[]{:S(2)}) async-start(bf16[8,64,640]{2,1,0:T(8,128)(2,1)} %bitcast.5), calls=%async_computation.1 | async-start | bytes 1310720 | tf_op jit(solution)/shard_map/all_to_all | solution.py:540
  47.1 0.7 pad_add_fusion.sides
  47.8 0.0 copy-done
  47.8 5.0 %put_heads.1 = (bf16[8,128,1024]{2,1,0:T(8,128)(2,1)}, bf16[16,640]{1,0:T(8,128)(2,1)}, f32[16,640]{1,0:T(8,128)}) custom-call(s32[8]{0:T(128)} %get-tuple-element.22.order_ref.order, s32[8]{0:T(128)} %get-tuple-element.41.holder, s32[2]{0:T(128)} %pad_add_fusion.sides, bf16[8,128,1024]{2,1,0:T(8,128)(2,1)} %other_last.3, ...), custom_call_target="tpu_custom_call", output_to_operand_aliasing={{0}: (8, {})} | custom-call | flops 4000000000 | bytes 4194304 | tf_op jit(solution)/shard_map/put_heads/pallas_call | solution.py:213
  52.8 0.1 collective-permute-start.1
  52.9 1.4 collective-permute-done.1.edge_came
  54.3 0.0 copy-start.6
  54.3 10.3 %all-to-all-done.1.parts = bf16[8,64,640]{2,1,0:T(8,128)(2,1)S(1)} async-done(((bf16[8,64,640]{2,1,0:T(8,128)(2,1)}), bf16[8,64,640]{2,1,0:T(8,128)(2,1)S(1)}, u32[]{:S(2)}, u32[]{:S(2)}) %all-to-all-start.1) | async-done | bytes 655392 | tf_op jit(solution)/shard_map/all_to_all | solution.py:540
  64.6 0.0 copy-start.3
  64.6 0.0 copy-done.6
  64.6 0.9 copy-done.3
  65.5 2.2 %normalize.1 = bf16[8,80,640]{2,1,0:T(8,128)(2,1)} custom-call(bf16[8,64,640]{2,1,0:T(8,128)(2,1)} %copy-done.3, f32[16,640]{1,0:T(8,128)} %get-tuple-element.30.edge, bf16[16,640]{1,0:T(8,128)(2,1)} %copy-done.6), custom_call_target="tpu_custom_call" | custom-call | flops 1500000000 | bytes 1048576 | tf_op jit(solution)/shard_map/normalize/pallas_call | solution.py:275
  67.7 3.5 %all-to-all-start.2 = ((bf16[8,80,640]{2,1,0:T(8,128)(2,1)}), bf16[8,80,640]{2,1,0:T(8,128)(2,1)S(1)}, u32[]{:S(2)}, u32[]{:S(2)}) async-start(bf16[8,80,640]{2,1,0:T(8,128)(2,1)} %normalize.1), calls=%async_computation.2 | async-start | bytes 1638400 | tf_op jit(solution)/shard_map/all_to_all | solution.py:540
  71.3 0.5 fusion.6
  71.8 20.8 %all-to-all-done.2.shares.edge_parts = bf16[8,80,640]{2,1,0:T(8,128)(2,1)S(1)} async-done(((bf16[8,80,640]{2,1,0:T(8,128)(2,1)}), bf16[8,80,640]{2,1,0:T(8,128)(2,1)S(1)}, u32[]{:S(2)}, u32[]{:S(2)}) %all-to-all-start.2) | async-done | bytes 819232 | tf_op jit(solution)/shard_map/all_to_all | solution.py:540
  92.6 0.0 copy-start.1
  92.6 0.0 collective-permute-start.2
  92.6 0.9 copy-done.1
  93.5 17.6 %scan.2 = (bf16[8,128,1024]{2,1,0:T(8,128)(2,1)}, bf16[16,22,8,128]{3,2,1,0:T(8,128)(2,1)}) custom-call(s32[8]{0:T(128)} %get-tuple-element.22.order_ref.order, s32[8]{0:T(128)} %get-tuple-element.41.holder, s32[2]{0:T(128)} %pad_add_fusion.sides, bf16[8,80,640]{2,1,0:T(8,128)(2,1)} %copy-done.1, bf16[8,80,640]{2,1,0:T(8,128)(2,1)} %copy-done.1, ...), custom_call_target="tpu_custom_call" | custom-call | flops 15000000512 | bytes 4194304 | tf_op jit(solution)/shard_map/scan/pallas_call | solution.py:377
  111.2 9.6 %all-to-all-start.3 = ((bf16[16,22,8,128]{3,2,1,0:T(8,128)(2,1)}), bf16[16,22,8,128]{3,2,1,0:T(8,128)(2,1)S(1)}, u32[]{:S(2)}, u32[]{:S(2)}) async-start(bf16[16,22,8,128]{3,2,1,0:T(8,128)(2,1)} %get-tuple-element.35), calls=%async_computation.3 | async-start | bytes 1441792 | tf_op jit(solution)/shard_map/all_to_all | solution.py:540
  120.8 0.0 collective-permute-done.2.shares.edge_parts
  120.8 0.0 copy-start.5
  120.8 0.9 copy-done.5
  121.7 17.7 %scan.3 = (bf16[8,128,1024]{2,1,0:T(8,128)(2,1)}, bf16[16,16,8,128]{3,2,1,0:T(8,128)(2,1)}) custom-call(s32[8]{0:T(128)} %get-tuple-element.22.order_ref.order, s32[8]{0:T(128)} %get-tuple-element.41.holder, s32[2]{0:T(128)} %pad_add_fusion.sides, bf16[8,80,640]{2,1,0:T(8,128)(2,1)} %copy-done.5, ...), custom_call_target="tpu_custom_call", output_to_operand_aliasing={{0}: (14, {})} | custom-call | flops 15000000512 | bytes 4194304 | tf_op jit(solution)/shard_map/scan/pallas_call | solution.py:377
  139.4 0.0 all-to-all-done.3.came
  139.4 0.0 copy-start.2
  139.4 7.2 %all-to-all-start.4 = ((bf16[16,16,8,128]{3,2,1,0:T(8,128)(2,1)}), bf16[16,16,8,128]{3,2,1,0:T(8,128)(2,1)S(1)}, u32[]{:S(2)}, u32[]{:S(2)}) async-start(bf16[16,16,8,128]{3,2,1,0:T(8,128)(2,1)} %get-tuple-element.37), calls=%async_computation.4 | async-start | bytes 1048576 | tf_op jit(solution)/shard_map/all_to_all | solution.py:540
  146.6 0.0 copy-done.2
  146.6 5.3 %place.1 = (f32[32,16,1024]{2,1,0:T(8,128)}, f32[3,32,1024]{2,1,0:T(8,128)}) custom-call(s32[16]{0:T(128)} %get-tuple-element.43.slots, s32[16]{0:T(128)} %get-tuple-element.44.other_slots.slots, bf16[16,22,8,128]{3,2,1,0:T(8,128)(2,1)} %copy-done.2, f32[32,16,1024]{2,1,0:T(8,128)} %ssm.3, f32[3,32,1024]{2,1,0:T(8,128)} %bitcast.15), custom_call_target="tpu_custom_call" | custom-call | flops 6000000000 | bytes 6291456 | tf_op jit(solution)/shard_map/place/pallas_call | solution.py:465
  151.9 4.4 %all-to-all-done.4.came = bf16[16,16,8,128]{3,2,1,0:T(8,128)(2,1)S(1)} async-done(((bf16[16,16,8,128]{3,2,1,0:T(8,128)(2,1)}), bf16[16,16,8,128]{3,2,1,0:T(8,128)(2,1)S(1)}, u32[]{:S(2)}, u32[]{:S(2)}) %all-to-all-start.4) | async-done | bytes 524320 | tf_op jit(solution)/shard_map/all_to_all | solution.py:540
  156.3 0.0 copy-start.4
  156.3 0.8 copy-done.4
  157.1 2.7 %store.1 = f32[32,16,1024]{2,1,0:T(8,128)} custom-call(s32[16]{0:T(128)} %get-tuple-element.44.other_slots.slots, bf16[16,16,8,128]{3,2,1,0:T(8,128)(2,1)} %copy-done.4, f32[32,16,1024]{2,1,0:T(8,128)} %get-tuple-element.39.ssm_in), custom_call_target="tpu_custom_call", output_to_operand_aliasing={{}: (2, {})} | custom-call | flops 2000000000 | bytes 2097152 | tf_op jit(solution)/shard_map/store/pallas_call | solution.py:516
  (9 shorter events, 0.1 us)
Async XLA Ops:
  12.3 26.3 %all-to-all-start = ((bf16[16,38,8,128]{3,2,1,0:T(8,128)(2,1)}), bf16[16,38,8,128]{3,2,1,0:T(8,128)(2,1)S(1)}, u32[]{:S(2)}, u32[]{:S(2)}) async-start(bf16[16,38,8,128]{3,2,1,0:T(8,128)(2,1)} %pack.1), calls=%async_computation | async-start | bytes 2490368 | tf_op jit(solution)/shard_map/all_to_all | solution.py:540
  30.7 2.3 %collective-permute-start = (bf16[4,128,640]{2,1,0:T(8,128)(2,1)}, bf16[4,128,640]{2,1,0:T(8,128)(2,1)S(1)}, u32[]{:S(2)}, u32[]{:S(2)}) collective-permute-start(bf16[4,128,640]{2,1,0:T(8,128)(2,1)} %get-tuple-element.25), channel_id=1, source_target_pairs={{0,1},{1,0},{2,3},{3,2},{4,5},{5,4},{6,7},{7,6},{8,9},{9,8},{10,11... | collective-permute-start | bytes 1966088 | tf_op jit(solution)/shard_map/ppermute | solution.py:587
  38.6 9.1 %copy-start = (bf16[16,38,8,128]{3,2,1,0:T(8,128)(2,1)}, bf16[16,38,8,128]{3,2,1,0:T(8,128)(2,1)S(1)}, u32[]{:S(2)}) copy-start(bf16[16,38,8,128]{3,2,1,0:T(8,128)(2,1)S(1)} %all-to-all-done.fetched.start) | copy-start | bytes 3735556
  38.6 26.0 %all-to-all-start.1 = ((bf16[8,64,640]{2,1,0:T(8,128)(2,1)}), bf16[8,64,640]{2,1,0:T(8,128)(2,1)S(1)}, u32[]{:S(2)}, u32[]{:S(2)}) async-start(bf16[8,64,640]{2,1,0:T(8,128)(2,1)} %bitcast.5), calls=%async_computation.1 | async-start | bytes 1310720 | tf_op jit(solution)/shard_map/all_to_all | solution.py:540
  52.8 1.5 collective-permute-start.1
  54.3 10.3 %copy-start.6 = (bf16[16,640]{1,0:T(8,128)(2,1)}, bf16[16,640]{1,0:T(8,128)(2,1)S(1)}, u32[]{:S(2)}) copy-start(bf16[16,640]{1,0:T(8,128)(2,1)S(1)} %collective-permute-done.1.edge_came) | copy-start | bytes 61444
  64.6 0.9 copy-start.3
  67.7 24.9 %all-to-all-start.2 = ((bf16[8,80,640]{2,1,0:T(8,128)(2,1)}), bf16[8,80,640]{2,1,0:T(8,128)(2,1)S(1)}, u32[]{:S(2)}, u32[]{:S(2)}) async-start(bf16[8,80,640]{2,1,0:T(8,128)(2,1)} %normalize.1), calls=%async_computation.2 | async-start | bytes 1638400 | tf_op jit(solution)/shard_map/all_to_all | solution.py:540
  92.6 0.9 copy-start.1
  92.6 28.2 %collective-permute-start.2 = (bf16[8,80,640]{2,1,0:T(8,128)(2,1)S(1)}, bf16[8,80,640]{2,1,0:T(8,128)(2,1)S(1)}, u32[]{:S(2)}, u32[]{:S(2)}) collective-permute-start(bf16[8,80,640]{2,1,0:T(8,128)(2,1)S(1)} %all-to-all-done.2.shares.edge_parts), channel_id=1, source_target_pairs={{0,1},{1,0},{2,3},{3,2},{4,5},{5,4},{6,7},{7,6},{8,9},{9,8},{10,11... | collective-permute-start | bytes 2457608 | tf_op jit(solution)/shard_map/ppermute | solution.py:595
  111.2 28.2 %all-to-all-start.3 = ((bf16[16,22,8,128]{3,2,1,0:T(8,128)(2,1)}), bf16[16,22,8,128]{3,2,1,0:T(8,128)(2,1)S(1)}, u32[]{:S(2)}, u32[]{:S(2)}) async-start(bf16[16,22,8,128]{3,2,1,0:T(8,128)(2,1)} %get-tuple-element.35), calls=%async_computation.3 | async-start | bytes 1441792 | tf_op jit(solution)/shard_map/all_to_all | solution.py:540
  120.8 0.9 copy-start.5
  139.4 7.2 %copy-start.2 = (bf16[16,22,8,128]{3,2,1,0:T(8,128)(2,1)}, bf16[16,22,8,128]{3,2,1,0:T(8,128)(2,1)S(1)}, u32[]{:S(2)}) copy-start(bf16[16,22,8,128]{3,2,1,0:T(8,128)(2,1)S(1)} %all-to-all-done.3.came) | copy-start | bytes 2162692
  139.4 16.9 %all-to-all-start.4 = ((bf16[16,16,8,128]{3,2,1,0:T(8,128)(2,1)}), bf16[16,16,8,128]{3,2,1,0:T(8,128)(2,1)S(1)}, u32[]{:S(2)}, u32[]{:S(2)}) async-start(bf16[16,16,8,128]{3,2,1,0:T(8,128)(2,1)} %get-tuple-element.37), calls=%async_computation.4 | async-start | bytes 1048576 | tf_op jit(solution)/shard_map/all_to_all | solution.py:540
  156.3 0.8 copy-start.4

commit v5 on v4

v5 whole, which is shorter than its diff:
```python
import functools

import jax
import jax.numpy as jnp
from jax import lax
from jax.experimental import pallas as pl
from jax.experimental.pallas import tpu as pltpu
from jax.sharding import Mesh, PartitionSpec as P

EPSILON = 1e-06
NORM_FLOOR = 0.25
LOG2_E = 1.4426950408889634

GROUPS = 16
REQUESTS = 8
CHUNKS = 2
PER = REQUESTS // CHUNKS
TURN = 128
INNER = 1024
RANK = 512
STATE = 16
USED = RANK + 2 * STATE
WIDE = 640
SLOTS = 32
KEPT = 3
DEPTH = 8
CORES = 2
SHARE = PER * TURN // DEPTH
HEAD = 16
EDGE = 4
EDGES = PER * EDGE
PAIR = 2

ORDER, HOLDER, OWN, OTHER, SIDES, ROUTING = 0, 8, 16, 32, 48, 64
FETCHED = CHUNKS * (STATE + KEPT)
RETURNED = STATE + CHUNKS * KEPT
LANES = 128
TILES = INNER // LANES
UNROLL = 16

F32 = jnp.float32
BF16 = jnp.bfloat16
SWAP = [(0, 1), (1, 0)]


def params():
    return pltpu.CompilerParams(vmem_limit_bytes=56 * 2**20)


def cost(us, bytes_accessed):
    return pl.CostEstimate(
        flops=int(us * 1.0e9), bytes_accessed=bytes_accessed, transcendentals=0
    )


def rows_to_tiles(tiles, first, rows):
    for tile in range(TILES):
        tiles[pl.ds(first + tile, rows.shape[0], stride=TILES), :] = rows[
            :, tile * LANES : (tile + 1) * LANES
        ]


def block_of(part, tile):
    return slice(part * 8, (part + 1) * 8), slice(tile * LANES, (tile + 1) * LANES)


def pack_kernel(
    holders, places, ssm, conv, routing, out, slots, ranks, states, inputs, packed, sems, out_sems
):
    me = lax.axis_index("dp")
    core = lax.axis_index("core")

    def copy(e):
        return pltpu.make_async_copy(ssm.at[slots[e]], states.at[e], sems.at[e])

    def begin(g, carry):
        held = [holders[g * REQUESTS + i] for i in range(REQUESTS)]
        rank = [jnp.int32(0)] * REQUESTS
        for i in range(REQUESTS):
            for j in range(i + 1, REQUESTS):
                below = (held[j] < held[i]).astype(jnp.int32)
                rank[i] = rank[i] + below
                rank[j] = rank[j] + (1 - below)
        found = [jnp.int32(-1)] * CHUNKS
        for i in range(REQUESTS):
            here = held[i] == me
            place = places[g * REQUESTS + i]
            for c in range(CHUNKS):
                found[c] = jnp.where(here & (rank[i] % CHUNKS == c), place, found[c])
            ranks[g * REQUESTS + i] = rank[i]
        for c in range(CHUNKS):
            slots[g * CHUNKS + c] = jnp.maximum(found[c], 0)
            copy(g * CHUNKS + c).start()
        first = jnp.where(found[0] < 0, SLOTS, found[0])
        second = jnp.where(found[1] < 0, SLOTS, found[1])
        routing[OWN + g] = jnp.where(core == 0, first, second)
        routing[OTHER + g] = jnp.where(core == 0, second, first)
        return carry

    lax.fori_loop(0, GROUPS, begin, 0)
    for i in range(REQUESTS):
        rank = ranks[me * REQUESTS + i]
        at = rank // CHUNKS + jnp.where(rank % CHUNKS == core, PER, 0)
        routing[ORDER + at] = jnp.int32(i)
        routing[HOLDER + at] = holders[me * REQUESTS + i]
    routing[SIDES] = 1 - core
    routing[SIDES + 1] = core
    for k in range(KEPT):
        rows_to_tiles(inputs, k * SLOTS * TILES, conv[k])

    def finish(g, carry):
        for c in range(CHUNKS):
            e = g * CHUNKS + c
            for k in range(KEPT):
                row = pl.multiple_of((k * SLOTS + slots[e]) * TILES, TILES)
                packed[g, CHUNKS * STATE + c * KEPT + k] = inputs[pl.ds(row, TILES), :].astype(BF16)
            copy(e).wait()
            for part in range(STATE // 8):
                for tile in range(TILES):
                    rows, cols = block_of(part, tile)
                    packed[g, c * STATE + part * TILES + tile] = states[e, rows, cols].astype(BF16)
        pltpu.make_async_copy(packed.at[g], out.at[g], out_sems.at[g]).start()
        return carry

    def end(g, carry):
        pltpu.make_async_copy(packed.at[g], out.at[g], out_sems.at[g]).wait()
        return carry

    lax.fori_loop(0, GROUPS, finish, 0)
    lax.fori_loop(0, GROUPS, end, 0)


def pack(holders, places, ssm, conv):
    anywhere = pl.BlockSpec(memory_space=pl.ANY)
    return pl.pallas_call(
        pack_kernel,
        grid_spec=pltpu.PrefetchScalarGridSpec(
            num_scalar_prefetch=2,
            grid=(1,),
            in_specs=[
                anywhere,
                pl.BlockSpec((KEPT, SLOTS, INNER), lambda i, h, p: (0, 0, 0)),
            ],
            out_specs=[pl.BlockSpec(memory_space=pltpu.SMEM), anywhere],
            scratch_shapes=[
                pltpu.SMEM((GROUPS * CHUNKS,), jnp.int32),
                pltpu.SMEM((GROUPS * REQUESTS,), jnp.int32),
                pltpu.VMEM((GROUPS * CHUNKS, STATE, INNER), F32),
                pltpu.VMEM((KEPT * SLOTS * TILES, LANES), F32),
                pltpu.VMEM((GROUPS, FETCHED, TILES, LANES), BF16),
                pltpu.SemaphoreType.DMA((GROUPS * CHUNKS,)),
                pltpu.SemaphoreType.DMA((GROUPS,)),
            ],
        ),
        out_shape=[
            jax.ShapeDtypeStruct((ROUTING,), jnp.int32),
            jax.ShapeDtypeStruct((GROUPS, FETCHED, TILES, LANES), BF16),
        ],
        compiler_params=params(),
        cost_estimate=cost(4, 4 * 2**20),
        name="pack",
    )(holders, places, ssm, conv)


def silu(v):
    half = 0.5 * v
    return half + half * jnp.tanh(half)


def project(values, x_weight):
    return lax.dot_general(
        values, x_weight[...], (((1,), (1,)), ((), ())), preferred_element_type=F32
    )


def conv_kernel(
    routing, hidden, hidden_too, weight, bias, x_weight, conv_out, sent, kept, rows
):
    step = pl.program_id(0)
    rows[:8, :] = jnp.zeros((8, INNER), F32)
    for which, source in enumerate((hidden, hidden_too)):
        for tile in range(TILES):
            cols = slice(tile * LANES, (tile + 1) * LANES)
            rows[8:, cols] = source[0, :, cols].astype(F32)
            total = jnp.zeros((TURN, LANES), F32) + bias[:, cols]
            for tap in range(KEPT + 1):
                first = 8 - KEPT + tap
                total = total + rows[first : first + TURN, cols] * weight[tap : tap + 1, cols]
            conv_out[which, :, cols] = silu(total).astype(BF16)
    part = project(conv_out[...].reshape(PAIR * TURN, INNER), x_weight).reshape(PAIR, TURN, USED)
    rest = jnp.zeros((PAIR, TURN, WIDE - USED), F32)

    @pl.when(step < PER // PAIR)
    def _():
        sent[:, :, :USED] = part.astype(BF16)
        sent[:, :, USED:] = rest.astype(BF16)

    @pl.when(step >= PER // PAIR)
    def _():
        kept[:, :, :USED] = part
        kept[:, :, USED:] = rest


def convolve(routing, hidden, weight, bias, x_weight):
    half = PER // PAIR
    return pl.pallas_call(
        conv_kernel,
        grid_spec=pltpu.PrefetchScalarGridSpec(
            num_scalar_prefetch=1,
            grid=(REQUESTS // PAIR,),
            in_specs=[
                pl.BlockSpec((1, TURN, INNER), lambda i, r: (r[ORDER + PAIR * i], 0, 0)),
                pl.BlockSpec((1, TURN, INNER), lambda i, r: (r[ORDER + PAIR * i + 1], 0, 0)),
                pl.BlockSpec((KEPT + 1, INNER), lambda i, r: (0, 0)),
                pl.BlockSpec((1, INNER), lambda i, r: (0, 0)),
                pl.BlockSpec((USED, INNER), lambda i, r: (0, 0)),
            ],
            out_specs=[
                pl.BlockSpec((PAIR, TURN, INNER), lambda i, r: (i, 0, 0)),
                pl.BlockSpec((PAIR, TURN, WIDE), lambda i, r: (jnp.minimum(i, half - 1), 0, 0)),
                pl.BlockSpec((PAIR, TURN, WIDE), lambda i, r: (jnp.maximum(i - half, 0), 0, 0)),
            ],
            scratch_shapes=[pltpu.VMEM((8 + TURN, INNER), F32)],
        ),
        out_shape=[
            jax.ShapeDtypeStruct((REQUESTS, TURN, INNER), BF16),
            jax.ShapeDtypeStruct((PER, TURN, WIDE), BF16),
            jax.ShapeDtypeStruct((PER, TURN, WIDE), F32),
        ],
        compiler_params=params(),
        cost_estimate=cost(8, 8 * 2**20),
        name="convolve",
    )(routing, hidden, hidden, weight, bias, x_weight)


def head_kernel(
    routing, hidden, fetched, weight, bias, x_weight, conv_in,
    conv_out, sent, kept, starts, rows, tiles, head, sems, start_sems,
):
    arriving = []
    for i in range(REQUESTS):
        first = CHUNKS * STATE + routing[SIDES + i // PER] * KEPT
        arriving.append(
            pltpu.make_async_copy(
                fetched.at[routing[HOLDER + i], pl.ds(first, KEPT)], starts.at[i], start_sems.at[i]
            )
        )
        arriving[i].start()
    leaving = []
    for i in range(REQUESTS):
        arriving[i].wait()
        for k in range(KEPT):
            tiles[k * TILES : (k + 1) * TILES, :] = starts[i, k].astype(F32)
        for tile in range(TILES):
            rows[8 - KEPT : 8, tile * LANES : (tile + 1) * LANES] = tiles[
                pl.ds(tile, KEPT, stride=TILES), :
            ]
        rows[8:, :] = hidden[routing[ORDER + i]].astype(F32)
        total = jnp.zeros((HEAD, INNER), F32) + bias[...]
        for tap in range(KEPT + 1):
            first = 8 - KEPT + tap
            total = total + rows[first : first + HEAD, :] * weight[tap : tap + 1, :]
        head[i] = silu(total).astype(BF16)
        leaving.append(pltpu.make_async_copy(head.at[i], conv_out.at[i, :HEAD], sems.at[i]))
        leaving[i].start()
    part = project(head[...].reshape(REQUESTS * HEAD, INNER), x_weight)
    part = part.reshape(REQUESTS, HEAD, USED)[:, :EDGE]
    rest = jnp.zeros((EDGES, WIDE - USED), F32)
    sent[:, :USED] = part[:PER].reshape(EDGES, USED).astype(BF16)
    sent[:, USED:] = rest.astype(BF16)
    kept[:, :USED] = part[PER:].reshape(EDGES, USED)
    kept[:, USED:] = rest
    for one in leaving:
        one.wait()


def put_heads(routing, hidden, fetched, weight, bias, x_weight, conv_out):
    anywhere = pl.BlockSpec(memory_space=pl.ANY)
    edges = pl.BlockSpec((EDGES, WIDE), lambda i, r: (0, 0))
    return pl.pallas_call(
        head_kernel,
        grid_spec=pltpu.PrefetchScalarGridSpec(
            num_scalar_prefetch=1,
            grid=(1,),
            in_specs=[
                pl.BlockSpec((REQUESTS, HEAD, INNER), lambda i, r: (0, 0, 0)),
                anywhere,
                pl.BlockSpec((KEPT + 1, INNER), lambda i, r: (0, 0)),
                pl.BlockSpec((1, INNER), lambda i, r: (0, 0)),
                pl.BlockSpec((USED, INNER), lambda i, r: (0, 0)),
                anywhere,
            ],
            out_specs=[anywhere, edges, edges],
            scratch_shapes=[
                pltpu.VMEM((REQUESTS, KEPT, TILES, LANES), BF16),
                pltpu.VMEM((8 + HEAD, INNER), F32),
                pltpu.VMEM((KEPT * TILES, LANES), F32),
                pltpu.VMEM((REQUESTS, HEAD, INNER), BF16),
                pltpu.SemaphoreType.DMA((REQUESTS,)),
                pltpu.SemaphoreType.DMA((REQUESTS,)),
            ],
        ),
        out_shape=[
            jax.ShapeDtypeStruct(conv_out.shape, conv_out.dtype),
            jax.ShapeDtypeStruct((EDGES, WIDE), BF16),
            jax.ShapeDtypeStruct((EDGES, WIDE), F32),
        ],
        input_output_aliases={6: 0},
        compiler_params=params(),
        cost_estimate=cost(4, 4 * 2**20),
        name="put_heads",
    )(routing, hidden, fetched, weight, bias, x_weight, conv_out)


def norm(total):
    rank = total[:, :RANK]
    inject = total[:, RANK : RANK + STATE]
    readout = total[:, RANK + STATE : USED]
    rank = rank * lax.rsqrt(jnp.mean(rank * rank, axis=1, keepdims=True) + EPSILON)
    inject = inject * lax.rsqrt(
        jnp.maximum(jnp.mean(inject * inject, axis=1, keepdims=True), NORM_FLOOR)
    )
    readout = readout * lax.rsqrt(
        jnp.maximum(jnp.mean(readout * readout, axis=1, keepdims=True), NORM_FLOOR)
    )
    rest = jnp.zeros((total.shape[0], WIDE - USED), F32)
    return jnp.concatenate([rank, inject, readout, rest], axis=1)


def norm_kernel(parts, edge, edge_came, out, came, sem):
    arriving = pltpu.make_async_copy(edge_came, came, sem)
    arriving.start()
    total = parts[0].astype(F32)
    for k in range(1, DEPTH):
        total = total + parts[k].astype(F32)
    joined = norm(total).astype(BF16)
    arriving.wait()
    edges = (edge[...] + came[...].astype(F32)).astype(BF16)
    for k in range(DEPTH):
        out[k, :SHARE] = joined
        out[k, SHARE:] = edges


def normalize(parts, edge, edge_came):
    return pl.pallas_call(
        norm_kernel,
        in_specs=[
            pl.BlockSpec(memory_space=pltpu.VMEM),
            pl.BlockSpec(memory_space=pltpu.VMEM),
            pl.BlockSpec(memory_space=pl.ANY),
        ],
        scratch_shapes=[pltpu.VMEM((EDGES, WIDE), BF16), pltpu.SemaphoreType.DMA],
        out_shape=jax.ShapeDtypeStruct((DEPTH, SHARE + EDGES, WIDE), BF16),
        compiler_params=params(),
        cost_estimate=cost(1.5, 2**20),
        name="normalize",
    )(parts, edge, edge_came)


def scan_kernel(
    own, routing, came, dt_weight, dt_bias, a_log, skip, conv, gate, start,
    last, other_last, base, gated, final, dts, us, spread, rates, states, shares, sem,
):
    step = pl.program_id(0)
    to = routing[HOLDER + (PER if own else 0) + step]

    @pl.when(step == 0)
    def _():
        arriving = pltpu.make_async_copy(came, shares, sem)
        arriving.start()
        rows_to_tiles(rates, 0, -LOG2_E * jnp.exp(a_log[...]))
        arriving.wait()
        total = shares[0, SHARE:].astype(F32)
        for k in range(1, DEPTH):
            total = total + shares[k, SHARE:].astype(F32)
        total = norm(total)
        edge = lax.broadcasted_iota(jnp.int32, (HEAD, WIDE), 0) < KEPT
        rest = jnp.zeros((HEAD - EDGE, WIDE), F32)
        for k in range(PER):
            at = k * (DEPTH // PER)
            first = jnp.concatenate([total[k * EDGE : (k + 1) * EDGE], rest], axis=0)
            shares[at, :HEAD] = jnp.where(edge, first, shares[at, :HEAD].astype(F32)).astype(BF16)

    span = DEPTH // PER
    normed = shares[pl.ds(step * span, span), :SHARE].reshape(TURN, WIDE)
    columns = normed[:, RANK:].astype(F32).T[: 2 * STATE]
    for t in range(TURN):
        spread[t * 2 * STATE : (t + 1) * 2 * STATE, :] = jnp.broadcast_to(
            columns[:, t : t + 1], (2 * STATE, LANES)
        )
    if own:
        for which, (rows, at) in enumerate(((last, to), (other_last, routing[HOLDER + step]))):
            rows_to_tiles(states, 0, rows[0].astype(F32)[HEAD - KEPT :, :])
            for k in range(KEPT):
                final[at, STATE + which * KEPT + k] = states[
                    k * TILES : (k + 1) * TILES, :
                ].astype(BF16)
    for part in range(STATE // 8):
        for tile in range(TILES):
            states[pl.ds(part * 8 * TILES + tile, 8, stride=TILES), :] = start[
                0, part * TILES + tile
            ].astype(F32)
    rank = normed[:, :RANK]
    pair = 2 * LANES
    for block in range(INNER // pair):
        cols = slice(block * pair, (block + 1) * pair)
        raw = jnp.dot(rank, dt_weight[:, cols], preferred_element_type=F32) + dt_bias[:, cols]
        dt = jnp.maximum(raw, 0.0) + jnp.log1p(jnp.exp(-jnp.abs(raw)))
        for k in range(2):
            tile = 2 * block + k
            dts[pl.ds(tile, TURN, stride=TILES), :] = dt[:, k * LANES : (k + 1) * LANES]
            us[pl.ds(tile, TURN, stride=TILES), :] = conv[
                0, :, tile * LANES : (tile + 1) * LANES
            ].astype(F32)
    decay = [rates[n * TILES : (n + 1) * TILES, :] for n in range(STATE)]

    def steps(i, carried):
        carried = list(carried)
        for k in range(UNROLL):
            t = i * UNROLL + k
            at = pl.multiple_of(t * TILES, TILES)
            row = pl.multiple_of(t * 2 * STATE, 2 * STATE)
            dt = dts[pl.ds(at, TILES), :]
            drive = dt * us[pl.ds(at, TILES), :]
            sums = [None] * 4
            for n in range(STATE):
                carried[n] = (
                    jnp.exp2(dt * decay[n]) * carried[n] + drive * spread[pl.ds(row + n, 1), :]
                )
                term = carried[n] * spread[pl.ds(row + STATE + n, 1), :]
                sums[n % 4] = term if sums[n % 4] is None else sums[n % 4] + term
            dts[pl.ds(at, TILES), :] = (sums[0] + sums[1]) + (sums[2] + sums[3])
        return tuple(carried)

    carried = tuple(states[n * TILES : (n + 1) * TILES, :] for n in range(STATE))
    carried = lax.fori_loop(0, TURN // UNROLL, steps, carried)
    for n in range(STATE):
        states[n * TILES : (n + 1) * TILES, :] = carried[n]
    for part in range(STATE // 8):
        for tile in range(TILES):
            final[to, part * TILES + tile] = states[
                pl.ds(part * 8 * TILES + tile, 8, stride=TILES), :
            ].astype(BF16)
    for tile in range(TILES):
        cols = slice(tile * LANES, (tile + 1) * LANES)
        z = gate[0, :, cols].astype(F32)
        y = dts[pl.ds(tile, TURN, stride=TILES), :] + skip[:, cols] * conv[0, :, cols].astype(F32)
        gated[0, :, cols] = (y * silu(z)).astype(BF16)


def scan(routing, came, dt_weight, dt_bias, a_log, skip, conv, gate, fetched, hidden, base):
    own = base is None
    first = PER if own else 0
    blocks = RETURNED if own else STATE
    whole = lambda shape: pl.BlockSpec(shape, lambda i, r: (0,) * len(shape))
    ends = lambda at: pl.BlockSpec(
        (1, HEAD, INNER), lambda i, r: (r[ORDER + at + i], TURN // HEAD - 1, 0)
    )
    return pl.pallas_call(
        functools.partial(scan_kernel, own),
        grid_spec=pltpu.PrefetchScalarGridSpec(
            num_scalar_prefetch=1,
            grid=(PER,),
            in_specs=[
                pl.BlockSpec(memory_space=pl.ANY),
                whole((RANK, INNER)),
                whole((1, INNER)),
                whole((STATE, INNER)),
                whole((1, INNER)),
                pl.BlockSpec((1, TURN, INNER), lambda i, r: (first + i, 0, 0)),
                pl.BlockSpec((1, TURN, INNER), lambda i, r: (r[ORDER + first + i], 0, 0)),
                pl.BlockSpec(
                    (1, STATE, TILES, LANES),
                    lambda i, r: (r[HOLDER + first + i], r[SIDES + own], 0, 0),
                ),
                ends(PER),
                ends(0),
                pl.BlockSpec(memory_space=pl.ANY),
            ],
            out_specs=[
                pl.BlockSpec((1, TURN, INNER), lambda i, r: (r[ORDER + first + i], 0, 0)),
                whole((GROUPS, blocks, TILES, LANES)),
            ],
            scratch_shapes=[
                pltpu.VMEM((TURN * TILES, LANES), F32),
                pltpu.VMEM((TURN * TILES, LANES), F32),
                pltpu.VMEM((TURN * 2 * STATE, LANES), F32),
                pltpu.VMEM((STATE * TILES, LANES), F32),
                pltpu.VMEM((STATE * TILES, LANES), F32),
                pltpu.VMEM((DEPTH, SHARE + EDGES, WIDE), BF16),
                pltpu.SemaphoreType.DMA,
            ],
        ),
        out_shape=[
            jax.ShapeDtypeStruct((REQUESTS, TURN, INNER), BF16),
            jax.ShapeDtypeStruct((GROUPS, blocks, TILES, LANES), BF16),
        ],
        input_output_aliases={} if own else {11: 0},
        compiler_params=params(),
        cost_estimate=cost(15, 4 * 2**20),
        name="scan",
    )(routing, came, dt_weight, dt_bias, a_log, skip, conv, gate, fetched, hidden,
      hidden, skip if own else base)


def widen(came, wide, g, row):
    for part in range(STATE // 8):
        for tile in range(TILES):
            rows, cols = block_of(part, tile)
            wide[row, rows, cols] = came[g, part * TILES + tile].astype(F32)


def place_kernel(routing, came, ssm, conv, new_ssm, new_conv, inputs, sem):
    base = pltpu.make_async_copy(ssm, new_ssm, sem)
    base.start()
    for k in range(KEPT):
        rows_to_tiles(inputs, k * SLOTS * TILES, conv[k])

    def put(slot, g, first):
        for k in range(KEPT):
            row = pl.multiple_of((k * SLOTS + slot) * TILES, TILES)
            inputs[pl.ds(row, TILES), :] = came[g, first + k].astype(F32)

    def each(g, carry):
        slot = routing[OWN + g]
        other_slot = routing[OTHER + g]

        @pl.when(slot < SLOTS)
        def _():
            widen(came, new_ssm, g, slot)
            put(slot, g, STATE)

        @pl.when(other_slot < SLOTS)
        def _():
            put(other_slot, g, STATE + KEPT)

        return carry

    base.wait()
    lax.fori_loop(0, GROUPS, each, 0)
    for k in range(KEPT):
        for tile in range(TILES):
            new_conv[k, :, tile * LANES : (tile + 1) * LANES] = inputs[
                pl.ds(k * SLOTS * TILES + tile, SLOTS, stride=TILES), :
            ]


def place(routing, came, ssm, conv):
    rows = pl.BlockSpec((KEPT, SLOTS, INNER), lambda i, r: (0, 0, 0))
    return pl.pallas_call(
        place_kernel,
        grid_spec=pltpu.PrefetchScalarGridSpec(
            num_scalar_prefetch=1,
            grid=(1,),
            in_specs=[
                pl.BlockSpec((GROUPS, RETURNED, TILES, LANES), lambda i, r: (0, 0, 0, 0)),
                pl.BlockSpec(memory_space=pl.ANY),
                rows,
            ],
            out_specs=[pl.BlockSpec((SLOTS, STATE, INNER), lambda i, r: (0, 0, 0)), rows],
            scratch_shapes=[
                pltpu.VMEM((KEPT * SLOTS * TILES, LANES), F32),
                pltpu.SemaphoreType.DMA,
            ],
        ),
        out_shape=[
            jax.ShapeDtypeStruct((SLOTS, STATE, INNER), F32),
            jax.ShapeDtypeStruct((KEPT, SLOTS, INNER), F32),
        ],
        compiler_params=params(),
        cost_estimate=cost(6, 6 * 2**20),
        name="place",
    )(routing, came, ssm, conv)


def store_kernel(routing, came, ssm_in, new_ssm, states, wide, sem, sems):
    def copy(g):
        return pltpu.make_async_copy(wide.at[g], new_ssm.at[routing[OTHER + g]], sems.at[g])

    def begin(g, carry):
        @pl.when(routing[OTHER + g] < SLOTS)
        def _():
            widen(states, wide, g, g)
            copy(g).start()

        return carry

    def finish(g, carry):
        @pl.when(routing[OTHER + g] < SLOTS)
        def _():
            copy(g).wait()

        return carry

    arriving = pltpu.make_async_copy(came, states, sem)
    arriving.start()
    arriving.wait()
    lax.fori_loop(0, GROUPS, begin, 0)
    lax.fori_loop(0, GROUPS, finish, 0)


def store(routing, came, ssm):
    anywhere = pl.BlockSpec(memory_space=pl.ANY)
    return pl.pallas_call(
        store_kernel,
        grid_spec=pltpu.PrefetchScalarGridSpec(
            num_scalar_prefetch=1,
            grid=(1,),
            in_specs=[anywhere, anywhere],
            out_specs=anywhere,
            scratch_shapes=[
                pltpu.VMEM((GROUPS, STATE, TILES, LANES), BF16),
                pltpu.VMEM((GROUPS, STATE, INNER), F32),
                pltpu.SemaphoreType.DMA,
                pltpu.SemaphoreType.DMA((GROUPS,)),
            ],
        ),
        out_shape=jax.ShapeDtypeStruct((SLOTS, STATE, INNER), F32),
        input_output_aliases={2: 0},
        compiler_params=params(),
        cost_estimate=cost(2, 2 * 2**20),
        name="store",
    )(routing, came, ssm)


def exchange(values, axis):
    return lax.all_to_all(values, axis, split_axis=0, concat_axis=0, tiled=True)


def body(
    hidden_x,
    gate_z,
    conv_weight,
    conv_bias,
    x_weight,
    dt_weight,
    dt_bias,
    a_log,
    skip_gain,
    ssm_cache,
    conv_cache,
    holder_of,
    slot_of,
):
    conv_rows = jnp.swapaxes(conv_cache, 0, 1)
    bias = conv_bias.reshape(1, INNER)
    x_weight = x_weight.T
    routing, packed = pack(holder_of, slot_of, ssm_cache, conv_rows)
    fetched = exchange(packed, "dp")
    conv, sent, kept = convolve(routing, hidden_x, conv_weight, bias, x_weight)
    parts = (kept + lax.ppermute(sent, "core", SWAP).astype(F32)).astype(BF16)
    parts, fetched = lax.optimization_barrier((parts, fetched))
    parts = exchange(parts.reshape(DEPTH, SHARE, WIDE), "z")
    conv, edge_sent, edge = put_heads(
        routing, hidden_x, fetched, conv_weight, bias, x_weight, conv
    )
    normed = exchange(normalize(parts, edge, lax.ppermute(edge_sent, "core", SWAP)), "z")
    gated, came = None, []
    for values in (normed, lax.ppermute(normed, "core", SWAP)):
        gated, final = scan(
            routing,
            values,
            dt_weight,
            dt_bias.reshape(1, INNER),
            a_log,
            skip_gain.reshape(1, INNER),
            conv,
            gate_z,
            fetched,
            hidden_x,
            gated,
        )
        if came:
            came[0], final = lax.optimization_barrier((came[0], final))
        came.append(exchange(final, "dp"))
    new_ssm, new_conv = place(routing, came[0], ssm_cache, conv_rows)
    new_ssm = store(routing, came[1], new_ssm)
    return (gated, new_ssm, jnp.swapaxes(new_conv, 0, 1))


def solution(mesh):
    fine = Mesh(mesh.devices.reshape(GROUPS, DEPTH, CORES), ("dp", "z", "core"))
    tensor = ("z", "core")
    placed = (
        P("dp", None, tensor),
        P("dp", None, tensor),
        P(None, tensor),
        P(tensor),
        P(tensor, None),
        P(None, tensor),
        P(tensor),
        P(None, tensor),
        P(tensor),
        P("dp", None, tensor),
        P("dp", None, tensor),
        P(),
        P(),
    )
    return jax.shard_map(
        body,
        mesh=fine,
        in_specs=placed,
        out_specs=(P("dp", None, tensor),) * 3,
        check_vma=False,
    )
```

time: 161 us -> 154 us (0.957)
  blocking collectives: 0 us -> 24.9 us
  waiting for transfers between devices: 42.6 us -> 22.8 us
  local copies, waits for them, and re-layouts: 8.96 us -> 3.45 us
  starting transfers between devices: 36.6 us -> 32.3 us
  other arithmetic: 4.4 us -> 2.33 us
    all_to_all x0 -> x1, blocking collectives: none -> 24.9 us  [exchange(): return lax.all_to_all(values, axis, split_axis=0, concat_axis=0, tiled=True)]
    all_to_all x5 -> x4, waiting for transfers between devices: 38.9 us -> 19.1 us  [exchange(): return lax.all_to_all(values, axis, split_axis=0, concat_axis=0, tiled=True)]
    all_to_all x5 -> x4, starting transfers between devices: 36.5 us -> 32.2 us  [exchange(): return lax.all_to_all(values, axis, split_axis=0, concat_axis=0, tiled=True)]
    unnamed x15 -> x14, local copies, waits for them, and re-layouts: 5.19 us -> 3.45 us
  transfers between devices with their start and end apart: 8 -> 7, of which waited for: 6 -> 5; matrix products, arithmetic and copies ran while one was open for 2% -> 2% of each run, Pallas kernels for 35% -> 36%
where the time goes in v5:
time: 154 us; the launch traced here: 153 us
  Pallas kernels  66.2 us (43%)
  starting transfers between devices  32.3 us (21%)
  blocking collectives  24.9 us (16%)
  waiting for transfers between devices  22.8 us (15%)
  local copies, waits for them, and re-layouts  3.45 us (2%)
  other arithmetic  2.33 us (2%)
    pallas_call x2, Pallas kernels, scan(): pl.pallas_call(functools.partial(scan_kernel, own), grid_spec=pltpu.Prefe...  34.4 us
    all_to_all x4, starting transfers between devices, exchange(): return lax.all_to_all(values, axis, split_axis=0, concat_axis=0, tiled=True)  32.2 us
    all_to_all x1, blocking collectives, exchange(): return lax.all_to_all(values, axis, split_axis=0, concat_axis=0, tiled=True)  24.9 us
    all_to_all x4, waiting for transfers between devices, exchange(): return lax.all_to_all(values, axis, split_axis=0, concat_axis=0, tiled=True)  19.1 us
    pallas_call x1, Pallas kernels, convolve(): pl.pallas_call(conv_kernel, grid_spec=pltpu.PrefetchScalarGridSpec(num_sc...  10.2 us
    pallas_call x1, Pallas kernels, pack(): pl.pallas_call(pack_kernel, grid_spec=pltpu.PrefetchScalarGridSpec(num_sc...  6.01 us
    pallas_call x1, Pallas kernels, place(): pl.pallas_call(place_kernel, grid_spec=pltpu.PrefetchScalarGridSpec(num_s...  5.22 us
    pallas_call x1, Pallas kernels, put_heads(): pl.pallas_call(head_kernel, grid_spec=pltpu.PrefetchScalarGridSpec(num_sc...  4.92 us
  transfers between devices with their start and end apart: 7, of which 5 were waited for; matrix products, arithmetic and copies ran while one was open for 2% of the time, Pallas kernels for 36%

profile of v5, /device:TPU:8, one launch (start us, length us, event | category | flops | bytes accessed | tf_op | source)
XLA Modules:
  0.0 152.8 jit_solution(16788606905547354292)
XLA Ops:
  0.6 6.0 %pack.1 = (s32[64]{0:T(128)}, bf16[16,38,8,128]{3,2,1,0:T(8,128)(2,1)}) custom-call(s32[128]{0:T(128)} %holders.1, s32[128]{0:T(128)} %places.1, f32[32,16,1024]{2,1,0:T(8,128)} %ssm.3, f32[3,32,1024]{2,1,0:T(8,128)} %bitcast.9), custom_call_target="tpu_custom_call" | custom-call | flops 4000000000 | bytes 4194304 | tf_op jit(solution)/shard_map/pack/pallas_call | solution.py:135
  6.6 7.4 %all-to-all-start = ((bf16[16,38,8,128]{3,2,1,0:T(8,128)(2,1)}), bf16[16,38,8,128]{3,2,1,0:T(8,128)(2,1)S(1)}, u32[]{:S(2)}, u32[]{:S(2)}) async-start(bf16[16,38,8,128]{3,2,1,0:T(8,128)(2,1)} %get-tuple-element.24), calls=%async_computation | async-start | bytes 2490368 | tf_op jit(solution)/shard_map/all_to_all | solution.py:627
  14.1 10.2 %convolve.1 = (bf16[8,128,1024]{2,1,0:T(8,128)(2,1)}, bf16[4,128,640]{2,1,0:T(8,128)(2,1)}, f32[4,128,640]{2,1,0:T(8,128)}) custom-call(s32[64]{0:T(128)} %get-tuple-element.21.routing, bf16[8,128,1024]{2,1,0:T(8,128)(2,1)} %other_last.3, bf16[8,128,1024]{2,1,0:T(8,128)(2,1)} %other_last.3, f32[4,1024]{1,0:T(4,128)} %weight.3, f32[1,1024]{1,0:T(1,128)} %bitcast.11, ...), custom_call_target="tpu_custom_call" | custom-call | flops 8000000000 | bytes 8388608 | tf_op jit(solution)/shard_map/convolve/pallas_call | solution.py:206
  24.3 0.0 collective-permute-start
  24.3 2.3 %collective-permute-done = bf16[4,128,640]{2,1,0:T(8,128)(2,1)S(1)} collective-permute-done((bf16[4,128,640]{2,1,0:T(8,128)(2,1)}, bf16[4,128,640]{2,1,0:T(8,128)(2,1)S(1)}, u32[]{:S(2)}, u32[]{:S(2)}) %collective-permute-start) | collective-permute-done | bytes 655392 | tf_op jit(solution)/shard_map/ppermute | solution.py:651
  26.6 2.3 %add_convert_fusion = bf16[4,128,640]{2,1,0:T(8,128)(2,1)} fusion(f32[4,128,640]{2,1,0:T(8,128)} %get-tuple-element.22, bf16[4,128,640]{2,1,0:T(8,128)(2,1)S(1)} %collective-permute-done), kind=kLoop, calls=%fused_computation | loop fusion | flops 983040 | bytes 2621440 | tf_op jit(solution)/shard_map/convert_element_type | solution.py:651
  28.9 3.8 %all-to-all-done.fetched.start = bf16[16,38,8,128]{3,2,1,0:T(8,128)(2,1)S(1)} async-done(((bf16[16,38,8,128]{3,2,1,0:T(8,128)(2,1)}), bf16[16,38,8,128]{3,2,1,0:T(8,128)(2,1)S(1)}, u32[]{:S(2)}, u32[]{:S(2)}) %all-to-all-start) | async-done | bytes 1245216 | tf_op jit(solution)/shard_map/all_to_all | solution.py:627
  32.8 0.0 copy-start
  32.8 8.5 %all-to-all-start.1 = ((bf16[8,64,640]{2,1,0:T(8,128)(2,1)}), bf16[8,64,640]{2,1,0:T(8,128)(2,1)S(1)}, u32[]{:S(2)}, u32[]{:S(2)}) async-start(bf16[8,64,640]{2,1,0:T(8,128)(2,1)} %bitcast.3), calls=%async_computation.1 | async-start | bytes 1310720 | tf_op jit(solution)/shard_map/all_to_all | solution.py:627
  41.2 0.0 copy-done
  41.3 4.9 %put_heads.1 = (bf16[8,128,1024]{2,1,0:T(8,128)(2,1)}, bf16[16,640]{1,0:T(8,128)(2,1)}, f32[16,640]{1,0:T(8,128)}) custom-call(s32[64]{0:T(128)} %get-tuple-element.21.routing, bf16[8,128,1024]{2,1,0:T(8,128)(2,1)} %other_last.3, bf16[16,38,8,128]{3,2,1,0:T(8,128)(2,1)} %copy-done, f32[4,1024]{1,0:T(4,128)} %weight.3, ...), custom_call_target="tpu_custom_call", output_to_operand_aliasing={{0}: (6, {})} | custom-call | flops 4000000000 | bytes 4194304 | tf_op jit(solution)/shard_map/put_heads/pallas_call | solution.py:280
  46.2 0.1 collective-permute-start.1
  46.3 1.4 collective-permute-done.1.edge_came
  47.7 0.0 copy-start.6
  47.7 11.1 %all-to-all-done.1.parts = bf16[8,64,640]{2,1,0:T(8,128)(2,1)S(1)} async-done(((bf16[8,64,640]{2,1,0:T(8,128)(2,1)}), bf16[8,64,640]{2,1,0:T(8,128)(2,1)S(1)}, u32[]{:S(2)}, u32[]{:S(2)}) %all-to-all-start.1) | async-done | bytes 655392 | tf_op jit(solution)/shard_map/all_to_all | solution.py:627
  58.7 0.0 copy-start.3
  58.7 0.0 copy-done.6
  58.7 0.8 copy-done.3
  59.6 2.8 %normalize.1 = bf16[8,80,640]{2,1,0:T(8,128)(2,1)} custom-call(bf16[8,64,640]{2,1,0:T(8,128)(2,1)} %copy-done.3, f32[16,640]{1,0:T(8,128)} %get-tuple-element.28.edge, bf16[16,640]{1,0:T(8,128)(2,1)} %copy-done.6), custom_call_target="tpu_custom_call" | custom-call | flops 1500000000 | bytes 1048576 | tf_op jit(solution)/shard_map/normalize/pallas_call | solution.py:345
  62.4 24.9 %all_to_all.25.came = bf16[8,80,640]{2,1,0:T(8,128)(2,1)S(1)} all-to-all(bf16[8,80,640]{2,1,0:T(8,128)(2,1)} %normalize.1), channel_id=1, replica_groups=mesh['dp'=16,'z'=8,'core'=2] {'z'}, dimensions={0} | all-to-all | bytes 1638400 | tf_op jit(solution)/shard_map/all_to_all | solution.py:627
  87.3 0.0 copy-start.1
  87.3 0.0 collective-permute-start.2
  87.3 0.9 copy-done.1
  88.2 17.2 %scan.2 = (bf16[8,128,1024]{2,1,0:T(8,128)(2,1)}, bf16[16,22,8,128]{3,2,1,0:T(8,128)(2,1)}) custom-call(s32[64]{0:T(128)} %get-tuple-element.21.routing, bf16[8,80,640]{2,1,0:T(8,128)(2,1)} %copy-done.1, bf16[512,1024]{1,0:T(8,128)(2,1)} %dt_weight.3, f32[1,1024]{1,0:T(1,128)} %bitcast.13, f32[16,1024]{1,0:T(8,128)} %a_log.3, f32[1,1024]{1,0:T(1,128)} %bitcast.15, ...), custom_call_target="tpu_custom_call" | custom-call | flops 15000000512 | bytes 4194304 | tf_op jit(solution)/shard_map/scan/pallas_call | solution.py:459
  105.4 9.1 %all-to-all-start.3 = ((bf16[16,22,8,128]{3,2,1,0:T(8,128)(2,1)}), bf16[16,22,8,128]{3,2,1,0:T(8,128)(2,1)S(1)}, u32[]{:S(2)}, u32[]{:S(2)}) async-start(bf16[16,22,8,128]{3,2,1,0:T(8,128)(2,1)} %get-tuple-element.33), calls=%async_computation.3 | async-start | bytes 1441792 | tf_op jit(solution)/shard_map/all_to_all | solution.py:627
  114.5 0.0 collective-permute-done.2.came
  114.5 0.0 copy-start.5
  114.5 0.9 copy-done.5
  115.4 17.2 %scan.3 = (bf16[8,128,1024]{2,1,0:T(8,128)(2,1)}, bf16[16,16,8,128]{3,2,1,0:T(8,128)(2,1)}) custom-call(s32[64]{0:T(128)} %get-tuple-element.21.routing, bf16[8,80,640]{2,1,0:T(8,128)(2,1)} %copy-done.5, bf16[512,1024]{1,0:T(8,128)(2,1)} %dt_weight.3, f32[1,1024]{1,0:T(1,128)} %bitcast.14, f32[16,1024]{1,0:T(8,128)} %a_log.3, ...), custom_call_target="tpu_custom_call", output_to_operand_aliasing={{0}: (11, {})} | custom-call | flops 15000000512 | bytes 4194304 | tf_op jit(solution)/shard_map/scan/pallas_call | solution.py:459
  132.6 0.0 all-to-all-done.3.came
  132.6 0.0 copy-start.2
  132.6 7.2 %all-to-all-start.4 = ((bf16[16,16,8,128]{3,2,1,0:T(8,128)(2,1)}), bf16[16,16,8,128]{3,2,1,0:T(8,128)(2,1)S(1)}, u32[]{:S(2)}, u32[]{:S(2)}) async-start(bf16[16,16,8,128]{3,2,1,0:T(8,128)(2,1)} %get-tuple-element.35), calls=%async_computation.4 | async-start | bytes 1048576 | tf_op jit(solution)/shard_map/all_to_all | solution.py:627
  139.9 0.0 copy-done.2
  139.9 5.2 %place.1 = (f32[32,16,1024]{2,1,0:T(8,128)}, f32[3,32,1024]{2,1,0:T(8,128)}) custom-call(s32[64]{0:T(128)} %get-tuple-element.21.routing, bf16[16,22,8,128]{3,2,1,0:T(8,128)(2,1)} %copy-done.2, f32[32,16,1024]{2,1,0:T(8,128)} %ssm.3, f32[3,32,1024]{2,1,0:T(8,128)} %bitcast.10), custom_call_target="tpu_custom_call" | custom-call | flops 6000000000 | bytes 6291456 | tf_op jit(solution)/shard_map/place/pallas_call | solution.py:550
  145.1 4.2 %all-to-all-done.4.came = bf16[16,16,8,128]{3,2,1,0:T(8,128)(2,1)S(1)} async-done(((bf16[16,16,8,128]{3,2,1,0:T(8,128)(2,1)}), bf16[16,16,8,128]{3,2,1,0:T(8,128)(2,1)S(1)}, u32[]{:S(2)}, u32[]{:S(2)}) %all-to-all-start.4) | async-done | bytes 524320 | tf_op jit(solution)/shard_map/all_to_all | solution.py:627
  149.3 0.0 copy-start.4
  149.3 0.8 copy-done.4
  150.1 2.7 %store.1 = f32[32,16,1024]{2,1,0:T(8,128)} custom-call(s32[64]{0:T(128)} %get-tuple-element.21.routing, bf16[16,16,8,128]{3,2,1,0:T(8,128)(2,1)} %copy-done.4, f32[32,16,1024]{2,1,0:T(8,128)} %get-tuple-element.37.ssm_in), custom_call_target="tpu_custom_call", output_to_operand_aliasing={{}: (2, {})} | custom-call | flops 2000000000 | bytes 2097152 | tf_op jit(solution)/shard_map/store/pallas_call | solution.py:604
Async XLA Ops:
  6.6 26.1 %all-to-all-start = ((bf16[16,38,8,128]{3,2,1,0:T(8,128)(2,1)}), bf16[16,38,8,128]{3,2,1,0:T(8,128)(2,1)S(1)}, u32[]{:S(2)}, u32[]{:S(2)}) async-start(bf16[16,38,8,128]{3,2,1,0:T(8,128)(2,1)} %get-tuple-element.24), calls=%async_computation | async-start | bytes 2490368 | tf_op jit(solution)/shard_map/all_to_all | solution.py:627
  24.3 2.3 %collective-permute-start = (bf16[4,128,640]{2,1,0:T(8,128)(2,1)}, bf16[4,128,640]{2,1,0:T(8,128)(2,1)S(1)}, u32[]{:S(2)}, u32[]{:S(2)}) collective-permute-start(bf16[4,128,640]{2,1,0:T(8,128)(2,1)} %get-tuple-element.23), channel_id=1, source_target_pairs={{0,1},{1,0},{2,3},{3,2},{4,5},{5,4},{6,7},{7,6},{8,9},{9,8},{10,11... | collective-permute-start | bytes 1966088 | tf_op jit(solution)/shard_map/ppermute | solution.py:651
  32.8 8.5 %copy-start = (bf16[16,38,8,128]{3,2,1,0:T(8,128)(2,1)}, bf16[16,38,8,128]{3,2,1,0:T(8,128)(2,1)S(1)}, u32[]{:S(2)}) copy-start(bf16[16,38,8,128]{3,2,1,0:T(8,128)(2,1)S(1)} %all-to-all-done.fetched.start) | copy-start | bytes 3735556
  32.8 26.0 %all-to-all-start.1 = ((bf16[8,64,640]{2,1,0:T(8,128)(2,1)}), bf16[8,64,640]{2,1,0:T(8,128)(2,1)S(1)}, u32[]{:S(2)}, u32[]{:S(2)}) async-start(bf16[8,64,640]{2,1,0:T(8,128)(2,1)} %bitcast.3), calls=%async_computation.1 | async-start | bytes 1310720 | tf_op jit(solution)/shard_map/all_to_all | solution.py:627
  46.2 1.5 collective-permute-start.1
  47.7 11.1 %copy-start.6 = (bf16[16,640]{1,0:T(8,128)(2,1)}, bf16[16,640]{1,0:T(8,128)(2,1)S(1)}, u32[]{:S(2)}) copy-start(bf16[16,640]{1,0:T(8,128)(2,1)S(1)} %collective-permute-done.1.edge_came) | copy-start | bytes 61444
  58.7 0.8 copy-start.3
  87.3 0.9 copy-start.1
  87.3 27.2 %collective-permute-start.2 = (bf16[8,80,640]{2,1,0:T(8,128)(2,1)S(1)}, bf16[8,80,640]{2,1,0:T(8,128)(2,1)S(1)}, u32[]{:S(2)}, u32[]{:S(2)}) collective-permute-start(bf16[8,80,640]{2,1,0:T(8,128)(2,1)S(1)} %all_to_all.25.came), channel_id=1, source_target_pairs={{0,1},{1,0},{2,3},{3,2},{4,5},{5,4},{6,7},{7,6},{8,9},{9,8},{10,11... | collective-permute-start | bytes 2457608 | tf_op jit(solution)/shard_map/ppermute | solution.py:659
  105.4 27.2 %all-to-all-start.3 = ((bf16[16,22,8,128]{3,2,1,0:T(8,128)(2,1)}), bf16[16,22,8,128]{3,2,1,0:T(8,128)(2,1)S(1)}, u32[]{:S(2)}, u32[]{:S(2)}) async-start(bf16[16,22,8,128]{3,2,1,0:T(8,128)(2,1)} %get-tuple-element.33), calls=%async_computation.3 | async-start | bytes 1441792 | tf_op jit(solution)/shard_map/all_to_all | solution.py:627
  114.5 0.9 copy-start.5
  132.6 7.3 %copy-start.2 = (bf16[16,22,8,128]{3,2,1,0:T(8,128)(2,1)}, bf16[16,22,8,128]{3,2,1,0:T(8,128)(2,1)S(1)}, u32[]{:S(2)}) copy-start(bf16[16,22,8,128]{3,2,1,0:T(8,128)(2,1)S(1)} %all-to-all-done.3.came) | copy-start | bytes 2162692
  132.6 16.7 %all-to-all-start.4 = ((bf16[16,16,8,128]{3,2,1,0:T(8,128)(2,1)}), bf16[16,16,8,128]{3,2,1,0:T(8,128)(2,1)S(1)}, u32[]{:S(2)}, u32[]{:S(2)}) async-start(bf16[16,16,8,128]{3,2,1,0:T(8,128)(2,1)} %get-tuple-element.35), calls=%async_computation.4 | async-start | bytes 1048576 | tf_op jit(solution)/shard_map/all_to_all | solution.py:627
  149.3 0.8 copy-start.4

commit v6 on v5

--- a/solution.py
+++ b/solution.py
@@ -20,7 +20,7 @@
 RANK = 512
 STATE = 16
 USED = RANK + 2 * STATE
-WIDE = 640
+QUARTERS = RANK // 128
 SLOTS = 32
 KEPT = 3
 DEPTH = 8
@@ -30,6 +30,13 @@
 EDGE = 4
 EDGES = PER * EDGE
 PAIR = 2
+SPANS = TURN // SHARE
+
+VECTORS = SHARE * QUARTERS
+GROUP = 16
+SUMMED = VECTORS + GROUP
+EDGED = EDGES * QUARTERS
+GATHERED = SUMMED + EDGED
 
 ORDER, HOLDER, OWN, OTHER, SIDES, ROUTING = 0, 8, 16, 32, 48, 64
 FETCHED = CHUNKS * (STATE + KEPT)
@@ -187,18 +194,26 @@
                 first = 8 - KEPT + tap
                 total = total + rows[first : first + TURN, cols] * weight[tap : tap + 1, cols]
             conv_out[which, :, cols] = silu(total).astype(BF16)
-    part = project(conv_out[...].reshape(PAIR * TURN, INNER), x_weight).reshape(PAIR, TURN, USED)
-    rest = jnp.zeros((PAIR, TURN, WIDE - USED), F32)
+    part = project(conv_out[...].reshape(PAIR * TURN, INNER), x_weight)
+
+    def put(out):
+        for span in range(PAIR * SPANS):
+            rows_of = part[span * SHARE : (span + 1) * SHARE]
+            at = (span // SPANS, span % SPANS)
+            for q in range(QUARTERS):
+                out[at[0], at[1], q * SHARE : (q + 1) * SHARE] = rows_of[
+                    :, q * LANES : (q + 1) * LANES
+                ].astype(out.dtype)
+            vectors = [rows_of[a * GROUP : (a + 1) * GROUP, RANK:] for a in range(SHARE // GROUP)]
+            out[at[0], at[1], VECTORS:] = jnp.concatenate(vectors, axis=1).astype(out.dtype)
 
     @pl.when(step < PER // PAIR)
     def _():
-        sent[:, :, :USED] = part.astype(BF16)
-        sent[:, :, USED:] = rest.astype(BF16)
+        put(sent)
 
     @pl.when(step >= PER // PAIR)
     def _():
-        kept[:, :, :USED] = part
-        kept[:, :, USED:] = rest
+        put(kept)
 
 
 def convolve(routing, hidden, weight, bias, x_weight):
@@ -217,15 +232,19 @@
             ],
             out_specs=[
                 pl.BlockSpec((PAIR, TURN, INNER), lambda i, r: (i, 0, 0)),
-                pl.BlockSpec((PAIR, TURN, WIDE), lambda i, r: (jnp.minimum(i, half - 1), 0, 0)),
-                pl.BlockSpec((PAIR, TURN, WIDE), lambda i, r: (jnp.maximum(i - half, 0), 0, 0)),
+                pl.BlockSpec(
+                    (PAIR, SPANS, SUMMED, LANES), lambda i, r: (jnp.minimum(i, half - 1), 0, 0, 0)
+                ),
+                pl.BlockSpec(
+                    (PAIR, SPANS, SUMMED, LANES), lambda i, r: (jnp.maximum(i - half, 0), 0, 0, 0)
+                ),
             ],
             scratch_shapes=[pltpu.VMEM((8 + TURN, INNER), F32)],
         ),
         out_shape=[
             jax.ShapeDtypeStruct((REQUESTS, TURN, INNER), BF16),
-            jax.ShapeDtypeStruct((PER, TURN, WIDE), BF16),
-            jax.ShapeDtypeStruct((PER, TURN, WIDE), F32),
+            jax.ShapeDtypeStruct((PER, SPANS, SUMMED, LANES), BF16),
+            jax.ShapeDtypeStruct((PER, SPANS, SUMMED, LANES), F32),
         ],
         compiler_params=params(),
         cost_estimate=cost(8, 8 * 2**20),
@@ -235,7 +254,7 @@
 
 def head_kernel(
     routing, hidden, fetched, weight, bias, x_weight, conv_in,
-    conv_out, sent, kept, starts, rows, tiles, head, sems, start_sems,
+    conv_out, sent, kept, starts, rows, tiles, head, edges, sems, start_sems,
 ):
     arriving = []
     for i in range(REQUESTS):
@@ -264,19 +283,28 @@
         leaving.append(pltpu.make_async_copy(head.at[i], conv_out.at[i, :HEAD], sems.at[i]))
         leaving[i].start()
     part = project(head[...].reshape(REQUESTS * HEAD, INNER), x_weight)
-    part = part.reshape(REQUESTS, HEAD, USED)[:, :EDGE]
-    rest = jnp.zeros((EDGES, WIDE - USED), F32)
-    sent[:, :USED] = part[:PER].reshape(EDGES, USED).astype(BF16)
-    sent[:, USED:] = rest.astype(BF16)
-    kept[:, :USED] = part[PER:].reshape(EDGES, USED)
-    kept[:, USED:] = rest
+    for i in range(REQUESTS):
+        half, k = i // PER, i % PER
+        for q in range(QUARTERS):
+            at = q * EDGES + k * EDGE
+            edges[half, at : at + EDGE] = part[
+                i * HEAD : i * HEAD + EDGE, q * LANES : (q + 1) * LANES
+            ]
+        last = k * EDGE + KEPT
+        edges[half, last : last + 1] = jnp.concatenate(
+            [part[i * HEAD + j : i * HEAD + j + 1, RANK:] for j in range(KEPT)]
+            + [jnp.zeros((1, LANES - KEPT * 2 * STATE), F32)],
+            axis=1,
+        )
+    sent[...] = edges[0].astype(BF16)
+    kept[...] = edges[1]
     for one in leaving:
         one.wait()
 
 
 def put_heads(routing, hidden, fetched, weight, bias, x_weight, conv_out):
     anywhere = pl.BlockSpec(memory_space=pl.ANY)
-    edges = pl.BlockSpec((EDGES, WIDE), lambda i, r: (0, 0))
+    edges = pl.BlockSpec((EDGED, LANES), lambda i, r: (0, 0))
     return pl.pallas_call(
         head_kernel,
         grid_spec=pltpu.PrefetchScalarGridSpec(
@@ -296,14 +324,15 @@
                 pltpu.VMEM((8 + HEAD, INNER), F32),
                 pltpu.VMEM((KEPT * TILES, LANES), F32),
                 pltpu.VMEM((REQUESTS, HEAD, INNER), BF16),
+                pltpu.VMEM((CHUNKS, EDGED, LANES), F32),
                 pltpu.SemaphoreType.DMA((REQUESTS,)),
                 pltpu.SemaphoreType.DMA((REQUESTS,)),
             ],
         ),
         out_shape=[
             jax.ShapeDtypeStruct(conv_out.shape, conv_out.dtype),
-            jax.ShapeDtypeStruct((EDGES, WIDE), BF16),
-            jax.ShapeDtypeStruct((EDGES, WIDE), F32),
+            jax.ShapeDtypeStruct((EDGED, LANES), BF16),
+            jax.ShapeDtypeStruct((EDGED, LANES), F32),
         ],
         input_output_aliases={6: 0},
         compiler_params=params(),
@@ -312,19 +341,19 @@
     )(routing, hidden, fetched, weight, bias, x_weight, conv_out)
 
 
-def norm(total):
-    rank = total[:, :RANK]
-    inject = total[:, RANK : RANK + STATE]
-    readout = total[:, RANK + STATE : USED]
-    rank = rank * lax.rsqrt(jnp.mean(rank * rank, axis=1, keepdims=True) + EPSILON)
-    inject = inject * lax.rsqrt(
-        jnp.maximum(jnp.mean(inject * inject, axis=1, keepdims=True), NORM_FLOOR)
-    )
-    readout = readout * lax.rsqrt(
-        jnp.maximum(jnp.mean(readout * readout, axis=1, keepdims=True), NORM_FLOOR)
-    )
-    rest = jnp.zeros((total.shape[0], WIDE - USED), F32)
-    return jnp.concatenate([rank, inject, readout, rest], axis=1)
+def norm_rank(quarters):
+    square = sum(jnp.sum(q * q, axis=1, keepdims=True) for q in quarters)
+    scale = lax.rsqrt(square * (1.0 / RANK) + EPSILON)
+    return [q * scale for q in quarters]
+
+
+def norm_vectors(values):
+    parts = []
+    for first in range(0, values.shape[1], STATE):
+        one = values[:, first : first + STATE]
+        mean = jnp.mean(one * one, axis=1, keepdims=True)
+        parts.append(one * lax.rsqrt(jnp.maximum(mean, NORM_FLOOR)))
+    return jnp.concatenate(parts, axis=1)
 
 
 def norm_kernel(parts, edge, edge_came, out, came, sem):
@@ -333,12 +362,16 @@
     total = parts[0].astype(F32)
     for k in range(1, DEPTH):
         total = total + parts[k].astype(F32)
-    joined = norm(total).astype(BF16)
+    ranks = norm_rank([total[q * SHARE : (q + 1) * SHARE] for q in range(QUARTERS)])
+    ranks = [q.astype(BF16) for q in ranks]
+    vectors = norm_vectors(total[VECTORS:]).astype(BF16)
     arriving.wait()
     edges = (edge[...] + came[...].astype(F32)).astype(BF16)
     for k in range(DEPTH):
-        out[k, :SHARE] = joined
-        out[k, SHARE:] = edges
+        for q in range(QUARTERS):
+            out[k, q * SHARE : (q + 1) * SHARE] = ranks[q]
+        out[k, VECTORS:SUMMED] = vectors
+        out[k, SUMMED:] = edges
 
 
 def normalize(parts, edge, edge_came):
@@ -349,8 +382,8 @@
             pl.BlockSpec(memory_space=pltpu.VMEM),
             pl.BlockSpec(memory_space=pl.ANY),
         ],
-        scratch_shapes=[pltpu.VMEM((EDGES, WIDE), BF16), pltpu.SemaphoreType.DMA],
-        out_shape=jax.ShapeDtypeStruct((DEPTH, SHARE + EDGES, WIDE), BF16),
+        scratch_shapes=[pltpu.VMEM((EDGED, LANES), BF16), pltpu.SemaphoreType.DMA],
+        out_shape=jax.ShapeDtypeStruct((DEPTH, GATHERED, LANES), BF16),
         compiler_params=params(),
         cost_estimate=cost(1.5, 2**20),
         name="normalize",
@@ -370,24 +403,48 @@
         arriving.start()
         rows_to_tiles(rates, 0, -LOG2_E * jnp.exp(a_log[...]))
         arriving.wait()
-        total = shares[0, SHARE:].astype(F32)
+        total = shares[0, SUMMED:].astype(F32)
         for k in range(1, DEPTH):
-            total = total + shares[k, SHARE:].astype(F32)
-        total = norm(total)
-        edge = lax.broadcasted_iota(jnp.int32, (HEAD, WIDE), 0) < KEPT
-        rest = jnp.zeros((HEAD - EDGE, WIDE), F32)
+            total = total + shares[k, SUMMED:].astype(F32)
+        quarters = [total[q * EDGES : (q + 1) * EDGES] for q in range(QUARTERS)]
+        row = lax.broadcasted_iota(jnp.int32, (GROUP, LANES), 0) < KEPT
+        lane = lax.broadcasted_iota(jnp.int32, (GROUP, LANES), 1) < 2 * STATE
+
+        def patch(at, first, values, where):
+            old = shares[at, first : first + GROUP].astype(F32)
+            shares[at, first : first + GROUP] = jnp.where(where, values, old).astype(BF16)
+
+        below = jnp.zeros((GROUP - EDGE, LANES), F32)
+        for q, values in enumerate(norm_rank(quarters)):
+            for k in range(PER):
+                values_of = jnp.concatenate([values[k * EDGE : (k + 1) * EDGE], below], axis=0)
+                patch(k * SPANS, q * SHARE, values_of, row)
+        beside = jnp.zeros((KEPT, LANES - 2 * STATE), F32)
+        below = jnp.zeros((GROUP - KEPT, LANES), F32)
         for k in range(PER):
-            at = k * (DEPTH // PER)
-            first = jnp.concatenate([total[k * EDGE : (k + 1) * EDGE], rest], axis=0)
-            shares[at, :HEAD] = jnp.where(edge, first, shares[at, :HEAD].astype(F32)).astype(BF16)
-
-    span = DEPTH // PER
-    normed = shares[pl.ds(step * span, span), :SHARE].reshape(TURN, WIDE)
-    columns = normed[:, RANK:].astype(F32).T[: 2 * STATE]
-    for t in range(TURN):
-        spread[t * 2 * STATE : (t + 1) * 2 * STATE, :] = jnp.broadcast_to(
-            columns[:, t : t + 1], (2 * STATE, LANES)
+            last = k * EDGE + KEPT
+            flat = norm_vectors(quarters[0][last : last + 1, : KEPT * 2 * STATE])
+            lines = [flat[:, j * 2 * STATE : (j + 1) * 2 * STATE] for j in range(KEPT)]
+            values_of = jnp.concatenate([jnp.concatenate(lines, axis=0), beside], axis=1)
+            values_of = jnp.concatenate([values_of, below], axis=0)
+            patch(k * SPANS, VECTORS, values_of, row & lane)
+
+    ranks = []
+    for span in range(SPANS):
+        at = step * SPANS + span
+        ranks.append(
+            jnp.concatenate(
+                [shares[at, q * SHARE : (q + 1) * SHARE] for q in range(QUARTERS)], axis=1
+            )
         )
+        columns = shares[at, VECTORS:SUMMED].astype(F32).T
+        for k in range(SHARE):
+            a, t = k // GROUP, span * SHARE + k
+            spread[t * 2 * STATE : (t + 1) * 2 * STATE, :] = jnp.broadcast_to(
+                columns[a * 2 * STATE : (a + 1) * 2 * STATE, k % GROUP : k % GROUP + 1],
+                (2 * STATE, LANES),
+            )
+    rank = jnp.concatenate(ranks, axis=0)
     if own:
         for which, (rows, at) in enumerate(((last, to), (other_last, routing[HOLDER + step]))):
             rows_to_tiles(states, 0, rows[0].astype(F32)[HEAD - KEPT :, :])
@@ -400,7 +457,6 @@
             states[pl.ds(part * 8 * TILES + tile, 8, stride=TILES), :] = start[
                 0, part * TILES + tile
             ].astype(F32)
-    rank = normed[:, :RANK]
     pair = 2 * LANES
     for block in range(INNER // pair):
         cols = slice(block * pair, (block + 1) * pair)
@@ -487,7 +543,7 @@
                 pltpu.VMEM((TURN * 2 * STATE, LANES), F32),
                 pltpu.VMEM((STATE * TILES, LANES), F32),
                 pltpu.VMEM((STATE * TILES, LANES), F32),
-                pltpu.VMEM((DEPTH, SHARE + EDGES, WIDE), BF16),
+                pltpu.VMEM((DEPTH, GATHERED, LANES), BF16),
                 pltpu.SemaphoreType.DMA,
             ],
         ),
@@ -650,7 +706,7 @@
     conv, sent, kept = convolve(routing, hidden_x, conv_weight, bias, x_weight)
     parts = (kept + lax.ppermute(sent, "core", SWAP).astype(F32)).astype(BF16)
     parts, fetched = lax.optimization_barrier((parts, fetched))
-    parts = exchange(parts.reshape(DEPTH, SHARE, WIDE), "z")
+    parts = exchange(parts.reshape(DEPTH, SUMMED, LANES), "z")
     conv, edge_sent, edge = put_heads(
         routing, hidden_x, fetched, conv_weight, bias, x_weight, conv
     )

time: 154 us -> 149 us (0.968)
  blocking collectives: 24.9 us -> 20.8 us
  waiting for transfers between devices: 22.8 us -> 20.6 us
    all_to_all x1, blocking collectives: 24.9 us -> 20.8 us  [exchange(): return lax.all_to_all(values, axis, split_axis=0, concat_axis=0, tiled=True)]
    all_to_all x4, waiting for transfers between devices: 19.1 us -> 17.1 us  [exchange(): return lax.all_to_all(values, axis, split_axis=0, concat_axis=0, tiled=True)]
  transfers between devices with their start and end apart: 7 -> 7, of which waited for: 5 -> 5; matrix products, arithmetic and copies ran while one was open for 2% -> 1% of each run, Pallas kernels for 36% -> 37%
where the time goes in v6:
time: 149 us; the launch traced here: 147 us
  Pallas kernels  66.5 us (45%)
  starting transfers between devices  33.3 us (22%)
  blocking collectives  20.8 us (14%)
  waiting for transfers between devices  20.6 us (14%)
  local copies, waits for them, and re-layouts  3.29 us (2%)
  other arithmetic  2.16 us (1%)
    pallas_call x2, Pallas kernels, scan(): pl.pallas_call(functools.partial(scan_kernel, own), grid_spec=pltpu.Prefe...  34.6 us
    all_to_all x4, starting transfers between devices, exchange(): return lax.all_to_all(values, axis, split_axis=0, concat_axis=0, tiled=True)  33.2 us
    all_to_all x1, blocking collectives, exchange(): return lax.all_to_all(values, axis, split_axis=0, concat_axis=0, tiled=True)  20.8 us
    all_to_all x4, waiting for transfers between devices, exchange(): return lax.all_to_all(values, axis, split_axis=0, concat_axis=0, tiled=True)  17.1 us
    pallas_call x1, Pallas kernels, convolve(): pl.pallas_call(conv_kernel, grid_spec=pltpu.PrefetchScalarGridSpec(num_sc...  10.4 us
    pallas_call x1, Pallas kernels, pack(): pl.pallas_call(pack_kernel, grid_spec=pltpu.PrefetchScalarGridSpec(num_sc...  6.06 us
    pallas_call x1, Pallas kernels, place(): pl.pallas_call(place_kernel, grid_spec=pltpu.PrefetchScalarGridSpec(num_s...  5.21 us
    pallas_call x1, Pallas kernels, put_heads(): pl.pallas_call(head_kernel, grid_spec=pltpu.PrefetchScalarGridSpec(num_sc...  4.92 us
  transfers between devices with their start and end apart: 7, of which 5 were waited for; matrix products, arithmetic and copies ran while one was open for 1% of the time, Pallas kernels for 37%

profile of v6, /device:TPU:8, one launch (start us, length us, event | category | flops | bytes accessed | tf_op | source)
XLA Modules:
  0.0 147.4 jit_solution(7313961499305357533)
XLA Ops:
  0.6 6.1 %pack.1 = (s32[64]{0:T(128)}, bf16[16,38,8,128]{3,2,1,0:T(8,128)(2,1)}) custom-call(s32[128]{0:T(128)} %holders.1, s32[128]{0:T(128)} %places.1, f32[32,16,1024]{2,1,0:T(8,128)} %ssm.3, f32[3,32,1024]{2,1,0:T(8,128)} %bitcast.9), custom_call_target="tpu_custom_call" | custom-call | flops 4000000000 | bytes 4194304 | tf_op jit(solution)/shard_map/pack/pallas_call | solution.py:142
  6.7 7.7 %all-to-all-start = ((bf16[16,38,8,128]{3,2,1,0:T(8,128)(2,1)}), bf16[16,38,8,128]{3,2,1,0:T(8,128)(2,1)S(1)}, u32[]{:S(2)}, u32[]{:S(2)}) async-start(bf16[16,38,8,128]{3,2,1,0:T(8,128)(2,1)} %get-tuple-element.24), calls=%async_computation | async-start | bytes 2490368 | tf_op jit(solution)/shard_map/all_to_all | solution.py:683
  14.4 10.4 %convolve.1 = (bf16[8,128,1024]{2,1,0:T(8,128)(2,1)}, bf16[4,2,272,128]{3,2,1,0:T(8,128)(2,1)}, f32[4,2,272,128]{3,2,1,0:T(8,128)}) custom-call(s32[64]{0:T(128)} %get-tuple-element.21.routing, bf16[8,128,1024]{2,1,0:T(8,128)(2,1)} %other_last.3, bf16[8,128,1024]{2,1,0:T(8,128)(2,1)} %other_last.3, f32[4,1024]{1,0:T(4,128)} %weight.3, f32[1,1024]{1,0:T(1,128)} %bitcast.11, ...), custom_call_target="tpu_custom_call" | custom-call | flops 8000000000 | bytes 8388608 | tf_op jit(solution)/shard_map/convolve/pallas_call | solution.py:221
  24.8 0.0 collective-permute-start
  24.8 2.2 %collective-permute-done = bf16[4,2,272,128]{3,2,1,0:T(8,128)(2,1)S(1)} collective-permute-done((bf16[4,2,272,128]{3,2,1,0:T(8,128)(2,1)}, bf16[4,2,272,128]{3,2,1,0:T(8,128)(2,1)S(1)}, u32[]{:S(2)}, u32[]{:S(2)}) %collective-permute-start) | collective-permute-done | bytes 557088 | tf_op jit(solution)/shard_map/ppermute | solution.py:707
  26.9 2.2 %add_convert_fusion = bf16[4,2,272,128]{3,2,1,0:T(8,128)(2,1)} fusion(f32[4,2,272,128]{3,2,1,0:T(8,128)} %get-tuple-element.22, bf16[4,2,272,128]{3,2,1,0:T(8,128)(2,1)S(1)} %collective-permute-done), kind=kLoop, calls=%fused_computation | loop fusion | flops 835584 | bytes 2228224 | tf_op jit(solution)/shard_map/convert_element_type | solution.py:707
  29.1 4.0 %all-to-all-done.fetched.start = bf16[16,38,8,128]{3,2,1,0:T(8,128)(2,1)S(1)} async-done(((bf16[16,38,8,128]{3,2,1,0:T(8,128)(2,1)}), bf16[16,38,8,128]{3,2,1,0:T(8,128)(2,1)S(1)}, u32[]{:S(2)}, u32[]{:S(2)}) %all-to-all-start) | async-done | bytes 1245216 | tf_op jit(solution)/shard_map/all_to_all | solution.py:683
  33.0 0.0 copy-start
  33.0 8.5 %all-to-all-start.1 = ((bf16[8,272,128]{2,1,0:T(8,128)(2,1)}), bf16[8,272,128]{2,1,0:T(8,128)(2,1)S(1)}, u32[]{:S(2)}, u32[]{:S(2)}) async-start(bf16[8,272,128]{2,1,0:T(8,128)(2,1)} %bitcast.3), calls=%async_computation.1 | async-start | bytes 1114112 | tf_op jit(solution)/shard_map/all_to_all | solution.py:683
  41.5 0.0 copy-done
  41.5 4.9 %put_heads.1 = (bf16[8,128,1024]{2,1,0:T(8,128)(2,1)}, bf16[64,128]{1,0:T(8,128)(2,1)}, f32[64,128]{1,0:T(8,128)}) custom-call(s32[64]{0:T(128)} %get-tuple-element.21.routing, bf16[8,128,1024]{2,1,0:T(8,128)(2,1)} %other_last.3, bf16[16,38,8,128]{3,2,1,0:T(8,128)(2,1)} %copy-done, f32[4,1024]{1,0:T(4,128)} %weight.3, ...), custom_call_target="tpu_custom_call", output_to_operand_aliasing={{0}: (6, {})} | custom-call | flops 4000000000 | bytes 4194304 | tf_op jit(solution)/shard_map/put_heads/pallas_call | solution.py:308
  46.4 0.1 collective-permute-start.1
  46.5 1.4 collective-permute-done.1.edge_came
  47.9 0.0 copy-start.6
  47.9 8.9 %all-to-all-done.1.parts = bf16[8,272,128]{2,1,0:T(8,128)(2,1)S(1)} async-done(((bf16[8,272,128]{2,1,0:T(8,128)(2,1)}), bf16[8,272,128]{2,1,0:T(8,128)(2,1)S(1)}, u32[]{:S(2)}, u32[]{:S(2)}) %all-to-all-start.1) | async-done | bytes 557088 | tf_op jit(solution)/shard_map/all_to_all | solution.py:683
  56.9 0.0 copy-start.3
  56.9 0.0 copy-done.6
  56.9 0.8 copy-done.3
  57.7 2.7 %normalize.1 = bf16[8,336,128]{2,1,0:T(8,128)(2,1)} custom-call(bf16[8,272,128]{2,1,0:T(8,128)(2,1)} %copy-done.3, f32[64,128]{1,0:T(8,128)} %get-tuple-element.28.edge, bf16[64,128]{1,0:T(8,128)(2,1)} %copy-done.6), custom_call_target="tpu_custom_call" | custom-call | flops 1500000000 | bytes 1048576 | tf_op jit(solution)/shard_map/normalize/pallas_call | solution.py:378
  60.3 20.8 %all_to_all.25.came = bf16[8,336,128]{2,1,0:T(8,128)(2,1)S(1)} all-to-all(bf16[8,336,128]{2,1,0:T(8,128)(2,1)} %normalize.1), channel_id=1, replica_groups=mesh['dp'=16,'z'=8,'core'=2] {'z'}, dimensions={0} | all-to-all | bytes 1376256 | tf_op jit(solution)/shard_map/all_to_all | solution.py:683
  81.2 0.0 copy-start.2
  81.2 0.0 collective-permute-start.2
  81.2 0.8 copy-done.2
  82.0 17.3 %scan.2 = (bf16[8,128,1024]{2,1,0:T(8,128)(2,1)}, bf16[16,22,8,128]{3,2,1,0:T(8,128)(2,1)}) custom-call(s32[64]{0:T(128)} %get-tuple-element.21.routing, bf16[8,336,128]{2,1,0:T(8,128)(2,1)} %copy-done.2, bf16[512,1024]{1,0:T(8,128)(2,1)} %dt_weight.3, f32[1,1024]{1,0:T(1,128)} %bitcast.13, f32[16,1024]{1,0:T(8,128)} %a_log.3, f32[1,1024]{1,0:T(1,128)} %bitcast.15, ...), custom_call_target="tpu_custom_call" | custom-call | flops 15000000512 | bytes 4194304 | tf_op jit(solution)/shard_map/scan/pallas_call | solution.py:515
  99.3 9.9 %all-to-all-start.3 = ((bf16[16,22,8,128]{3,2,1,0:T(8,128)(2,1)}), bf16[16,22,8,128]{3,2,1,0:T(8,128)(2,1)S(1)}, u32[]{:S(2)}, u32[]{:S(2)}) async-start(bf16[16,22,8,128]{3,2,1,0:T(8,128)(2,1)} %get-tuple-element.33), calls=%async_computation.3 | async-start | bytes 1441792 | tf_op jit(solution)/shard_map/all_to_all | solution.py:683
  109.2 0.0 collective-permute-done.2.came
  109.2 0.0 copy-start.5
  109.2 0.8 copy-done.5
  110.1 17.3 %scan.3 = (bf16[8,128,1024]{2,1,0:T(8,128)(2,1)}, bf16[16,16,8,128]{3,2,1,0:T(8,128)(2,1)}) custom-call(s32[64]{0:T(128)} %get-tuple-element.21.routing, bf16[8,336,128]{2,1,0:T(8,128)(2,1)} %copy-done.5, bf16[512,1024]{1,0:T(8,128)(2,1)} %dt_weight.3, f32[1,1024]{1,0:T(1,128)} %bitcast.14, f32[16,1024]{1,0:T(8,128)} %a_log.3, ...), custom_call_target="tpu_custom_call", output_to_operand_aliasing={{0}: (11, {})} | custom-call | flops 15000000512 | bytes 4194304 | tf_op jit(solution)/shard_map/scan/pallas_call | solution.py:515
  127.3 0.0 all-to-all-done.3.came
  127.3 0.0 copy-start.1
  127.4 7.2 %all-to-all-start.4 = ((bf16[16,16,8,128]{3,2,1,0:T(8,128)(2,1)}), bf16[16,16,8,128]{3,2,1,0:T(8,128)(2,1)S(1)}, u32[]{:S(2)}, u32[]{:S(2)}) async-start(bf16[16,16,8,128]{3,2,1,0:T(8,128)(2,1)} %get-tuple-element.35), calls=%async_computation.4 | async-start | bytes 1048576 | tf_op jit(solution)/shard_map/all_to_all | solution.py:683
  134.6 0.0 copy-done.1
  134.6 5.2 %place.1 = (f32[32,16,1024]{2,1,0:T(8,128)}, f32[3,32,1024]{2,1,0:T(8,128)}) custom-call(s32[64]{0:T(128)} %get-tuple-element.21.routing, bf16[16,22,8,128]{3,2,1,0:T(8,128)(2,1)} %copy-done.1, f32[32,16,1024]{2,1,0:T(8,128)} %ssm.3, f32[3,32,1024]{2,1,0:T(8,128)} %bitcast.10), custom_call_target="tpu_custom_call" | custom-call | flops 6000000000 | bytes 6291456 | tf_op jit(solution)/shard_map/place/pallas_call | solution.py:606
  139.8 4.2 %all-to-all-done.4.came = bf16[16,16,8,128]{3,2,1,0:T(8,128)(2,1)S(1)} async-done(((bf16[16,16,8,128]{3,2,1,0:T(8,128)(2,1)}), bf16[16,16,8,128]{3,2,1,0:T(8,128)(2,1)S(1)}, u32[]{:S(2)}, u32[]{:S(2)}) %all-to-all-start.4) | async-done | bytes 524320 | tf_op jit(solution)/shard_map/all_to_all | solution.py:683
  144.0 0.0 copy-start.4
  144.0 0.8 copy-done.4
  144.8 2.6 %store.1 = f32[32,16,1024]{2,1,0:T(8,128)} custom-call(s32[64]{0:T(128)} %get-tuple-element.21.routing, bf16[16,16,8,128]{3,2,1,0:T(8,128)(2,1)} %copy-done.4, f32[32,16,1024]{2,1,0:T(8,128)} %get-tuple-element.37.ssm_in), custom_call_target="tpu_custom_call", output_to_operand_aliasing={{}: (2, {})} | custom-call | flops 2000000000 | bytes 2097152 | tf_op jit(solution)/shard_map/store/pallas_call | solution.py:660
Async XLA Ops:
  6.7 26.3 %all-to-all-start = ((bf16[16,38,8,128]{3,2,1,0:T(8,128)(2,1)}), bf16[16,38,8,128]{3,2,1,0:T(8,128)(2,1)S(1)}, u32[]{:S(2)}, u32[]{:S(2)}) async-start(bf16[16,38,8,128]{3,2,1,0:T(8,128)(2,1)} %get-tuple-element.24), calls=%async_computation | async-start | bytes 2490368 | tf_op jit(solution)/shard_map/all_to_all | solution.py:683
  24.8 2.2 %collective-permute-start = (bf16[4,2,272,128]{3,2,1,0:T(8,128)(2,1)}, bf16[4,2,272,128]{3,2,1,0:T(8,128)(2,1)S(1)}, u32[]{:S(2)}, u32[]{:S(2)}) collective-permute-start(bf16[4,2,272,128]{3,2,1,0:T(8,128)(2,1)} %get-tuple-element.23), channel_id=1, source_target_pairs={{0,1},{1,0},{2,3},{3,2},{4,5},{5,4},{6,7},{7,6},{8,9},{9,8},{10,11... | collective-permute-start | bytes 1671176 | tf_op jit(solution)/shard_map/ppermute | solution.py:707
  33.0 8.5 %copy-start = (bf16[16,38,8,128]{3,2,1,0:T(8,128)(2,1)}, bf16[16,38,8,128]{3,2,1,0:T(8,128)(2,1)S(1)}, u32[]{:S(2)}) copy-start(bf16[16,38,8,128]{3,2,1,0:T(8,128)(2,1)S(1)} %all-to-all-done.fetched.start) | copy-start | bytes 3735556
  33.0 23.8 %all-to-all-start.1 = ((bf16[8,272,128]{2,1,0:T(8,128)(2,1)}), bf16[8,272,128]{2,1,0:T(8,128)(2,1)S(1)}, u32[]{:S(2)}, u32[]{:S(2)}) async-start(bf16[8,272,128]{2,1,0:T(8,128)(2,1)} %bitcast.3), calls=%async_computation.1 | async-start | bytes 1114112 | tf_op jit(solution)/shard_map/all_to_all | solution.py:683
  46.4 1.5 %collective-permute-start.1 = (bf16[64,128]{1,0:T(8,128)(2,1)}, bf16[64,128]{1,0:T(8,128)(2,1)S(1)}, u32[]{:S(2)}, u32[]{:S(2)}) collective-permute-start(bf16[64,128]{1,0:T(8,128)(2,1)} %get-tuple-element.29), channel_id=1, source_target_pairs={{0,1},{1,0},{2,3},{3,2},{4,5},{5,4},{6,7},{7,6},{8,9},{9,8},{10,11... | collective-permute-start | bytes 49160 | tf_op jit(solution)/shard_map/ppermute | solution.py:713
  47.9 8.9 %copy-start.6 = (bf16[64,128]{1,0:T(8,128)(2,1)}, bf16[64,128]{1,0:T(8,128)(2,1)S(1)}, u32[]{:S(2)}) copy-start(bf16[64,128]{1,0:T(8,128)(2,1)S(1)} %collective-permute-done.1.edge_came) | copy-start | bytes 49156
  56.9 0.8 copy-start.3
  81.2 0.8 copy-start.2
  81.2 28.0 %collective-permute-start.2 = (bf16[8,336,128]{2,1,0:T(8,128)(2,1)S(1)}, bf16[8,336,128]{2,1,0:T(8,128)(2,1)S(1)}, u32[]{:S(2)}, u32[]{:S(2)}) collective-permute-start(bf16[8,336,128]{2,1,0:T(8,128)(2,1)S(1)} %all_to_all.25.came), channel_id=1, source_target_pairs={{0,1},{1,0},{2,3},{3,2},{4,5},{5,4},{6,7},{7,6},{8,9},{9,8},{10,11... | collective-permute-start | bytes 2064392 | tf_op jit(solution)/shard_map/ppermute | solution.py:715
  99.3 28.0 %all-to-all-start.3 = ((bf16[16,22,8,128]{3,2,1,0:T(8,128)(2,1)}), bf16[16,22,8,128]{3,2,1,0:T(8,128)(2,1)S(1)}, u32[]{:S(2)}, u32[]{:S(2)}) async-start(bf16[16,22,8,128]{3,2,1,0:T(8,128)(2,1)} %get-tuple-element.33), calls=%async_computation.3 | async-start | bytes 1441792 | tf_op jit(solution)/shard_map/all_to_all | solution.py:683
  109.2 0.8 copy-start.5
  127.3 7.3 %copy-start.1 = (bf16[16,22,8,128]{3,2,1,0:T(8,128)(2,1)}, bf16[16,22,8,128]{3,2,1,0:T(8,128)(2,1)S(1)}, u32[]{:S(2)}) copy-start(bf16[16,22,8,128]{3,2,1,0:T(8,128)(2,1)S(1)} %all-to-all-done.3.came) | copy-start | bytes 2162692
  127.4 16.6 %all-to-all-start.4 = ((bf16[16,16,8,128]{3,2,1,0:T(8,128)(2,1)}), bf16[16,16,8,128]{3,2,1,0:T(8,128)(2,1)S(1)}, u32[]{:S(2)}, u32[]{:S(2)}) async-start(bf16[16,16,8,128]{3,2,1,0:T(8,128)(2,1)} %get-tuple-element.35), calls=%async_computation.4 | async-start | bytes 1048576 | tf_op jit(solution)/shard_map/all_to_all | solution.py:683
  144.0 0.8 copy-start.4

commit v7 on v6

--- a/solution.py
+++ b/solution.py
@@ -50,8 +50,8 @@
 SWAP = [(0, 1), (1, 0)]
 
 
-def params():
-    return pltpu.CompilerParams(vmem_limit_bytes=56 * 2**20)
+def params(mib=56):
+    return pltpu.CompilerParams(vmem_limit_bytes=mib * 2**20)
 
 
 def cost(us, bytes_accessed):
@@ -72,10 +72,13 @@
 
 
 def pack_kernel(
-    holders, places, ssm, conv, routing, out, slots, ranks, states, inputs, packed, sems, out_sems
+    holders, places, ssm, conv, routing, out, slots, ranks, states, lines, inputs, packed, sems,
+    out_sems, lines_sem,
 ):
     me = lax.axis_index("dp")
     core = lax.axis_index("core")
+    arriving = pltpu.make_async_copy(conv, lines, lines_sem)
+    arriving.start()
 
     def copy(e):
         return pltpu.make_async_copy(ssm.at[slots[e]], states.at[e], sems.at[e])
@@ -96,8 +99,12 @@
                 found[c] = jnp.where(here & (rank[i] % CHUNKS == c), place, found[c])
             ranks[g * REQUESTS + i] = rank[i]
         for c in range(CHUNKS):
-            slots[g * CHUNKS + c] = jnp.maximum(found[c], 0)
-            copy(g * CHUNKS + c).start()
+            slots[g * CHUNKS + c] = found[c]
+
+            @pl.when(found[c] >= 0)
+            def _():
+                copy(g * CHUNKS + c).start()
+
         first = jnp.where(found[0] < 0, SLOTS, found[0])
         second = jnp.where(found[1] < 0, SLOTS, found[1])
         routing[OWN + g] = jnp.where(core == 0, first, second)
@@ -112,12 +119,15 @@
         routing[HOLDER + at] = holders[me * REQUESTS + i]
     routing[SIDES] = 1 - core
     routing[SIDES + 1] = core
+    arriving.wait()
     for k in range(KEPT):
-        rows_to_tiles(inputs, k * SLOTS * TILES, conv[k])
-
-    def finish(g, carry):
-        for c in range(CHUNKS):
-            e = g * CHUNKS + c
+        rows_to_tiles(inputs, k * SLOTS * TILES, lines[k])
+
+    def fill(g, c):
+        e = g * CHUNKS + c
+
+        @pl.when(slots[e] >= 0)
+        def _():
             for k in range(KEPT):
                 row = pl.multiple_of((k * SLOTS + slots[e]) * TILES, TILES)
                 packed[g, CHUNKS * STATE + c * KEPT + k] = inputs[pl.ds(row, TILES), :].astype(BF16)
@@ -126,6 +136,10 @@
                 for tile in range(TILES):
                     rows, cols = block_of(part, tile)
                     packed[g, c * STATE + part * TILES + tile] = states[e, rows, cols].astype(BF16)
+
+    def finish(g, carry):
+        for c in range(CHUNKS):
+            fill(g, c)
         pltpu.make_async_copy(packed.at[g], out.at[g], out_sems.at[g]).start()
         return carry
 
@@ -144,19 +158,18 @@
         grid_spec=pltpu.PrefetchScalarGridSpec(
             num_scalar_prefetch=2,
             grid=(1,),
-            in_specs=[
-                anywhere,
-                pl.BlockSpec((KEPT, SLOTS, INNER), lambda i, h, p: (0, 0, 0)),
-            ],
+            in_specs=[anywhere, anywhere],
             out_specs=[pl.BlockSpec(memory_space=pltpu.SMEM), anywhere],
             scratch_shapes=[
                 pltpu.SMEM((GROUPS * CHUNKS,), jnp.int32),
                 pltpu.SMEM((GROUPS * REQUESTS,), jnp.int32),
                 pltpu.VMEM((GROUPS * CHUNKS, STATE, INNER), F32),
+                pltpu.VMEM((KEPT, SLOTS, INNER), F32),
                 pltpu.VMEM((KEPT * SLOTS * TILES, LANES), F32),
                 pltpu.VMEM((GROUPS, FETCHED, TILES, LANES), BF16),
                 pltpu.SemaphoreType.DMA((GROUPS * CHUNKS,)),
                 pltpu.SemaphoreType.DMA((GROUPS,)),
+                pltpu.SemaphoreType.DMA,
             ],
         ),
         out_shape=[
@@ -384,7 +397,7 @@
         ],
         scratch_shapes=[pltpu.VMEM((EDGED, LANES), BF16), pltpu.SemaphoreType.DMA],
         out_shape=jax.ShapeDtypeStruct((DEPTH, GATHERED, LANES), BF16),
-        compiler_params=params(),
+        compiler_params=params(12),
         cost_estimate=cost(1.5, 2**20),
         name="normalize",
     )(parts, edge, edge_came)
@@ -552,7 +565,7 @@
             jax.ShapeDtypeStruct((GROUPS, blocks, TILES, LANES), BF16),
         ],
         input_output_aliases={} if own else {11: 0},
-        compiler_params=params(),
+        compiler_params=params(20 if own else 56),
         cost_estimate=cost(15, 4 * 2**20),
         name="scan",
     )(routing, came, dt_weight, dt_bias, a_log, skip, conv, gate, fetched, hidden,
@@ -623,7 +636,7 @@
             jax.ShapeDtypeStruct((SLOTS, STATE, INNER), F32),
             jax.ShapeDtypeStruct((KEPT, SLOTS, INNER), F32),
         ],
-        compiler_params=params(),
+        compiler_params=params(20),
         cost_estimate=cost(6, 6 * 2**20),
         name="place",
     )(routing, came, ssm, conv)
@@ -673,7 +686,7 @@
         ),
         out_shape=jax.ShapeDtypeStruct((SLOTS, STATE, INNER), F32),
         input_output_aliases={2: 0},
-        compiler_params=params(),
+        compiler_params=params(8),
         cost_estimate=cost(2, 2 * 2**20),
         name="store",
     )(routing, came, ssm)

time: 149 us -> 141 us (0.946)
  Pallas kernels: 66.5 us -> 56.6 us
  waiting for transfers between devices: 20.6 us -> 23.1 us
    pallas_call x1, Pallas kernels: 5.21 us -> 2.53 us  [place(): pl.pallas_call(place_kernel, grid_spec=pltpu.PrefetchScalarGridSpec(num_s...]
    pallas_call x2, Pallas kernels: 34.6 us -> 31.9 us  [scan(): pl.pallas_call(functools.partial(scan_kernel, own), grid_spec=pltpu.Prefe...]
    all_to_all x4, waiting for transfers between devices: 17.1 us -> 19.5 us  [exchange(): return lax.all_to_all(values, axis, split_axis=0, concat_axis=0, tiled=True)]
    pallas_call x1, Pallas kernels: 2.67 us -> 0.41 us  [normalize(): pl.pallas_call(norm_kernel, in_specs=[pl.BlockSpec(memory_space=pltpu.VME...]
    unnamed x14 -> x30, local copies, waits for them, and re-layouts: 3.29 us -> 4.23 us
  transfers between devices with their start and end apart: 7 -> 7, of which waited for: 5 -> 5; matrix products, arithmetic and copies ran while one was open for 1% -> 2% of each run, Pallas kernels for 37% -> 36%
where the time goes in v7:
time: 141 us; the launch traced here: 140 us
  Pallas kernels  56.6 us (40%)
  starting transfers between devices  32.9 us (23%)
  waiting for transfers between devices  23.1 us (16%)
  blocking collectives  20 us (14%)
  local copies, waits for them, and re-layouts  4.23 us (3%)
  other arithmetic  2.17 us (2%)
    all_to_all x4, starting transfers between devices, exchange(): return lax.all_to_all(values, axis, split_axis=0, concat_axis=0, tiled=True)  32.8 us
    pallas_call x2, Pallas kernels, scan(): pl.pallas_call(functools.partial(scan_kernel, own), grid_spec=pltpu.Prefe...  31.9 us
    all_to_all x1, blocking collectives, exchange(): return lax.all_to_all(values, axis, split_axis=0, concat_axis=0, tiled=True)  20 us
    all_to_all x4, waiting for transfers between devices, exchange(): return lax.all_to_all(values, axis, split_axis=0, concat_axis=0, tiled=True)  19.5 us
    pallas_call x1, Pallas kernels, convolve(): pl.pallas_call(conv_kernel, grid_spec=pltpu.PrefetchScalarGridSpec(num_sc...  10.4 us
    pallas_call x1, Pallas kernels, put_heads(): pl.pallas_call(head_kernel, grid_spec=pltpu.PrefetchScalarGridSpec(num_sc...  4.92 us
    pallas_call x1, Pallas kernels, pack(): pl.pallas_call(pack_kernel, grid_spec=pltpu.PrefetchScalarGridSpec(num_sc...  4.81 us
    unnamed x30, local copies, waits for them, and re-layouts  4.23 us
  transfers between devices with their start and end apart: 7, of which 5 were waited for; matrix products, arithmetic and copies ran while one was open for 2% of the time, Pallas kernels for 36%

profile of v7, /device:TPU:8, one launch (start us, length us, event | category | flops | bytes accessed | tf_op | source)
XLA Modules:
  0.0 139.9 jit_solution(6697878233433871359)
XLA Ops:
  0.6 4.8 %pack.1 = (s32[64]{0:T(128)}, bf16[16,38,8,128]{3,2,1,0:T(8,128)(2,1)}) custom-call(s32[128]{0:T(128)} %holders.1, s32[128]{0:T(128)} %places.1, f32[32,16,1024]{2,1,0:T(8,128)} %ssm.3, f32[3,32,1024]{2,1,0:T(8,128)} %bitcast.7), custom_call_target="tpu_custom_call" | custom-call | flops 4000000000 | bytes 4194304 | tf_op jit(solution)/shard_map/pack/pallas_call | solution.py:156
  5.5 7.2 %all-to-all-start = ((bf16[16,38,8,128]{3,2,1,0:T(8,128)(2,1)}), bf16[16,38,8,128]{3,2,1,0:T(8,128)(2,1)S(1)}, u32[]{:S(2)}, u32[]{:S(2)}) async-start(bf16[16,38,8,128]{3,2,1,0:T(8,128)(2,1)} %get-tuple-element.24), calls=%async_computation | async-start | bytes 2490368 | tf_op jit(solution)/shard_map/all_to_all | solution.py:696
  12.7 10.4 %convolve.1 = (bf16[8,128,1024]{2,1,0:T(8,128)(2,1)}, bf16[4,2,272,128]{3,2,1,0:T(8,128)(2,1)}, f32[4,2,272,128]{3,2,1,0:T(8,128)}) custom-call(s32[64]{0:T(128)} %get-tuple-element.21.routing, bf16[8,128,1024]{2,1,0:T(8,128)(2,1)} %other_last.3, bf16[8,128,1024]{2,1,0:T(8,128)(2,1)} %other_last.3, f32[4,1024]{1,0:T(4,128)} %weight.3, f32[1,1024]{1,0:T(1,128)} %bitcast.16, ...), custom_call_target="tpu_custom_call" | custom-call | flops 8000000000 | bytes 8388608 | tf_op jit(solution)/shard_map/convolve/pallas_call | solution.py:234
  23.1 0.0 collective-permute-start
  23.1 2.2 %collective-permute-done = bf16[4,2,272,128]{3,2,1,0:T(8,128)(2,1)S(1)} collective-permute-done((bf16[4,2,272,128]{3,2,1,0:T(8,128)(2,1)}, bf16[4,2,272,128]{3,2,1,0:T(8,128)(2,1)S(1)}, u32[]{:S(2)}, u32[]{:S(2)}) %collective-permute-start) | collective-permute-done | bytes 557088 | tf_op jit(solution)/shard_map/ppermute | solution.py:720
  25.2 2.2 %add_convert_fusion = bf16[4,2,272,128]{3,2,1,0:T(8,128)(2,1)} fusion(f32[4,2,272,128]{3,2,1,0:T(8,128)} %get-tuple-element.22, bf16[4,2,272,128]{3,2,1,0:T(8,128)(2,1)S(1)} %collective-permute-done), kind=kLoop, calls=%fused_computation | loop fusion | flops 835584 | bytes 2228224 | tf_op jit(solution)/shard_map/convert_element_type | solution.py:720
  27.4 3.9 %all-to-all-done.fetched.start = bf16[16,38,8,128]{3,2,1,0:T(8,128)(2,1)S(1)} async-done(((bf16[16,38,8,128]{3,2,1,0:T(8,128)(2,1)}), bf16[16,38,8,128]{3,2,1,0:T(8,128)(2,1)S(1)}, u32[]{:S(2)}, u32[]{:S(2)}) %all-to-all-start) | async-done | bytes 1245216 | tf_op jit(solution)/shard_map/all_to_all | solution.py:696
  31.3 0.0 copy-start
  31.3 8.5 %all-to-all-start.1 = ((bf16[8,272,128]{2,1,0:T(8,128)(2,1)}), bf16[8,272,128]{2,1,0:T(8,128)(2,1)S(1)}, u32[]{:S(2)}, u32[]{:S(2)}) async-start(bf16[8,272,128]{2,1,0:T(8,128)(2,1)} %bitcast.3), calls=%async_computation.1 | async-start | bytes 1114112 | tf_op jit(solution)/shard_map/all_to_all | solution.py:696
  39.8 0.0 copy-done
  39.8 4.9 %put_heads.1 = (bf16[8,128,1024]{2,1,0:T(8,128)(2,1)}, bf16[64,128]{1,0:T(8,128)(2,1)}, f32[64,128]{1,0:T(8,128)}) custom-call(s32[64]{0:T(128)} %get-tuple-element.21.routing, bf16[8,128,1024]{2,1,0:T(8,128)(2,1)} %other_last.3, bf16[16,38,8,128]{3,2,1,0:T(8,128)(2,1)} %copy-done, f32[4,1024]{1,0:T(4,128)} %weight.3, ...), custom_call_target="tpu_custom_call", output_to_operand_aliasing={{0}: (6, {})} | custom-call | flops 4000000000 | bytes 4194304 | tf_op jit(solution)/shard_map/put_heads/pallas_call | solution.py:321
  44.7 0.1 collective-permute-start.1
  44.8 1.4 collective-permute-done.1.edge_came
  46.2 8.9 %all-to-all-done.1.parts = bf16[8,272,128]{2,1,0:T(8,128)(2,1)S(1)} async-done(((bf16[8,272,128]{2,1,0:T(8,128)(2,1)}), bf16[8,272,128]{2,1,0:T(8,128)(2,1)S(1)}, u32[]{:S(2)}, u32[]{:S(2)}) %all-to-all-start.1) | async-done | bytes 557088 | tf_op jit(solution)/shard_map/all_to_all | solution.py:696
  55.2 0.0 copy-start.11
  55.2 0.8 copy-done.11
  55.9 0.0 copy-start.1
  55.9 0.0 copy-start.2
  55.9 0.0 copy-start.3
  55.9 0.0 copy-start.5
  55.9 0.0 copy-start.7
  55.9 0.0 copy-start.8
  56.0 0.0 copy-start.9
  56.0 0.0 copy-start.12
  56.0 0.4 normalize.1
  56.4 20.0 %all_to_all.25.came = bf16[8,336,128]{2,1,0:T(8,128)(2,1)S(1)} all-to-all(bf16[8,336,128]{2,1,0:T(8,128)(2,1)S(1)} %normalize.1), channel_id=1, replica_groups=mesh['dp'=16,'z'=8,'core'=2] {'z'}, dimensions={0} | all-to-all | bytes 1376256 | tf_op jit(solution)/shard_map/all_to_all | solution.py:696
  76.4 0.0 collective-permute-start.2
  76.4 0.0 copy-done.1
  76.4 0.0 copy-done.2
  76.4 0.0 copy-done.3
  76.5 0.0 copy-done.5
  76.5 0.0 copy-done.7
  76.5 0.0 copy-done.8
  76.5 0.0 copy-done.9
  76.5 0.0 copy-done.12
  76.5 0.0 copy-start.10
  76.5 1.6 %copy-done.10 = bf16[8,128,1024]{2,1,0:T(8,128)(2,1)S(1)} copy-done((bf16[8,128,1024]{2,1,0:T(8,128)(2,1)S(1)}, bf16[8,128,1024]{2,1,0:T(8,128)(2,1)}, u32[]{:S(2)}) %copy-start.10) | copy-done | bytes 2097176
  78.1 14.5 %scan.2 = (bf16[8,128,1024]{2,1,0:T(8,128)(2,1)}, bf16[16,22,8,128]{3,2,1,0:T(8,128)(2,1)}) custom-call(s32[64]{0:T(128)S(1)} %copy-done.12, bf16[8,336,128]{2,1,0:T(8,128)(2,1)S(1)} %all_to_all.25.came, bf16[512,1024]{1,0:T(8,128)(2,1)S(1)} %copy-done.5, f32[1,1024]{1,0:T(1,128)S(1)} %bitcast.10, f32[16,1024]{1,0:T(8,128)S(1)} %copy-done.7, ...), custom_call_target="tpu_custom_call" | custom-call | flops 15000000512 | bytes 4194304 | tf_op jit(solution)/shard_map/scan/pallas_call | solution.py:528
  92.6 9.9 %all-to-all-start.3 = ((bf16[16,22,8,128]{3,2,1,0:T(8,128)(2,1)}), bf16[16,22,8,128]{3,2,1,0:T(8,128)(2,1)S(1)}, u32[]{:S(2)}, u32[]{:S(2)}) async-start(bf16[16,22,8,128]{3,2,1,0:T(8,128)(2,1)} %get-tuple-element.33), calls=%async_computation.3 | async-start | bytes 1441792 | tf_op jit(solution)/shard_map/all_to_all | solution.py:696
  102.5 0.0 collective-permute-done.2.came
  102.5 0.0 copy-start.14
  102.6 0.8 copy-done.14
  103.4 0.0 copy-start.4
  103.4 0.0 copy-start.13
  103.4 17.4 %scan.3 = (bf16[8,128,1024]{2,1,0:T(8,128)(2,1)}, bf16[16,16,8,128]{3,2,1,0:T(8,128)(2,1)}) custom-call(s32[64]{0:T(128)} %get-tuple-element.21.routing, bf16[8,336,128]{2,1,0:T(8,128)(2,1)} %copy-done.14, bf16[512,1024]{1,0:T(8,128)(2,1)} %dt_weight.3, f32[1,1024]{1,0:T(1,128)} %bitcast.9, f32[16,1024]{1,0:T(8,128)} %a_log.3, ...), custom_call_target="tpu_custom_call", output_to_operand_aliasing={{0}: (11, {})} | custom-call | flops 15000000512 | bytes 4194304 | tf_op jit(solution)/shard_map/scan/pallas_call | solution.py:528
  120.8 0.0 all-to-all-done.3.came
  120.8 7.2 %all-to-all-start.4 = ((bf16[16,16,8,128]{3,2,1,0:T(8,128)(2,1)}), bf16[16,16,8,128]{3,2,1,0:T(8,128)(2,1)S(1)}, u32[]{:S(2)}, u32[]{:S(2)}) async-start(bf16[16,16,8,128]{3,2,1,0:T(8,128)(2,1)} %get-tuple-element.35), calls=%async_computation.4 | async-start | bytes 1048576 | tf_op jit(solution)/shard_map/all_to_all | solution.py:696
  128.1 0.0 copy-done.4
  128.1 0.0 copy-done.13
  128.1 0.0 copy-start.6
  128.1 1.0 copy-done.6
  129.1 2.5 %place.1 = (f32[32,16,1024]{2,1,0:T(8,128)}, f32[3,32,1024]{2,1,0:T(8,128)}) custom-call(s32[64]{0:T(128)S(1)} %copy-done.13, bf16[16,22,8,128]{3,2,1,0:T(8,128)(2,1)S(1)} %all-to-all-done.3.came, f32[32,16,1024]{2,1,0:T(8,128)S(1)} %copy-done.4, f32[3,32,1024]{2,1,0:T(8,128)S(1)} %bitcast.8), custom_call_target="tpu_custom_call" | custom-call | flops 6000000000 | bytes 6291456 | tf_op jit(solution)/shard_map/place/pallas_call | solution.py:619
  131.6 6.7 %all-to-all-done.4.came = bf16[16,16,8,128]{3,2,1,0:T(8,128)(2,1)S(1)} async-done(((bf16[16,16,8,128]{3,2,1,0:T(8,128)(2,1)}), bf16[16,16,8,128]{3,2,1,0:T(8,128)(2,1)S(1)}, u32[]{:S(2)}, u32[]{:S(2)}) %all-to-all-start.4) | async-done | bytes 524320 | tf_op jit(solution)/shard_map/all_to_all | solution.py:696
  138.3 1.6 %store.1 = f32[32,16,1024]{2,1,0:T(8,128)} custom-call(s32[64]{0:T(128)S(1)} %copy-done.13, bf16[16,16,8,128]{3,2,1,0:T(8,128)(2,1)S(1)} %all-to-all-done.4.came, f32[32,16,1024]{2,1,0:T(8,128)} %get-tuple-element.37.ssm_in), custom_call_target="tpu_custom_call", output_to_operand_aliasing={{}: (2, {})} | custom-call | flops 2000000000 | bytes 2097152 | tf_op jit(solution)/shard_map/store/pallas_call | solution.py:673
Async XLA Ops:
  5.5 25.9 %all-to-all-start = ((bf16[16,38,8,128]{3,2,1,0:T(8,128)(2,1)}), bf16[16,38,8,128]{3,2,1,0:T(8,128)(2,1)S(1)}, u32[]{:S(2)}, u32[]{:S(2)}) async-start(bf16[16,38,8,128]{3,2,1,0:T(8,128)(2,1)} %get-tuple-element.24), calls=%async_computation | async-start | bytes 2490368 | tf_op jit(solution)/shard_map/all_to_all | solution.py:696
  23.1 2.2 %collective-permute-start = (bf16[4,2,272,128]{3,2,1,0:T(8,128)(2,1)}, bf16[4,2,272,128]{3,2,1,0:T(8,128)(2,1)S(1)}, u32[]{:S(2)}, u32[]{:S(2)}) collective-permute-start(bf16[4,2,272,128]{3,2,1,0:T(8,128)(2,1)} %get-tuple-element.23), channel_id=1, source_target_pairs={{0,1},{1,0},{2,3},{3,2},{4,5},{5,4},{6,7},{7,6},{8,9},{9,8},{10,11... | collective-permute-start | bytes 1671176 | tf_op jit(solution)/shard_map/ppermute | solution.py:720
  31.3 8.5 %copy-start = (bf16[16,38,8,128]{3,2,1,0:T(8,128)(2,1)}, bf16[16,38,8,128]{3,2,1,0:T(8,128)(2,1)S(1)}, u32[]{:S(2)}) copy-start(bf16[16,38,8,128]{3,2,1,0:T(8,128)(2,1)S(1)} %all-to-all-done.fetched.start) | copy-start | bytes 3735556
  31.3 23.8 %all-to-all-start.1 = ((bf16[8,272,128]{2,1,0:T(8,128)(2,1)}), bf16[8,272,128]{2,1,0:T(8,128)(2,1)S(1)}, u32[]{:S(2)}, u32[]{:S(2)}) async-start(bf16[8,272,128]{2,1,0:T(8,128)(2,1)} %bitcast.3), calls=%async_computation.1 | async-start | bytes 1114112 | tf_op jit(solution)/shard_map/all_to_all | solution.py:696
  44.7 1.5 %collective-permute-start.1 = (bf16[64,128]{1,0:T(8,128)(2,1)}, bf16[64,128]{1,0:T(8,128)(2,1)S(1)}, u32[]{:S(2)}, u32[]{:S(2)}) collective-permute-start(bf16[64,128]{1,0:T(8,128)(2,1)} %get-tuple-element.29), channel_id=1, source_target_pairs={{0,1},{1,0},{2,3},{3,2},{4,5},{5,4},{6,7},{7,6},{8,9},{9,8},{10,11... | collective-permute-start | bytes 49160 | tf_op jit(solution)/shard_map/ppermute | solution.py:726
  55.2 0.8 copy-start.11
  55.9 20.5 %copy-start.1 = (bf16[16,38,8,128]{3,2,1,0:T(8,128)(2,1)S(1)}, bf16[16,38,8,128]{3,2,1,0:T(8,128)(2,1)}, u32[]{:S(2)}) copy-start(bf16[16,38,8,128]{3,2,1,0:T(8,128)(2,1)} %copy-done) | copy-start | bytes 3735556
  55.9 20.5 %copy-start.2 = (bf16[8,128,1024]{2,1,0:T(8,128)(2,1)S(1)}, bf16[8,128,1024]{2,1,0:T(8,128)(2,1)}, u32[]{:S(2)}) copy-start(bf16[8,128,1024]{2,1,0:T(8,128)(2,1)} %other_last.3) | copy-start | bytes 6291460
  55.9 20.5 %copy-start.3 = (bf16[8,128,1024]{2,1,0:T(8,128)(2,1)S(1)}, bf16[8,128,1024]{2,1,0:T(8,128)(2,1)}, u32[]{:S(2)}) copy-start(bf16[8,128,1024]{2,1,0:T(8,128)(2,1)} %gate.3) | copy-start | bytes 6291460
  55.9 20.5 %copy-start.5 = (bf16[512,1024]{1,0:T(8,128)(2,1)S(1)}, bf16[512,1024]{1,0:T(8,128)(2,1)}, u32[]{:S(2)}) copy-start(bf16[512,1024]{1,0:T(8,128)(2,1)} %dt_weight.3) | copy-start | bytes 3145732
  55.9 20.5 %copy-start.7 = (f32[16,1024]{1,0:T(8,128)S(1)}, f32[16,1024]{1,0:T(8,128)}, u32[]{:S(2)}) copy-start(f32[16,1024]{1,0:T(8,128)} %a_log.3) | copy-start | bytes 196612
  55.9 20.5 %copy-start.8 = (f32[1024]{0:T(1024)S(1)}, f32[1024]{0:T(1024)}, u32[]{:S(2)}) copy-start(f32[1024]{0:T(1024)} %param.19) | copy-start | bytes 12292
  56.0 20.5 %copy-start.9 = (f32[1024]{0:T(1024)S(1)}, f32[1024]{0:T(1024)}, u32[]{:S(2)}) copy-start(f32[1024]{0:T(1024)} %param.21) | copy-start | bytes 12292
  56.0 20.5 %copy-start.12 = (s32[64]{0:T(128)S(1)}, s32[64]{0:T(128)}, u32[]{:S(2)}) copy-start(s32[64]{0:T(128)} %get-tuple-element.21.routing) | copy-start | bytes 772
  76.4 26.1 %collective-permute-start.2 = (bf16[8,336,128]{2,1,0:T(8,128)(2,1)S(1)}, bf16[8,336,128]{2,1,0:T(8,128)(2,1)S(1)}, u32[]{:S(2)}, u32[]{:S(2)}) collective-permute-start(bf16[8,336,128]{2,1,0:T(8,128)(2,1)S(1)} %all_to_all.25.came), channel_id=1, source_target_pairs={{0,1},{1,0},{2,3},{3,2},{4,5},{5,4},{6,7},{7,6},{8,9},{9,8},{10,11... | collective-permute-start | bytes 2064392 | tf_op jit(solution)/shard_map/ppermute | solution.py:728
  76.5 1.6 %copy-start.10 = (bf16[8,128,1024]{2,1,0:T(8,128)(2,1)S(1)}, bf16[8,128,1024]{2,1,0:T(8,128)(2,1)}, u32[]{:S(2)}) copy-start(bf16[8,128,1024]{2,1,0:T(8,128)(2,1)} %get-tuple-element.30.conv) | copy-start | bytes 6291460
  92.6 28.2 %all-to-all-start.3 = ((bf16[16,22,8,128]{3,2,1,0:T(8,128)(2,1)}), bf16[16,22,8,128]{3,2,1,0:T(8,128)(2,1)S(1)}, u32[]{:S(2)}, u32[]{:S(2)}) async-start(bf16[16,22,8,128]{3,2,1,0:T(8,128)(2,1)} %get-tuple-element.33), calls=%async_computation.3 | async-start | bytes 1441792 | tf_op jit(solution)/shard_map/all_to_all | solution.py:696
  102.5 0.9 copy-start.14
  103.4 24.7 %copy-start.4 = (f32[32,16,1024]{2,1,0:T(8,128)S(1)}, f32[32,16,1024]{2,1,0:T(8,128)}, u32[]{:S(2)}) copy-start(f32[32,16,1024]{2,1,0:T(8,128)} %ssm.3) | copy-start | bytes 6291460
  103.4 24.7 %copy-start.13 = (s32[64]{0:T(128)S(1)}, s32[64]{0:T(128)}, u32[]{:S(2)}) copy-start(s32[64]{0:T(128)} %get-tuple-element.21.routing) | copy-start | bytes 772
  120.8 17.5 %all-to-all-start.4 = ((bf16[16,16,8,128]{3,2,1,0:T(8,128)(2,1)}), bf16[16,16,8,128]{3,2,1,0:T(8,128)(2,1)S(1)}, u32[]{:S(2)}, u32[]{:S(2)}) async-start(bf16[16,16,8,128]{3,2,1,0:T(8,128)(2,1)} %get-tuple-element.35), calls=%async_computation.4 | async-start | bytes 1048576 | tf_op jit(solution)/shard_map/all_to_all | solution.py:696
  128.1 1.0 copy-start.6

commit v8 on v7

--- a/solution.py
+++ b/solution.py
@@ -43,7 +43,7 @@
 RETURNED = STATE + CHUNKS * KEPT
 LANES = 128
 TILES = INNER // LANES
-UNROLL = 16
+UNROLL = 32
 
 F32 = jnp.float32
 BF16 = jnp.bfloat16
@@ -259,7 +259,7 @@
             jax.ShapeDtypeStruct((PER, SPANS, SUMMED, LANES), BF16),
             jax.ShapeDtypeStruct((PER, SPANS, SUMMED, LANES), F32),
         ],
-        compiler_params=params(),
+        compiler_params=params(24),
         cost_estimate=cost(8, 8 * 2**20),
         name="convolve",
     )(routing, hidden, hidden, weight, bias, x_weight)
@@ -348,7 +348,7 @@
             jax.ShapeDtypeStruct((EDGED, LANES), F32),
         ],
         input_output_aliases={6: 0},
-        compiler_params=params(),
+        compiler_params=params(16),
         cost_estimate=cost(4, 4 * 2**20),
         name="put_heads",
     )(routing, hidden, fetched, weight, bias, x_weight, conv_out)

time: 141 us -> 138 us (0.979)
  local copies, waits for them, and re-layouts: 4.23 us -> 10.5 us
  Pallas kernels: 56.6 us -> 50.8 us
  starting transfers between devices: 32.9 us -> 29.3 us
    unnamed x30 -> x44, local copies, waits for them, and re-layouts: 4.23 us -> 10.5 us
    all_to_all x4, starting transfers between devices: 32.8 us -> 29.3 us  [exchange(): return lax.all_to_all(values, axis, split_axis=0, concat_axis=0, tiled=True)]
    pallas_call x1, Pallas kernels: 10.4 us -> 7.41 us  [convolve(): pl.pallas_call(conv_kernel, grid_spec=pltpu.PrefetchScalarGridSpec(num_sc...]
    pallas_call x1, Pallas kernels: 4.92 us -> 2.4 us  [put_heads(): pl.pallas_call(head_kernel, grid_spec=pltpu.PrefetchScalarGridSpec(num_sc...]
  transfers between devices with their start and end apart: 7 -> 7, of which waited for: 5 -> 5; matrix products, arithmetic and copies ran while one was open for 2% -> 1% of each run, Pallas kernels for 36% -> 32%
where the time goes in v8:
time: 138 us; the launch traced here: 137 us
  Pallas kernels  50.8 us (37%)
  starting transfers between devices  29.3 us (21%)
  waiting for transfers between devices  22.8 us (17%)
  blocking collectives  21.4 us (16%)
  local copies, waits for them, and re-layouts  10.5 us (8%)
    pallas_call x2, Pallas kernels, scan(): pl.pallas_call(functools.partial(scan_kernel, own), grid_spec=pltpu.Prefe...  31.7 us
    all_to_all x4, starting transfers between devices, exchange(): return lax.all_to_all(values, axis, split_axis=0, concat_axis=0, tiled=True)  29.3 us
    all_to_all x1, blocking collectives, exchange(): return lax.all_to_all(values, axis, split_axis=0, concat_axis=0, tiled=True)  21.4 us
    all_to_all x4, waiting for transfers between devices, exchange(): return lax.all_to_all(values, axis, split_axis=0, concat_axis=0, tiled=True)  19.7 us
    unnamed x44, local copies, waits for them, and re-layouts  10.5 us
    pallas_call x1, Pallas kernels, convolve(): pl.pallas_call(conv_kernel, grid_spec=pltpu.PrefetchScalarGridSpec(num_sc...  7.41 us
    pallas_call x1, Pallas kernels, pack(): pl.pallas_call(pack_kernel, grid_spec=pltpu.PrefetchScalarGridSpec(num_sc...  4.78 us
  transfers between devices with their start and end apart: 7, of which 5 were waited for; matrix products, arithmetic and copies ran while one was open for 1% of the time, Pallas kernels for 32%

profile of v8, /device:TPU:8, one launch (start us, length us, event | category | flops | bytes accessed | tf_op | source)
XLA Modules:
  0.0 136.6 jit_solution(3872610044629496881)
XLA Ops:
  0.6 4.8 %pack.1 = (s32[64]{0:T(128)}, bf16[16,38,8,128]{3,2,1,0:T(8,128)(2,1)}) custom-call(s32[128]{0:T(128)} %holders.1, s32[128]{0:T(128)} %places.1, f32[32,16,1024]{2,1,0:T(8,128)} %ssm.3, f32[3,32,1024]{2,1,0:T(8,128)} %bitcast.9), custom_call_target="tpu_custom_call" | custom-call | flops 4000000000 | bytes 4194304 | tf_op jit(solution)/shard_map/pack/pallas_call | solution.py:156
  5.4 0.0 copy-start.1
  5.4 0.0 copy-start.11
  5.4 0.0 copy-start.12
  5.5 0.0 copy-start.19
  5.5 7.4 %all-to-all-start = ((bf16[16,38,8,128]{3,2,1,0:T(8,128)(2,1)}), bf16[16,38,8,128]{3,2,1,0:T(8,128)(2,1)S(1)}, u32[]{:S(2)}, u32[]{:S(2)}) async-start(bf16[16,38,8,128]{3,2,1,0:T(8,128)(2,1)} %get-tuple-element.24), calls=%async_computation | async-start | bytes 2490368 | tf_op jit(solution)/shard_map/all_to_all | solution.py:696
  12.8 0.0 copy-done.1
  12.8 0.0 copy-done.11
  12.9 0.0 copy-done.12
  12.9 0.0 copy-done.19
  12.9 0.0 copy-start.6
  12.9 1.2 copy-done.6
  14.1 7.4 %convolve.1 = (bf16[8,128,1024]{2,1,0:T(8,128)(2,1)S(1)}, bf16[4,2,272,128]{3,2,1,0:T(8,128)(2,1)S(1)}, f32[4,2,272,128]{3,2,1,0:T(8,128)S(1)}) custom-call(s32[64]{0:T(128)S(1)} %copy-done.19, bf16[8,128,1024]{2,1,0:T(8,128)(2,1)S(1)} %copy-done.1, bf16[8,128,1024]{2,1,0:T(8,128)(2,1)S(1)} %copy-done.1, f32[4,1024]{1,0:T(4,128)S(1)} %copy-done.11, ...), custom_call_target="tpu_custom_call" | custom-call | flops 8000000000 | bytes 8388608 | tf_op jit(solution)/shard_map/convolve/pallas_call | solution.py:234
  21.5 0.0 copy-start.15
  21.5 1.3 copy-done.15
  22.9 0.0 copy-start.7
  22.9 0.0 collective-permute-start
  22.9 2.0 %collective-permute-done = bf16[4,2,272,128]{3,2,1,0:T(8,128)(2,1)S(1)} collective-permute-done((bf16[4,2,272,128]{3,2,1,0:T(8,128)(2,1)S(1)}, bf16[4,2,272,128]{3,2,1,0:T(8,128)(2,1)S(1)}, u32[]{:S(2)}, u32[]{:S(2)}) %collective-permute-start) | collective-permute-done | bytes 557088 | tf_op jit(solution)/shard_map/ppermute | solution.py:720
  24.8 0.9 add_convert_fusion
  25.8 5.8 %all-to-all-done.fetched.start = bf16[16,38,8,128]{3,2,1,0:T(8,128)(2,1)S(1)} async-done(((bf16[16,38,8,128]{3,2,1,0:T(8,128)(2,1)}), bf16[16,38,8,128]{3,2,1,0:T(8,128)(2,1)S(1)}, u32[]{:S(2)}, u32[]{:S(2)}) %all-to-all-start) | async-done | bytes 1245216 | tf_op jit(solution)/shard_map/all_to_all | solution.py:696
  31.5 0.0 copy-start
  31.5 8.5 %all-to-all-start.1 = ((bf16[8,272,128]{2,1,0:T(8,128)(2,1)}), bf16[8,272,128]{2,1,0:T(8,128)(2,1)S(1)}, u32[]{:S(2)}, u32[]{:S(2)}) async-start(bf16[8,272,128]{2,1,0:T(8,128)(2,1)} %bitcast.3), calls=%async_computation.1 | async-start | bytes 1114112 | tf_op jit(solution)/shard_map/all_to_all | solution.py:696
  40.0 0.0 copy-done.7
  40.0 0.0 copy-start.2
  40.0 1.6 %copy-done.2 = bf16[8,128,1024]{2,1,0:T(8,128)(2,1)S(1)} copy-done((bf16[8,128,1024]{2,1,0:T(8,128)(2,1)S(1)}, bf16[8,128,1024]{2,1,0:T(8,128)(2,1)}, u32[]{:S(2)}) %copy-start.2) | copy-done | bytes 2097176
  41.6 0.0 copy-start.16
  41.6 1.6 %copy-done.16 = bf16[8,128,1024]{2,1,0:T(8,128)(2,1)S(1)} copy-done((bf16[8,128,1024]{2,1,0:T(8,128)(2,1)S(1)}, bf16[8,128,1024]{2,1,0:T(8,128)(2,1)}, u32[]{:S(2)}) %copy-start.16) | copy-done | bytes 2097176
  43.2 2.4 %put_heads.1 = (bf16[8,128,1024]{2,1,0:T(8,128)(2,1)S(1)}, bf16[64,128]{1,0:T(8,128)(2,1)S(1)}, f32[64,128]{1,0:T(8,128)S(1)}) custom-call(s32[64]{0:T(128)S(1)} %copy-done.19, bf16[8,128,1024]{2,1,0:T(8,128)(2,1)S(1)} %copy-done.2, bf16[16,38,8,128]{3,2,1,0:T(8,128)(2,1)S(1)} %all-to-all-done.fetched.start, ...), custom_call_target="tpu_custom_call", output_to_operand_aliasing={{0}: (6, {})} | custom-call | flops 4000000000 | bytes 4194304 | tf_op jit(solution)/shard_map/put_heads/pallas_call | solution.py:321
  45.6 0.0 copy-start.17
  45.6 1.3 copy-done.17
  46.9 0.0 collective-permute-start.1
  46.9 1.2 collective-permute-done.1.edge_came
  48.1 7.2 %all-to-all-done.1.parts = bf16[8,272,128]{2,1,0:T(8,128)(2,1)S(1)} async-done(((bf16[8,272,128]{2,1,0:T(8,128)(2,1)}), bf16[8,272,128]{2,1,0:T(8,128)(2,1)S(1)}, u32[]{:S(2)}, u32[]{:S(2)}) %all-to-all-start.1) | async-done | bytes 557088 | tf_op jit(solution)/shard_map/all_to_all | solution.py:696
  55.3 0.0 copy-start.3
  55.3 0.0 copy-start.4
  55.3 0.0 copy-start.13
  55.4 0.0 copy-start.14
  55.4 0.4 normalize.1
  55.8 21.4 %all_to_all.25.came = bf16[8,336,128]{2,1,0:T(8,128)(2,1)S(1)} all-to-all(bf16[8,336,128]{2,1,0:T(8,128)(2,1)S(1)} %normalize.1), channel_id=1, replica_groups=mesh['dp'=16,'z'=8,'core'=2] {'z'}, dimensions={0} | all-to-all | bytes 1376256 | tf_op jit(solution)/shard_map/all_to_all | solution.py:696
  77.2 0.0 collective-permute-start.2
  77.2 0.0 copy-done
  77.2 0.0 copy-done.3
  77.2 0.0 copy-done.4
  77.2 0.0 copy-done.8
  77.2 0.0 copy-done.10
  77.2 0.0 copy-done.13
  77.2 0.0 copy-done.14
  77.2 0.0 copy-start.18
  77.2 1.6 %copy-done.18 = bf16[8,128,1024]{2,1,0:T(8,128)(2,1)S(1)} copy-done((bf16[8,128,1024]{2,1,0:T(8,128)(2,1)S(1)}, bf16[8,128,1024]{2,1,0:T(8,128)(2,1)}, u32[]{:S(2)}) %copy-start.18) | copy-done | bytes 2097176
  78.8 14.4 %scan.2 = (bf16[8,128,1024]{2,1,0:T(8,128)(2,1)}, bf16[16,22,8,128]{3,2,1,0:T(8,128)(2,1)}) custom-call(s32[64]{0:T(128)S(1)} %copy-done.19, bf16[8,336,128]{2,1,0:T(8,128)(2,1)S(1)} %all_to_all.25.came, bf16[512,1024]{1,0:T(8,128)(2,1)S(1)} %copy-done.8, f32[1,1024]{1,0:T(1,128)S(1)} %bitcast.14, f32[16,1024]{1,0:T(8,128)S(1)} %copy-done.10, ...), custom_call_target="tpu_custom_call" | custom-call | flops 15000000512 | bytes 4194304 | tf_op jit(solution)/shard_map/scan/pallas_call | solution.py:528
  93.2 6.2 %all-to-all-start.3 = ((bf16[16,22,8,128]{3,2,1,0:T(8,128)(2,1)}), bf16[16,22,8,128]{3,2,1,0:T(8,128)(2,1)S(1)}, u32[]{:S(2)}, u32[]{:S(2)}) async-start(bf16[16,22,8,128]{3,2,1,0:T(8,128)(2,1)} %get-tuple-element.33), calls=%async_computation.3 | async-start | bytes 1441792 | tf_op jit(solution)/shard_map/all_to_all | solution.py:696
  99.4 0.0 collective-permute-done.2.came
  99.4 0.0 copy-start.21
  99.5 0.8 copy-done.21
  100.3 17.3 %scan.3 = (bf16[8,128,1024]{2,1,0:T(8,128)(2,1)}, bf16[16,16,8,128]{3,2,1,0:T(8,128)(2,1)}) custom-call(s32[64]{0:T(128)} %get-tuple-element.21.routing, bf16[8,336,128]{2,1,0:T(8,128)(2,1)} %copy-done.21, bf16[512,1024]{1,0:T(8,128)(2,1)} %dt_weight.3, f32[1,1024]{1,0:T(1,128)} %bitcast.13, f32[16,1024]{1,0:T(8,128)} %a_log.3, ...), custom_call_target="tpu_custom_call", output_to_operand_aliasing={{0}: (11, {})} | custom-call | flops 15000000512 | bytes 4194304 | tf_op jit(solution)/shard_map/scan/pallas_call | solution.py:528
  117.6 0.0 all-to-all-done.3.came
  117.6 7.2 %all-to-all-start.4 = ((bf16[16,16,8,128]{3,2,1,0:T(8,128)(2,1)}), bf16[16,16,8,128]{3,2,1,0:T(8,128)(2,1)S(1)}, u32[]{:S(2)}, u32[]{:S(2)}) async-start(bf16[16,16,8,128]{3,2,1,0:T(8,128)(2,1)} %get-tuple-element.35), calls=%async_computation.4 | async-start | bytes 1048576 | tf_op jit(solution)/shard_map/all_to_all | solution.py:696
  124.8 0.0 copy-done.5
  124.8 0.0 copy-done.20
  124.8 0.0 copy-start.9
  124.9 1.0 copy-done.9
  125.8 2.5 %place.1 = (f32[32,16,1024]{2,1,0:T(8,128)}, f32[3,32,1024]{2,1,0:T(8,128)}) custom-call(s32[64]{0:T(128)S(1)} %copy-done.20, bf16[16,22,8,128]{3,2,1,0:T(8,128)(2,1)S(1)} %all-to-all-done.3.came, f32[32,16,1024]{2,1,0:T(8,128)S(1)} %copy-done.5, f32[3,32,1024]{2,1,0:T(8,128)S(1)} %bitcast.10), custom_call_target="tpu_custom_call" | custom-call | flops 6000000000 | bytes 6291456 | tf_op jit(solution)/shard_map/place/pallas_call | solution.py:619
  128.4 6.7 %all-to-all-done.4.came = bf16[16,16,8,128]{3,2,1,0:T(8,128)(2,1)S(1)} async-done(((bf16[16,16,8,128]{3,2,1,0:T(8,128)(2,1)}), bf16[16,16,8,128]{3,2,1,0:T(8,128)(2,1)S(1)}, u32[]{:S(2)}, u32[]{:S(2)}) %all-to-all-start.4) | async-done | bytes 524320 | tf_op jit(solution)/shard_map/all_to_all | solution.py:696
  135.0 1.6 %store.1 = f32[32,16,1024]{2,1,0:T(8,128)} custom-call(s32[64]{0:T(128)S(1)} %copy-done.20, bf16[16,16,8,128]{3,2,1,0:T(8,128)(2,1)S(1)} %all-to-all-done.4.came, f32[32,16,1024]{2,1,0:T(8,128)} %get-tuple-element.37.ssm_in), custom_call_target="tpu_custom_call", output_to_operand_aliasing={{}: (2, {})} | custom-call | flops 2000000000 | bytes 2097152 | tf_op jit(solution)/shard_map/store/pallas_call | solution.py:673
  (4 shorter events, 0.0 us)
Async XLA Ops:
  5.4 7.4 %copy-start.1 = (bf16[8,128,1024]{2,1,0:T(8,128)(2,1)S(1)}, bf16[8,128,1024]{2,1,0:T(8,128)(2,1)}, u32[]{:S(2)}) copy-start(bf16[8,128,1024]{2,1,0:T(8,128)(2,1)} %other_last.3) | copy-start | bytes 6291460
  5.4 7.4 %copy-start.11 = (f32[4,1024]{1,0:T(4,128)S(1)}, f32[4,1024]{1,0:T(4,128)}, u32[]{:S(2)}) copy-start(f32[4,1024]{1,0:T(4,128)} %weight.3) | copy-start | bytes 49156
  5.4 7.4 %copy-start.12 = (f32[1024]{0:T(1024)S(1)}, f32[1024]{0:T(1024)}, u32[]{:S(2)}) copy-start(f32[1024]{0:T(1024)} %param.16) | copy-start | bytes 12292
  5.5 7.4 %copy-start.19 = (s32[64]{0:T(128)S(1)}, s32[64]{0:T(128)}, u32[]{:S(2)}) copy-start(s32[64]{0:T(128)} %get-tuple-element.21.routing) | copy-start | bytes 772
  5.5 26.1 %all-to-all-start = ((bf16[16,38,8,128]{3,2,1,0:T(8,128)(2,1)}), bf16[16,38,8,128]{3,2,1,0:T(8,128)(2,1)S(1)}, u32[]{:S(2)}, u32[]{:S(2)}) async-start(bf16[16,38,8,128]{3,2,1,0:T(8,128)(2,1)} %get-tuple-element.24), calls=%async_computation | async-start | bytes 2490368 | tf_op jit(solution)/shard_map/all_to_all | solution.py:696
  12.9 1.3 copy-start.6
  21.5 1.3 copy-start.15
  22.9 17.1 %copy-start.7 = (bf16[1024,544]{0,1:T(8,128)(2,1)S(1)}, bf16[1024,544]{0,1:T(8,128)(2,1)}, u32[]{:S(2)}) copy-start(bf16[1024,544]{0,1:T(8,128)(2,1)} %param.17) | copy-start | bytes 3342340
  22.9 2.0 %collective-permute-start = (bf16[4,2,272,128]{3,2,1,0:T(8,128)(2,1)S(1)}, bf16[4,2,272,128]{3,2,1,0:T(8,128)(2,1)S(1)}, u32[]{:S(2)}, u32[]{:S(2)}) collective-permute-start(bf16[4,2,272,128]{3,2,1,0:T(8,128)(2,1)S(1)} %get-tuple-element.23), channel_id=1, source_target_pairs={{0,1},{1,0},{2,3},{3,2},{4,5},{5,4},{6,7},{7,6},{8,9},{9,8},{10,11... | collective-permute-start | bytes 1671176 | tf_op jit(solution)/shard_map/ppermute | solution.py:720
  31.5 45.7 %copy-start = (bf16[16,38,8,128]{3,2,1,0:T(8,128)(2,1)}, bf16[16,38,8,128]{3,2,1,0:T(8,128)(2,1)S(1)}, u32[]{:S(2)}) copy-start(bf16[16,38,8,128]{3,2,1,0:T(8,128)(2,1)S(1)} %all-to-all-done.fetched.start) | copy-start | bytes 3735556
  31.5 23.8 %all-to-all-start.1 = ((bf16[8,272,128]{2,1,0:T(8,128)(2,1)}), bf16[8,272,128]{2,1,0:T(8,128)(2,1)S(1)}, u32[]{:S(2)}, u32[]{:S(2)}) async-start(bf16[8,272,128]{2,1,0:T(8,128)(2,1)} %bitcast.3), calls=%async_computation.1 | async-start | bytes 1114112 | tf_op jit(solution)/shard_map/all_to_all | solution.py:696
  40.0 1.6 %copy-start.2 = (bf16[8,128,1024]{2,1,0:T(8,128)(2,1)S(1)}, bf16[8,128,1024]{2,1,0:T(8,128)(2,1)}, u32[]{:S(2)}) copy-start(bf16[8,128,1024]{2,1,0:T(8,128)(2,1)} %other_last.3) | copy-start | bytes 6291460
  41.6 1.6 %copy-start.16 = (bf16[8,128,1024]{2,1,0:T(8,128)(2,1)S(1)}, bf16[8,128,1024]{2,1,0:T(8,128)(2,1)}, u32[]{:S(2)}) copy-start(bf16[8,128,1024]{2,1,0:T(8,128)(2,1)} %copy-done.15) | copy-start | bytes 6291460
  45.6 1.3 copy-start.17
  46.9 1.2 collective-permute-start.1
  55.3 21.8 %copy-start.3 = (bf16[8,128,1024]{2,1,0:T(8,128)(2,1)S(1)}, bf16[8,128,1024]{2,1,0:T(8,128)(2,1)}, u32[]{:S(2)}) copy-start(bf16[8,128,1024]{2,1,0:T(8,128)(2,1)} %other_last.3) | copy-start | bytes 6291460
  55.3 21.8 %copy-start.4 = (bf16[8,128,1024]{2,1,0:T(8,128)(2,1)S(1)}, bf16[8,128,1024]{2,1,0:T(8,128)(2,1)}, u32[]{:S(2)}) copy-start(bf16[8,128,1024]{2,1,0:T(8,128)(2,1)} %gate.3) | copy-start | bytes 6291460
  55.3 21.9 %copy-start.8 = (bf16[512,1024]{1,0:T(8,128)(2,1)S(1)}, bf16[512,1024]{1,0:T(8,128)(2,1)}, u32[]{:S(2)}) copy-start(bf16[512,1024]{1,0:T(8,128)(2,1)} %dt_weight.3) | copy-start | bytes 3145732
  55.3 21.9 %copy-start.10 = (f32[16,1024]{1,0:T(8,128)S(1)}, f32[16,1024]{1,0:T(8,128)}, u32[]{:S(2)}) copy-start(f32[16,1024]{1,0:T(8,128)} %a_log.3) | copy-start | bytes 196612
  55.3 21.9 %copy-start.13 = (f32[1024]{0:T(1024)S(1)}, f32[1024]{0:T(1024)}, u32[]{:S(2)}) copy-start(f32[1024]{0:T(1024)} %param.19) | copy-start | bytes 12292
  55.4 21.9 %copy-start.14 = (f32[1024]{0:T(1024)S(1)}, f32[1024]{0:T(1024)}, u32[]{:S(2)}) copy-start(f32[1024]{0:T(1024)} %param.21) | copy-start | bytes 12292
  77.2 22.3 %collective-permute-start.2 = (bf16[8,336,128]{2,1,0:T(8,128)(2,1)S(1)}, bf16[8,336,128]{2,1,0:T(8,128)(2,1)S(1)}, u32[]{:S(2)}, u32[]{:S(2)}) collective-permute-start(bf16[8,336,128]{2,1,0:T(8,128)(2,1)S(1)} %all_to_all.25.came), channel_id=1, source_target_pairs={{0,1},{1,0},{2,3},{3,2},{4,5},{5,4},{6,7},{7,6},{8,9},{9,8},{10,11... | collective-permute-start | bytes 2064392 | tf_op jit(solution)/shard_map/ppermute | solution.py:728
  77.2 1.6 %copy-start.18 = (bf16[8,128,1024]{2,1,0:T(8,128)(2,1)S(1)}, bf16[8,128,1024]{2,1,0:T(8,128)(2,1)}, u32[]{:S(2)}) copy-start(bf16[8,128,1024]{2,1,0:T(8,128)(2,1)} %copy-done.17) | copy-start | bytes 6291460
  93.2 24.3 %all-to-all-start.3 = ((bf16[16,22,8,128]{3,2,1,0:T(8,128)(2,1)}), bf16[16,22,8,128]{3,2,1,0:T(8,128)(2,1)S(1)}, u32[]{:S(2)}, u32[]{:S(2)}) async-start(bf16[16,22,8,128]{3,2,1,0:T(8,128)(2,1)} %get-tuple-element.33), calls=%async_computation.3 | async-start | bytes 1441792 | tf_op jit(solution)/shard_map/all_to_all | solution.py:696
  99.4 0.9 copy-start.21
  100.3 24.5 %copy-start.5 = (f32[32,16,1024]{2,1,0:T(8,128)S(1)}, f32[32,16,1024]{2,1,0:T(8,128)}, u32[]{:S(2)}) copy-start(f32[32,16,1024]{2,1,0:T(8,128)} %ssm.3) | copy-start | bytes 6291460
  100.3 24.5 %copy-start.20 = (s32[64]{0:T(128)S(1)}, s32[64]{0:T(128)}, u32[]{:S(2)}) copy-start(s32[64]{0:T(128)} %get-tuple-element.21.routing) | copy-start | bytes 772
  117.6 17.5 %all-to-all-start.4 = ((bf16[16,16,8,128]{3,2,1,0:T(8,128)(2,1)}), bf16[16,16,8,128]{3,2,1,0:T(8,128)(2,1)S(1)}, u32[]{:S(2)}, u32[]{:S(2)}) async-start(bf16[16,16,8,128]{3,2,1,0:T(8,128)(2,1)} %get-tuple-element.35), calls=%async_computation.4 | async-start | bytes 1048576 | tf_op jit(solution)/shard_map/all_to_all | solution.py:696
  124.8 1.0 copy-start.9
